TPU v7x, 512 devices: a whole 4x4x16 slice. The times are simulated.
512 devices in a mesh: lon: 32 (over z_hi, y, x), lat: 16 (over z_lo, core).
Axes of the slice: x: 4, y: 4, z: 16 (z_hi: 2, z_lo: 8; z = z_hi * 8 + z_lo), core: 2. Of those that a mesh axis runs over, the one named last changes fastest.
Arguments:
- block_input: bfloat16 [2, 192, 384, 512], P(None, 'lat', 'lon')
- cotangent: bfloat16 [2, 192, 384, 512], P(None, 'lat', 'lon'), may hold values from -6 to 6
- norm_gain: float32 [512], replicated, may hold values from 0.1 to 1.9
- w_qkv: bfloat16 [512, 1536], replicated
- w_out: bfloat16 [512, 512], replicated, may hold values from -0.25 to 0.25
Outputs:
- input_grad: bfloat16 [2, 192, 384, 512], P(None, 'lat', 'lon')
- qkv_grad: float32 [512, 1536], P('lon')
- out_grad: float32 [512, 512], P('lon')
- gain_grad: float32 [512], replicated
All inputs are finite; a program needn't handle non-finite values.
Results may differ from a plain program's by a relative error of at most 0.035.
The roundings to bfloat16 on the way count: a program that leaves them out, or rounds other values in their place, can miss the bound.
Values may be sent and summed in bfloat16 or wider, within the bound.
No kernel may reach another device: no remote copies, remote signals or barrier semaphores. Data moves between devices by JAX's collectives and lax.ppermute only.
A program may use at most 64 MiB of HBM per device.

v0:
```python
import math

import jax
import jax.numpy as jnp
from jax import lax
from jax.sharding import PartitionSpec as P

HEADS = 16
WLAT = 6
WLON = 12


def passed_along(block, axis, distance):
    devices = range(lax.axis_size(axis))
    route = [((i - distance) % len(devices), i) for i in devices]
    return lax.ppermute(block, axis, route)


def ahead_lon(field, half_lon):
    lon_axis = field.ndim - 2
    length = field.shape[lon_axis]
    moved = passed_along(lax.slice_in_dim(field, 0, half_lon, axis=lon_axis), "lon", -1)
    return jnp.concatenate(
        [lax.slice_in_dim(field, half_lon, length, axis=lon_axis), moved], axis=lon_axis
    )


def ahead_lat(field, half_lat):
    lat_axis = field.ndim - 3
    length = field.shape[lat_axis]
    moved = passed_along(lax.slice_in_dim(field, 0, half_lat, axis=lat_axis), "lat", -1)
    return jnp.concatenate(
        [lax.slice_in_dim(field, half_lat, length, axis=lat_axis), moved], axis=lat_axis
    )


def behind_lon(field, half_lon):
    lon_axis = field.ndim - 2
    length = field.shape[lon_axis]
    moved = passed_along(
        lax.slice_in_dim(field, length - half_lon, length, axis=lon_axis), "lon", 1
    )
    return jnp.concatenate(
        [moved, lax.slice_in_dim(field, 0, length - half_lon, axis=lon_axis)], axis=lon_axis
    )


def behind_lat(field, half_lat):
    lat_axis = field.ndim - 3
    length = field.shape[lat_axis]
    moved = passed_along(
        lax.slice_in_dim(field, length - half_lat, length, axis=lat_axis), "lat", 1
    )
    return jnp.concatenate(
        [moved, lax.slice_in_dim(field, 0, length - half_lat, axis=lat_axis)], axis=lat_axis
    )


def reduce_weights(terms):
    band_sums = (
        lax.psum(terms[0].astype(jnp.bfloat16), "lat").astype(jnp.float32),
        lax.psum(terms[1].astype(jnp.bfloat16), "lat").astype(jnp.float32),
    )
    return (
        lax.psum_scatter(
            band_sums[0].astype(jnp.bfloat16), "lon", scatter_dimension=0, tiled=True
        ).astype(jnp.float32),
        lax.psum_scatter(
            band_sums[1].astype(jnp.bfloat16), "lon", scatter_dimension=0, tiled=True
        ).astype(jnp.float32),
    )


def layer_norm(inputs):
    values = inputs.astype(jnp.float32)
    centred = values - jnp.mean(values, axis=-1, keepdims=True)
    inverse = lax.rsqrt(jnp.mean(centred * centred, axis=-1, keepdims=True) + 1e-05)
    return (centred * inverse, inverse)


def per_device(block_input, cotangent, norm_gain, w_qkv, w_out):
    half_lat = WLAT // 2
    half_lon = WLON // 2
    levels = block_input.shape[0]
    lat_rows = block_input.shape[1]
    lon_cols = block_input.shape[2]
    feature = block_input.shape[3]
    head_dim = feature // HEADS
    score_scale = 1.0 / math.sqrt(head_dim)
    band_count = lat_rows // WLAT
    window_len = levels * WLAT * lon_cols
    token_count = band_count * window_len
    stacked = jnp.stack([block_input, cotangent])
    rolled = ahead_lat(ahead_lon(stacked, half_lon), half_lat)
    tiles = rolled.reshape(2, levels, band_count, WLAT, lon_cols, feature).transpose(
        0, 2, 1, 3, 4, 5
    )
    tokens = tiles[0].reshape(token_count, feature)
    grads_out = tiles[1].reshape(token_count, feature)
    global_rows = lax.axis_index("lat") * lat_rows + jnp.arange(lat_rows, dtype=jnp.int32)
    edge_rows = (global_rows >= lat_rows * lax.axis_size("lat") - half_lat).astype(jnp.int32)
    edge_grid = jnp.broadcast_to(edge_rows[:, None], (lat_rows, lon_cols))
    shaped_edge = edge_grid.reshape(band_count, 1, WLAT, lon_cols)
    edge_win = jnp.broadcast_to(shaped_edge, (band_count, levels, WLAT, lon_cols)).reshape(
        band_count, window_len
    )
    normed, inverse = layer_norm(tokens)
    hidden = (normed * norm_gain).astype(jnp.bfloat16)
    qkv = jnp.dot(hidden, w_qkv, preferred_element_type=jnp.float32).astype(jnp.bfloat16)
    d_attn = jnp.einsum("ne,de->nd", grads_out, w_out, preferred_element_type=jnp.float32).astype(
        jnp.bfloat16
    )

    def window_step(inputs):
        slab, grad_slab, edge_flag = inputs
        split = slab.reshape(window_len, 3, HEADS, head_dim)
        queries = split[:, 0]
        keys_win = split[:, 1]
        values_win = split[:, 2]
        grad_heads = grad_slab.reshape(window_len, HEADS, head_dim)
        scores = (
            jnp.einsum("qhd,khd->hqk", queries, keys_win, preferred_element_type=jnp.float32)
            * score_scale
        )
        allowed = edge_flag[:, None] == edge_flag[None, :]
        row_max = jnp.max(jnp.where(allowed, scores, -jnp.inf), axis=-1, keepdims=True)
        weights_raw = jnp.where(allowed, jnp.exp(scores - row_max), 0.0)
        prob_full = weights_raw / jnp.sum(weights_raw, axis=-1, keepdims=True)
        prob_half = prob_full.astype(jnp.bfloat16)
        attended = jnp.einsum(
            "hqk,khd->qhd", prob_half, values_win, preferred_element_type=jnp.float32
        )
        dprob = jnp.einsum(
            "qhd,khd->hqk", grad_heads, values_win, preferred_element_type=jnp.float32
        )
        row_delta = jnp.sum(prob_full * dprob, axis=-1, keepdims=True)
        dscore = (prob_full * (dprob - row_delta) * score_scale).astype(jnp.bfloat16)
        dquery = jnp.einsum("hqk,khd->qhd", dscore, keys_win, preferred_element_type=jnp.float32)
        dkey = jnp.einsum("hqk,qhd->khd", dscore, queries, preferred_element_type=jnp.float32)
        dvalue = jnp.einsum(
            "hqk,qhd->khd", prob_half, grad_heads, preferred_element_type=jnp.float32
        )
        dslab = (
            jnp.stack([dquery, dkey, dvalue], axis=1)
            .reshape(window_len, 3 * feature)
            .astype(jnp.bfloat16)
        )
        return (attended.reshape(window_len, feature).astype(jnp.bfloat16), dslab)

    attn_win, dqkv_win = lax.map(
        window_step,
        (
            qkv.reshape(band_count, window_len, 3 * feature),
            d_attn.reshape(band_count, window_len, feature),
            edge_win,
        ),
    )
    attended = attn_win.reshape(token_count, feature)
    dqkv = dqkv_win.reshape(token_count, 3 * feature)
    out_terms = jnp.einsum("nd,ne->de", attended, grads_out, preferred_element_type=jnp.float32)
    qkv_terms = jnp.einsum("nd,ne->de", hidden, dqkv, preferred_element_type=jnp.float32)
    dhidden = jnp.einsum("ne,de->nd", dqkv, w_qkv, preferred_element_type=jnp.float32)
    gain_local = jnp.sum(dhidden * normed, axis=0)
    dnorm = dhidden * norm_gain
    drolled = grads_out.astype(jnp.float32) + inverse * (
        dnorm
        - jnp.mean(dnorm, axis=-1, keepdims=True)
        - normed * jnp.mean(dnorm * normed, axis=-1, keepdims=True)
    )
    drolled = drolled.astype(jnp.bfloat16)
    grid = (
        drolled.reshape(band_count, levels, WLAT, lon_cols, feature)
        .transpose(1, 0, 2, 3, 4)
        .reshape(levels, lat_rows, lon_cols, feature)
    )
    input_grad = behind_lon(behind_lat(grid, half_lat), half_lon)
    qkv_grad, out_grad = reduce_weights((qkv_terms, out_terms))
    gain_grad = lax.psum(gain_local, ("lon", "lat"))
    return (input_grad, qkv_grad, out_grad, gain_grad)


def solution(mesh):
    return jax.shard_map(
        per_device,
        mesh=mesh,
        in_specs=(P(None, "lat", "lon", None), P(None, "lat", "lon", None), P(), P(), P()),
        out_specs=(P(None, "lat", "lon", None), P("lon", None), P("lon", None), P()),
        check_vma=False,
    )
```

profile of v0, /device:TPU:1, one launch (start us, length us, event | category | flops | bytes accessed | tf_op | source)
XLA Modules:
  0.0 922.8 jit_solution(4740838488443789281)
XLA Ops:
  7.2 2.1 fusion.44
  9.3 20.9 %collective-permute-start = (bf16[2,2,12,6,512]{4,1,3,2,0:T(2,128)(2,1)S(1)}, bf16[2,2,12,6,512]{4,1,3,2,0:T(2,128)(2,1)S(1)}, u32[]{:S(2)}, u32[]{:S(2)}) collective-permute-start(bf16[2,2,12,6,512]{4,1,3,2,0:T(2,128)(2,1)S(1)} %get-tuple-element.81), channel_id=1, source_target_pairs={{16,0},{32,16},{48,32},{64,48},{80,64},{96,80},{112,96},{128,112},... | collective-permute-start | bytes 884744 | tf_op jit(solution)/shard_map/ppermute | solution.py:16
  30.3 24.4 %collective-permute-done = bf16[2,2,12,6,512]{4,1,3,2,0:T(2,128)(2,1)S(1)} collective-permute-done((bf16[2,2,12,6,512]{4,1,3,2,0:T(2,128)(2,1)S(1)}, bf16[2,2,12,6,512]{4,1,3,2,0:T(2,128)(2,1)S(1)}, u32[]{:S(2)}, u32[]{:S(2)}) %collective-permute-start) | collective-permute-done | bytes 294944 | tf_op jit(solution)/shard_map/ppermute | solution.py:16
  54.6 0.2 pad_maximum_fusion.4
  54.8 3.4 collective-permute-start.1
  58.5 0.6 fusion.43
  59.1 2.9 collective-permute-done.1
  62.0 0.8 pad_maximum_fusion.1
  62.9 0.1 convert_reduce_fusion
  63.1 0.3 multiply_reduce_fusion.1
  63.4 0.9 slice_convert_fusion
  64.4 0.9 reshape.153
  65.2 1.1 reshape_squeeze.4
  66.3 1.5 convolution_convert_fusion.5
  67.9 2.7 convolution_convert_fusion.3
  70.5 39.4 %while.12 = (s32[]{:T(128)}, bf16[2,144,512]{2,1,0:T(8,128)(2,1)}, bf16[2,144,1536]{2,1,0:T(8,128)(2,1)}, bf16[2,144,1536]{2,1,0:T(8,128)(2,1)}, s32[2,144]{1,0:...) while((s32[]{:T(128)}, bf16[2,144,512]{2,1,0:T(8,128)(2,1)}, bf16[2,144,1536]{2,1,0:T(8,128)(2,1)}, ...), condition=%wide.region_6.7_spmd, body=%wide.region_2.6_spmd.sunk | while | flops 136127664 | bytes 41496896 | solution.py:150
  70.6 1.0 constant_dynamic-slice_fusion.6
  71.7 0.3 copy.52
  72.0 0.5 fusion.80
  72.5 0.9 fusion.81
  73.4 0.4 convolution_convert_fusion.7
  73.8 1.0 copy-done.6
  74.9 0.7 constant_dynamic-slice_fusion.8
  75.6 0.1 copy.54
  75.8 2.2 fusion.82
  77.9 1.9 fusion.83
  79.8 4.6 fusion.85
  84.4 4.5 fusion.84
  89.0 0.2 pad_maximum_fusion.6
  89.2 0.2 copy.55
  89.4 0.8 constant_dynamic-update-slice_fusion.3
  90.3 1.0 constant_dynamic-slice_fusion.6
  91.4 0.3 copy.52
  91.6 0.5 fusion.80
  92.2 0.9 fusion.81
  93.1 0.4 convolution_convert_fusion.7
  93.5 1.0 copy-done.6
  94.6 0.7 constant_dynamic-slice_fusion.8
  95.3 0.1 copy.54
  95.5 2.2 fusion.82
  97.6 1.9 fusion.83
  99.5 4.6 fusion.85
  104.1 4.5 fusion.84
  108.7 0.2 pad_maximum_fusion.6
  108.9 0.2 copy.55
  109.1 0.8 constant_dynamic-update-slice_fusion.3
  109.9 2.3 convolution_convert_fusion.4
  112.3 1.2 multiply_convert_fusion.1
  113.6 3.4 convolution_convert_fusion.2
  117.1 2.0 multiply_reduce_fusion.2
  119.1 0.3 add_convert_fusion
  119.5 0.3 copy.34
  119.9 1.9 collective-permute-start.2
  121.8 0.2 slice.59
  122.0 1.2 collective-permute-done.2
  123.2 0.2 fusion.49
  123.4 1.9 collective-permute-start.3
  125.3 112.4 %psum.23 = f32[512]{0:T(512)} all-reduce(f32[512]{0:T(512)S(1)} %get-tuple-element.57), channel_id=1, replica_groups=mesh['lon'=32,'lat'=16] {'lon','lat'}, use_global_device_ids=true, to_apply=%region_14.15 | all-reduce | flops 512 | bytes 4096 | tf_op jit(solution)/shard_map/psum | solution.py:178
  237.7 158.3 %reduce-scatter.5.cloned.1.call-done = bf16[16,512]{1,0:T(8,128)(2,1)} async-done(((bf16[512,512]{1,0:T(8,128)(2,1)}), bf16[16,512]{1,0:T(8,128)(2,1)}) %reduce-scatter.5.cloned.1.call-update) | async-done | bytes 16400 | tf_op jit(solution)/shard_map/reduce_scatter | solution.py:68
  396.1 339.4 %reduce-scatter.3.cloned.1.call-done = bf16[16,1536]{1,0:T(8,128)(2,1)} async-done(((bf16[512,1536]{1,0:T(8,128)(2,1)}), bf16[16,1536]{1,0:T(8,128)(2,1)}) %reduce-scatter.3.cloned.1.call-update) | async-done | bytes 49168 | tf_op jit(solution)/shard_map/reduce_scatter | solution.py:65
  735.5 1.1 fusion.45
  736.6 176.9 %all-reduce.3.cloned.1.call-done = (bf16[16,1536]{1,0:T(8,128)(2,1)}, bf16[16,512]{1,0:T(8,128)(2,1)}) async-done(((bf16[16,1536]{1,0:T(8,128)(2,1)}, bf16[16,512]{1,0:T(8,128)(2,1)}), (bf16[16,1536]{1,0:T(8,128)(2,1)}, bf16[16,512]{1,0:T(8,128)(2,1)})) %all-reduce.3.cloned.1.call-update) | async-done | bytes 65552 | tf_op jit(solution)/shard_map/psum | solution.py:61
  913.5 1.3 convert_element_type.101
  914.8 1.4 convert_element_type.99
  (41 shorter events, 1.3 us)
Async XLA Ops:
  7.2 60.7 %copy-start = (bf16[512,1536]{1,0:T(8,128)(2,1)S(1)}, bf16[512,1536]{1,0:T(8,128)(2,1)}, u32[]{:S(2)}) copy-start(bf16[512,1536]{1,0:T(8,128)(2,1)} %param.10) | copy-start | bytes 4718596
  7.2 388.9 %reduce-scatter.5.cloned.1.call-start = ((), (), s32[]{:S(2)}) async-start(), calls=%async_computation.3 | async-start | bytes 540672 | tf_op jit(solution)/shard_map/reduce_scatter | solution.py:68
  9.3 45.3 %collective-permute-start = (bf16[2,2,12,6,512]{4,1,3,2,0:T(2,128)(2,1)S(1)}, bf16[2,2,12,6,512]{4,1,3,2,0:T(2,128)(2,1)S(1)}, u32[]{:S(2)}, u32[]{:S(2)}) collective-permute-start(bf16[2,2,12,6,512]{4,1,3,2,0:T(2,128)(2,1)S(1)} %get-tuple-element.81), channel_id=1, source_target_pairs={{16,0},{32,16},{48,32},{64,48},{80,64},{96,80},{112,96},{128,112},... | collective-permute-start | bytes 884744 | tf_op jit(solution)/shard_map/ppermute | solution.py:16
  54.8 7.2 collective-permute-start.1
  62.9 3.5 copy-start.1
  63.4 4.5 copy-start.5
  66.3 4.2 copy-start.2
  73.4 1.4 copy-start.6
  93.1 1.4 copy-start.6
  112.2 623.2 %reduce-scatter.3.cloned.1.call-start = ((), (), s32[]{:S(2)}) async-start(), calls=%async_computation.2 | async-start | bytes 1622016 | tf_op jit(solution)/shard_map/reduce_scatter | solution.py:65
  113.6 3.5 copy-start.4
  117.0 2.1 copy-start.3
  117.0 796.5 %all-reduce.3.cloned.1.call-start = ((), (), s32[]{:S(2)}) async-start(), calls=%async_computation.4 | async-start | bytes 131072 | tf_op jit(solution)/shard_map/psum | solution.py:61
  119.9 3.3 collective-permute-start.2
  123.4 612.1 %collective-permute-start.3 = (bf16[2,12,6,512]{3,0,2,1:T(2,128)(2,1)S(1)}, bf16[2,12,6,512]{3,0,2,1:T(2,128)(2,1)S(1)}, u32[]{:S(2)}, u32[]{:S(2)}) collective-permute-start(bf16[2,12,6,512]{3,0,2,1:T(2,128)(2,1)S(1)} %fusion.49), channel_id=1, source_target_pairs={{496,0},{0,16},{16,32},{32,48},{48,64},{64,80},{80,96},{96,112},{1... | collective-permute-start | bytes 442376 | tf_op jit(solution)/shard_map/ppermute | solution.py:16
Sparse Core Ops, SparseCore 0:
  112.4 283.6 reduce-scatter.4
  403.3 332.1 reduce-scatter.2
  738.7 174.7 all-reduce.2
where the time goes:
time: 924 us; the launch traced here: 923 us
  waiting for transfers between devices  703 us (76%)
  blocking collectives  112 us (12%)
  matrix products  40.1 us (4%)
  starting transfers between devices  28.3 us (3%)
  between operations  14 us (2%)
  other arithmetic  12.9 us (1%)
  local copies, waits for them, and re-layouts  11.7 us (1%)
    reduce_scatter x1, waiting for transfers between devices, reduce_weights(): lax.psum_scatter(band_sums[0].astype(jnp.bfloat16), 'lon', scatter_dimens...  339 us
    psum x1, waiting for transfers between devices, reduce_weights(): lax.psum(terms[0].astype(jnp.bfloat16), 'lat').astype(jnp.float32)  177 us
    reduce_scatter x1, waiting for transfers between devices, reduce_weights(): lax.psum_scatter(band_sums[1].astype(jnp.bfloat16), 'lon', scatter_dimens...  158 us
    psum x1, blocking collectives, per_device(): gain_grad = lax.psum(gain_local, ('lon', 'lat'))  112 us
    ppermute x4, waiting for transfers between devices, passed_along(): return lax.ppermute(block, axis, route)  28.5 us
    ppermute x4, starting transfers between devices, passed_along(): return lax.ppermute(block, axis, route)  28.2 us
  transfers between devices with their start and end apart: 7, of which 6 were waited for; matrix products, arithmetic and copies ran while one was open for 1% of the time, Pallas kernels for 0%

commit v1 on v0

v1 whole, which is shorter than its diff:
```python
import functools
import math

import jax
import jax.numpy as jnp
from jax import lax
from jax.experimental import pallas as pl
from jax.experimental.pallas import tpu as pltpu
from jax.sharding import Mesh, PartitionSpec as P

HEADS = 16
HEAD_DIM = 32
WLAT = 6
WLON = 12
WINDOW = 144
TOKENS = 288
BLOCK = 36
GROUP = 4
BF16 = jnp.bfloat16
F32 = jnp.float32
LON = ("zh", "y", "x")
LAT = ("zl", "c")
ALL = LON + LAT
MIDS = ((1, 1), (2, 1), (1, 2), (2, 2))


def nn(a, b):
    return lax.dot_general(a, b, (((1,), (0,)), ((), ())), preferred_element_type=F32)


def nt(a, b):
    return lax.dot_general(a, b, (((1,), (1,)), ((), ())), preferred_element_type=F32)


def tn(a, b):
    return lax.dot_general(a, b, (((0,), (0,)), ((), ())), preferred_element_type=F32)


def attention_group(window, group, last, qkv, d_attn, attended, dqkv):
    feature = HEADS * HEAD_DIM
    width = GROUP * HEAD_DIM
    rows = pl.ds(pl.multiple_of(window * WINDOW, 16), WINDOW)
    at = group * width

    def columns(offset):
        return pl.ds(pl.multiple_of(at + offset, 128), width)

    queries = qkv[rows, columns(0)]
    keys = qkv[rows, columns(feature)]
    values = qkv[rows, columns(2 * feature)]
    grads = d_attn[rows, columns(0)]
    scale = 1.0 / math.sqrt(HEAD_DIM)
    lane_head = lax.broadcasted_iota(jnp.int32, (1, width), 1) // HEAD_DIM
    half = WINDOW // 2
    key_late = lax.broadcasted_iota(jnp.int32, (WINDOW, WINDOW), 0) >= half
    query_late = lax.broadcasted_iota(jnp.int32, (WINDOW, WINDOW), 1) >= half
    masked = jnp.logical_and(last == 1, window == 1)
    allowed = jnp.logical_or(key_late == query_late, jnp.logical_not(masked))

    dkey = jnp.zeros((WINDOW, width), F32)
    dvalue = jnp.zeros((WINDOW, width), F32)
    prob_parts, dscore_parts, key_parts, value_parts = [], [], [], []
    for head in range(GROUP):
        own = (lane_head == head).astype(BF16)
        keys_h = keys * own
        values_h = values * own
        scores = nt(keys_h, queries) * scale
        scores = jnp.where(allowed, scores, -jnp.inf)
        weights = jnp.exp(scores - jnp.max(scores, axis=0, keepdims=True))
        prob = weights * (1.0 / jnp.sum(weights, axis=0, keepdims=True))
        dprob = nt(values_h, grads)
        delta = jnp.sum(prob * dprob, axis=0, keepdims=True)
        dscore = (prob * (dprob - delta) * scale).astype(BF16)
        prob = prob.astype(BF16)
        dkey = dkey + nn(dscore, queries * own)
        dvalue = dvalue + nn(prob, grads * own)
        prob_parts.append(prob)
        dscore_parts.append(dscore)
        key_parts.append(keys_h)
        value_parts.append(values_h)
    prob_all = jnp.concatenate(prob_parts, axis=0)
    dscore_all = jnp.concatenate(dscore_parts, axis=0)
    attended[rows, columns(0)] = tn(prob_all, jnp.concatenate(value_parts, axis=0)).astype(BF16)
    dqkv[rows, columns(0)] = tn(dscore_all, jnp.concatenate(key_parts, axis=0)).astype(BF16)
    dqkv[rows, columns(feature)] = dkey.astype(BF16)
    dqkv[rows, columns(2 * feature)] = dvalue.astype(BF16)


def block_kernel(
    place, x_ref, dy_ref, gain_ref, w_qkv_ref, w_out_ref,
    drolled_ref, keep_ref, send_ref,
    normed_ref, hidden_ref, qkv_ref, d_attn_ref, attended_ref, dqkv_ref, total_ref,
):
    last = place[0]
    core = place[1]
    feature = HEADS * HEAD_DIM
    values = x_ref[...].astype(F32)
    centred = values - jnp.mean(values, axis=-1, keepdims=True)
    inverse = lax.rsqrt(jnp.mean(centred * centred, axis=-1, keepdims=True) + 1e-05)
    normed_ref[...] = centred * inverse
    hidden_ref[...] = (normed_ref[...] * gain_ref[...]).astype(BF16)
    qkv_ref[...] = nn(hidden_ref[...], w_qkv_ref[...]).astype(BF16)
    d_attn_ref[...] = nt(dy_ref[...], w_out_ref[...]).astype(BF16)

    groups = HEADS // GROUP

    @pl.loop(0, (TOKENS // WINDOW) * groups)
    def _(step):
        attention_group(
            step // groups, step % groups, last, qkv_ref, d_attn_ref, attended_ref, dqkv_ref
        )

    total_ref[:, 0 : 3 * feature] = tn(hidden_ref[...], dqkv_ref[...]).astype(BF16)
    total_ref[:, 3 * feature : 4 * feature] = tn(attended_ref[...], dy_ref[...]).astype(BF16)
    dhidden = nt(dqkv_ref[...], w_qkv_ref[...])
    normed = normed_ref[...]
    gain_local = jnp.sum(dhidden * normed, axis=0, keepdims=True)
    dnorm = dhidden * gain_ref[...]
    drolled = dy_ref[...].astype(F32) + inverse * (
        dnorm
        - jnp.mean(dnorm, axis=-1, keepdims=True)
        - normed * jnp.mean(dnorm * normed, axis=-1, keepdims=True)
    )
    drolled_ref[...] = drolled.astype(BF16)

    coarse = gain_local.astype(BF16)
    fine = (gain_local - coarse.astype(F32)).astype(BF16)
    gain_rows = [coarse[:, 128 * j : 128 * (j + 1)] for j in range(4)]
    gain_rows += [fine[:, 128 * j : 128 * (j + 1)] for j in range(4)]
    gain_tile = jnp.concatenate(
        [row.astype(F32) for row in gain_rows] + [jnp.zeros((8, 128), F32)], axis=0
    ).astype(BF16)

    @pl.loop(0, 16)
    def _(chunk):
        for half, out in ((core, keep_ref), (1 - core, send_ref)):
            start = pl.multiple_of(half * 256 + chunk * 16, 16)
            rows = total_ref[pl.ds(start, 16), :]
            for j in range(16):
                out[chunk, j] = rows[:, 128 * j : 128 * (j + 1)]
            out[chunk, 16] = gain_tile


def block(place, tokens, grads, norm_gain, w_qkv, w_out):
    feature = HEADS * HEAD_DIM
    vmem = pl.BlockSpec(memory_space=pltpu.VMEM)
    chunks = jax.ShapeDtypeStruct((16, 17, 16, 128), BF16)
    return pl.pallas_call(
        block_kernel,
        out_shape=(jax.ShapeDtypeStruct((TOKENS, feature), BF16), chunks, chunks),
        in_specs=[pl.BlockSpec(memory_space=pltpu.SMEM)] + [vmem] * 5,
        out_specs=(vmem, vmem, vmem),
        scratch_shapes=[
            pltpu.VMEM((TOKENS, feature), F32),
            pltpu.VMEM((TOKENS, feature), BF16),
            pltpu.VMEM((TOKENS, 3 * feature), BF16),
            pltpu.VMEM((TOKENS, feature), BF16),
            pltpu.VMEM((TOKENS, feature), BF16),
            pltpu.VMEM((TOKENS, 3 * feature), BF16),
            pltpu.VMEM((feature, 4 * feature), BF16),
        ],
        compiler_params=pltpu.CompilerParams(vmem_limit_bytes=40 * 1024 * 1024),
        cost_estimate=pl.CostEstimate(
            flops=2_000_000_000, bytes_accessed=6_000_000, transcendentals=700_000
        ),
        name="window_block",
    )(place, tokens, grads, norm_gain, w_qkv, w_out)


def index(zh, y, x, zl, c):
    return (((zh * 4 + y) * 4 + x) * 8 + zl) * 2 + c


def fetch_lon(pieces, diagonal):
    inside = [(i + 1, i) for i in range(32) if i % 16 != 15]
    normal = lax.ppermute(pieces, LON, inside)
    normal_diagonal = lax.ppermute(
        diagonal, ALL,
        [((i + 1) * 16 + (j + 1) % 16, i * 16 + j) for i in range(32) if i % 16 != 15 for j in range(16)],
    )
    crossing = []
    for k, (y, x) in enumerate(MIDS):
        shift = 1 if k == 3 else 0
        out, across = [], []
        for zh in range(2):
            for lat in range(16):
                zl, c = lat // 2, lat % 2
                source = (lat + shift) % 16
                middle = index(zh, y, x, zl, c)
                out.append((index(zh, 0, 0, source // 2, source % 2), middle))
                across.append((middle, index(1 - zh, 3, 3, zl, c)))
        part = diagonal if k == 3 else pieces[k]
        crossing.append(lax.ppermute(lax.ppermute(part, ALL, out), ALL, across))
    east = lax.axis_index(LON) % 16 == 15
    arrived = [jnp.where(east, crossing[k], normal[k]) for k in range(3)]
    return arrived + [jnp.where(east, crossing[3], normal_diagonal)]


def per_device(block_input, cotangent, norm_gain, w_qkv, w_out):
    half_lat, half_lon = WLAT // 2, WLON // 2
    levels, lat_rows, lon_cols, feature = block_input.shape
    stacked = jnp.stack([block_input, cotangent])

    def part(row, col):
        return stacked[:, :, row : row + half_lat, col : col + half_lon].reshape(2, BLOCK, feature)

    west = jnp.stack([part(row, 0) for row in (3, 6, 9)])
    diagonal = part(0, 0)
    lat_block = lax.ppermute(part(0, half_lon), LAT, [((i + 1) % 16, i) for i in range(16)])
    p0, p1, p2, corner = fetch_lon(west, diagonal)
    own = [part(row, half_lon) for row in (3, 6, 9)]
    tokens = jnp.concatenate([own[0], own[1], p0, p1, own[2], p2, lat_block, corner], axis=1)
    last = (lax.axis_index(LAT) == lax.axis_size("zl") * lax.axis_size("c") - 1).astype(jnp.int32)
    place = jnp.stack([last, lax.axis_index("c").astype(jnp.int32)])
    drolled, keep, send = block(
        place, tokens[0], tokens[1], norm_gain.reshape(1, feature), w_qkv, w_out
    )

    parts = drolled.reshape(8, BLOCK, feature)
    back_lon = lax.ppermute(
        jnp.stack([parts[2], parts[3], parts[5]]), LON, [(i, (i + 1) % 32) for i in range(32)]
    )
    back_lat = lax.ppermute(parts[6], LAT, [(i, (i + 1) % 16) for i in range(16)])
    back_corner = lax.ppermute(
        parts[7], ALL,
        [(i * 16 + j, ((i + 1) % 32) * 16 + (j + 1) % 16) for i in range(32) for j in range(16)],
    )

    def grid(piece):
        return piece.reshape(levels, half_lat, half_lon, feature)

    top = jnp.concatenate([grid(back_corner), grid(back_lat)], axis=2)
    rest = [
        jnp.concatenate([grid(back_lon[k]), grid(parts[own_at])], axis=2)
        for k, own_at in enumerate((0, 1, 4))
    ]
    input_grad = jnp.concatenate([top] + rest, axis=1)

    other = lax.ppermute(send, "c", [(0, 1), (1, 0)])
    pair = (keep.astype(F32) + other.astype(F32)).astype(BF16)
    plane = lax.all_to_all(pair, ("y", "x"), 0, 0, tiled=True)
    plane = jnp.sum(plane.astype(F32), axis=0)
    gain_part = jnp.broadcast_to(plane[16].astype(BF16), (16, 16, 128))
    column = lax.all_to_all(
        jnp.stack([plane[:16].astype(BF16), gain_part], axis=1), ("zh", "zl"), 0, 0, tiled=True
    )
    column = jnp.sum(column.astype(F32), axis=0)
    gain_rows = column[1]
    gain_grad = (gain_rows[0:4] + gain_rows[4:8]).reshape(feature)
    final = column[0].astype(BF16)
    fan = jnp.broadcast_to(final, (32, 16, 128))
    gathered = lax.all_to_all(fan, ("zh", "zl", "c"), 0, 0, tiled=True)
    gathered = gathered.reshape(16, 2, 16, 128)
    mine = lax.dynamic_index_in_dim(gathered, lax.axis_index("zh"), axis=1, keepdims=False)
    weights = mine.transpose(1, 0, 2).reshape(16, 4 * feature).astype(F32)
    return input_grad, weights[:, : 3 * feature], weights[:, 3 * feature :], gain_grad


def solution(mesh):
    fine = Mesh(mesh.devices.reshape(2, 4, 4, 8, 2), ALL)
    grid_spec = P(None, LAT, LON, None)
    return jax.shard_map(
        per_device,
        mesh=fine,
        in_specs=(grid_spec, grid_spec, P(), P(), P()),
        out_specs=(grid_spec, P(LON, None), P(LON, None), P()),
        check_vma=False,
    )
```

time: 924 us -> 163 us (0.18)
  waiting for transfers between devices: 703 us -> 31.2 us
  blocking collectives: 112 us -> 38.8 us
  matrix products: 40.1 us -> 0 us
  starting transfers between devices: 28.3 us -> 68 us
  Pallas kernels: 0 us -> 13.9 us
  between operations: 14 us -> 1.28 us
    reduce_scatter x2 -> x0, waiting for transfers between devices: 498 us -> none  [the longest x1 339 us: reduce_weights(): lax.psum_scatter(band_sums[0].astype(jnp.bfloat16), 'lon', scatter_dimens...]
    psum x1 -> x0, waiting for transfers between devices: 177 us -> none  [reduce_weights(): lax.psum(terms[0].astype(jnp.bfloat16), 'lat').astype(jnp.float32)]
    psum x1 -> x0, blocking collectives: 112 us -> none  [per_device(): gain_grad = lax.psum(gain_local, ('lon', 'lat'))]
    dot_general x17 -> x0, matrix products: 40.1 us -> none  [the longest x2 9.18 us: window_step(): jnp.einsum('hqk,khd->qhd', dscore, keys_win, preferred_element_type=jnp.f...]
    all_to_all x0 -> x1, blocking collectives: none -> 38.8 us  [per_device(): plane = lax.all_to_all(pair, ('y', 'x'), 0, 0, tiled=True)]
    all_to_all x0 -> x2, starting transfers between devices: none -> 24 us  [the longest x1 14.9 us: per_device(): gathered = lax.all_to_all(fan, ('zh', 'zl', 'c'), 0, 0, tiled=True)]
    ppermute x4 -> x15, starting transfers between devices: 28.2 us -> 43.9 us  [the longest x8 26.5 us: fetch_lon(): crossing.append(lax.ppermute(lax.ppermute(part, ALL, out), ALL, across))]
    all_to_all x0 -> x2, waiting for transfers between devices: none -> 14 us  [the longest x1 14 us: per_device(): gathered = lax.all_to_all(fan, ('zh', 'zl', 'c'), 0, 0, tiled=True)]
  transfers between devices with their start and end apart: 7 -> 17, of which waited for: 6 -> 4; matrix products, arithmetic and copies ran while one was open for 1% -> 2% of each run, Pallas kernels for 0% -> 0%
where the time goes in v1:
time: 163 us; the launch traced here: 162 us
  starting transfers between devices  68 us (42%)
  blocking collectives  38.8 us (24%)
  waiting for transfers between devices  31.2 us (19%)
  Pallas kernels  13.9 us (9%)
  local copies, waits for them, and re-layouts  5.27 us (3%)
  other arithmetic  3.91 us (2%)
    all_to_all x1, blocking collectives, per_device(): plane = lax.all_to_all(pair, ('y', 'x'), 0, 0, tiled=True)  38.8 us
    ppermute x8, starting transfers between devices, fetch_lon(): crossing.append(lax.ppermute(lax.ppermute(part, ALL, out), ALL, across))  26.5 us
    all_to_all x1, starting transfers between devices, per_device(): gathered = lax.all_to_all(fan, ('zh', 'zl', 'c'), 0, 0, tiled=True)  14.9 us
    all_to_all x1, waiting for transfers between devices, per_device(): gathered = lax.all_to_all(fan, ('zh', 'zl', 'c'), 0, 0, tiled=True)  14 us
    pallas_call x1, Pallas kernels, block(): pl.pallas_call(block_kernel, out_shape=(jax.ShapeDtypeStruct((TOKENS, fea...  13.9 us
    all_to_all x1, starting transfers between devices, per_device(): lax.all_to_all(jnp.stack([plane[:16].astype(BF16), gain_part], axis=1), (...  9.06 us
    ppermute x1, waiting for transfers between devices, per_device(): lax.ppermute(parts[7], ALL, [(i * 16 + j, (i + 1) % 32 * 16 + (j + 1) % 1...  8.79 us
    ppermute x1, waiting for transfers between devices, fetch_lon(): normal = lax.ppermute(pieces, LON, inside)  6.03 us
  transfers between devices with their start and end apart: 17, of which 4 were waited for; matrix products, arithmetic and copies ran while one was open for 2% of the time, Pallas kernels for 0%

profile of v1, /device:TPU:1, one launch (start us, length us, event | category | flops | bytes accessed | tf_op | source)
XLA Modules:
  0.0 162.4 jit_solution(4813772789224248461)
XLA Ops:
  0.6 0.0 copy-start.3
  0.7 1.5 pad_maximum_fusion.3
  2.2 0.1 copy.94
  2.3 1.3 collective-permute-start.10
  3.6 19.9 %collective-permute-start.8 = (bf16[2,36,512]{2,1,0:T(8,128)(2,1)S(1)}, bf16[2,36,512]{2,1,0:T(8,128)(2,1)S(1)}, u32[]{:S(2)}, u32[]{:S(2)}) collective-permute-start(bf16[2,36,512]{2,1,0:T(8,128)(2,1)S(1)} %copy.95), channel_id=1, source_target_pairs={{1,160},{2,161},{3,162},{4,163},{5,164},{6,165},{7,166},{8,167},{9... | collective-permute-start | bytes 221192 | tf_op jit(solution)/shard_map/ppermute | solution.py:193
  23.6 0.3 slice_maximum_fusion
  23.9 0.1 copy.83
  24.0 1.3 collective-permute-start.5
  25.3 0.1 copy.79
  25.4 1.3 collective-permute-start
  26.7 0.1 copy.82
  26.8 1.3 collective-permute-start.3
  28.1 0.1 copy.92
  28.2 0.1 copy.89
  28.3 0.1 copy.77
  28.4 0.1 copy.78
  28.5 0.0 collective-permute-done.8
  28.5 0.7 collective-permute-start.9
  29.2 0.1 pad_add_fusion.place
  29.3 0.0 collective-permute-done.5
  29.3 2.6 %collective-permute-start.7 = (bf16[2,36,512]{2,1,0:T(8,128)(2,1)S(1)}, bf16[2,36,512]{2,1,0:T(8,128)(2,1)S(1)}, u32[]{:S(2)}, u32[]{:S(2)}) collective-permute-start(bf16[2,36,512]{2,1,0:T(8,128)(2,1)S(1)} %copy.93), channel_id=1, source_target_pairs={{1,0},{2,1},{3,2},{4,3},{5,4},{6,5},{7,6},{8,7},{9,8},{10,9},{11,1... | collective-permute-start | bytes 221192 | tf_op jit(solution)/shard_map/ppermute | solution.py:209
  31.9 0.0 collective-permute-done
  31.9 1.3 collective-permute-start.2
  33.2 0.0 collective-permute-done.3
  33.2 0.7 collective-permute-start.6
  33.9 0.0 collective-permute-done.10
  33.9 0.7 collective-permute-start.1
  34.6 0.0 collective-permute-done.9
  34.6 0.7 collective-permute-start.4
  35.3 0.0 collective-permute-done.6
  35.3 0.0 collective-permute-done.1
  35.3 0.0 collective-permute-done.4
  35.3 6.0 %collective-permute-done.2 = bf16[3,2,36,512]{3,2,1,0:T(8,128)(2,1)S(1)} collective-permute-done((bf16[3,2,36,512]{3,2,1,0:T(8,128)(2,1)S(1)}, bf16[3,2,36,512]{3,2,1,0:T(8,128)(2,1)S(1)}, u32[]{:S(2)}, u32[]{:S(2)}) %collective-permute-start.2) | collective-permute-done | bytes 221216 | tf_op jit(solution)/shard_map/ppermute | solution.py:176
  41.4 0.0 collective-permute-done.7
  41.4 0.0 copy-start
  41.4 0.0 copy-start.1
  41.4 0.0 copy-start.2
  41.4 0.7 concatenate.18
  42.2 0.6 copy-done
  42.8 0.1 copy-done.1
  42.9 0.0 copy-done.2
  42.9 13.9 %window_block.1 = (bf16[288,512]{1,0:T(8,128)(2,1)S(1)}, bf16[16,17,16,128]{3,2,1,0:T(8,128)(2,1)S(1)}, bf16[16,17,16,128]{3,2,1,0:T(8,128)(2,1)S(1)}) custom-call(s32[2]{0:T(128)S(1)} %pad_add_fusion.place, bf16[288,512]{1,0:T(8,128)(2,1)S(1)} %get-tuple-element.23.x_ref, bf16[288,512]{1,0:T(8,128)(2,1)S(1)} %get-tuple-element.22.dy_ref, ...), custom_call_target="tpu_custom_call" | custom-call | flops 2000000000 | bytes 6000000 | tf_op jit(solution)/shard_map/window_block/pallas_call | solution.py:148
  56.8 2.7 %collective-permute-start.14 = (bf16[16,17,16,128]{3,2,1,0:T(8,128)(2,1)S(1)}, bf16[16,17,16,128]{3,2,1,0:T(8,128)(2,1)S(1)}, u32[]{:S(2)}, u32[]{:S(2)}) collective-permute-start(bf16[16,17,16,128]{3,2,1,0:T(8,128)(2,1)S(1)} %get-tuple-element.9), channel_id=1, source_target_pairs={{0,1},{1,0},{2,3},{3,2},{4,5},{5,4},{6,7},{7,6},{8,9},{9,8},{10,11... | collective-permute-start | bytes 3342344 | tf_op jit(solution)/shard_map/ppermute | solution.py:239
  59.6 2.4 %collective-permute-done.14 = bf16[16,17,16,128]{3,2,1,0:T(8,128)(2,1)S(1)} collective-permute-done((bf16[16,17,16,128]{3,2,1,0:T(8,128)(2,1)S(1)}, bf16[16,17,16,128]{3,2,1,0:T(8,128)(2,1)S(1)}, u32[]{:S(2)}, u32[]{:S(2)}) %collective-permute-start.14) | collective-permute-done | bytes 1114144 | tf_op jit(solution)/shard_map/ppermute | solution.py:239
  62.0 0.3 add_convert_fusion
  62.2 38.8 %all_to_all.15 = bf16[16,17,16,128]{3,2,1,0:T(8,128)(2,1)S(1)} all-to-all(bf16[16,17,16,128]{3,2,1,0:T(8,128)(2,1)S(1)} %add_convert_fusion), channel_id=1, replica_groups=mesh['zh'=2,'y'=4,'x'=4,'zl'=8,'c'=2] {'y','x'}, dimensions={0} | all-to-all | bytes 2228224 | tf_op jit(solution)/shard_map/all_to_all | solution.py:241
  101.1 0.2 reduce
  101.3 0.7 pad_maximum_fusion.1
  101.9 9.1 %all-to-all-start.1 = ((bf16[16,2,16,128]{3,2,1,0:T(8,128)(2,1)}), bf16[16,2,16,128]{3,2,1,0:T(8,128)(2,1)S(1)}, u32[]{:S(2)}, u32[]{:S(2)}) async-start(bf16[16,2,16,128]{3,2,1,0:T(8,128)(2,1)} %pad_maximum_fusion.1), calls=%async_computation.1 | async-start | bytes 262144 | tf_op jit(solution)/shard_map/all_to_all | solution.py:244
  111.1 5.3 %collective-permute-start.11 = (bf16[36,512]{1,0:T(8,128)(2,1)S(1)}, bf16[36,512]{1,0:T(8,128)(2,1)S(1)}, u32[]{:S(2)}, u32[]{:S(2)}) collective-permute-start(bf16[36,512]{1,0:T(8,128)(2,1)S(1)} %get-tuple-element.32), channel_id=1, source_target_pairs={{0,17},{1,18},{2,19},{3,20},{4,21},{5,22},{6,23},{7,24},{8,25},{9,... | collective-permute-start | bytes 110600 | tf_op jit(solution)/shard_map/ppermute | solution.py:224
  116.4 1.9 %collective-permute-start.12 = (bf16[36,512]{1,0:T(8,128)(2,1)S(1)}, bf16[36,512]{1,0:T(8,128)(2,1)S(1)}, u32[]{:S(2)}, u32[]{:S(2)}) collective-permute-start(bf16[36,512]{1,0:T(8,128)(2,1)S(1)} %get-tuple-element.39), channel_id=1, source_target_pairs={{0,1},{1,2},{2,3},{3,4},{4,5},{5,6},{6,7},{7,8},{8,9},{9,10},{10,1... | collective-permute-start | bytes 110600 | tf_op jit(solution)/shard_map/ppermute | solution.py:223
  118.4 2.3 %collective-permute-start.13 = (bf16[3,36,512]{2,1,0:T(8,128)(2,1)S(1)}, bf16[3,36,512]{2,1,0:T(8,128)(2,1)S(1)}, u32[]{:S(2)}, u32[]{:S(2)}) collective-permute-start(bf16[3,36,512]{2,1,0:T(8,128)(2,1)S(1)} %pad_maximum_fusion.2), channel_id=1, source_target_pairs={{0,16},{16,32},{32,48},{48,64},{64,80},{80,96},{96,112},{112,128},... | collective-permute-start | bytes 331784 | tf_op jit(solution)/shard_map/ppermute | solution.py:220
  120.7 8.8 %collective-permute-done.11 = bf16[36,512]{1,0:T(8,128)(2,1)S(1)} collective-permute-done((bf16[36,512]{1,0:T(8,128)(2,1)S(1)}, bf16[36,512]{1,0:T(8,128)(2,1)S(1)}, u32[]{:S(2)}, u32[]{:S(2)}) %collective-permute-start.11) | collective-permute-done | bytes 36896 | tf_op jit(solution)/shard_map/ppermute | solution.py:224
  129.6 0.0 collective-permute-done.12
  129.6 0.0 all-to-all-done.1
  129.6 0.7 broadcast_in_dim.3
  130.3 14.9 %all-to-all-start.2 = ((bf16[32,16,128]{2,1,0:T(8,128)(2,1)}), bf16[32,16,128]{2,1,0:T(8,128)(2,1)S(1)}, u32[]{:S(2)}, u32[]{:S(2)}) async-start(bf16[32,16,128]{2,1,0:T(8,128)(2,1)} %broadcast_in_dim.3), calls=%async_computation.2 | async-start | bytes 262144 | tf_op jit(solution)/shard_map/all_to_all | solution.py:252
  145.2 0.0 collective-permute-done.13
  145.4 0.1 maximum_maximum_fusion
  145.5 1.0 copy.101
  146.5 0.6 fusion.4
  147.1 14.0 %all-to-all-done.2 = bf16[32,16,128]{2,1,0:T(8,128)(2,1)S(1)} async-done(((bf16[32,16,128]{2,1,0:T(8,128)(2,1)}), bf16[32,16,128]{2,1,0:T(8,128)(2,1)S(1)}, u32[]{:S(2)}, u32[]{:S(2)}) %all-to-all-start.2) | async-done | bytes 131104 | tf_op jit(solution)/shard_map/all_to_all | solution.py:252
  161.1 0.6 slice.175
  161.7 0.6 slice.174
  (35 shorter events, 0.5 us)
Async XLA Ops:
  0.6 22.9 %copy-start.3 = (bf16[2,12,12,512]{3,0,2,1:T(2,128)(2,1)S(1)}, bf16[2,12,12,512]{3,0,2,1:T(2,128)(2,1)}, u32[]{:S(2)}) copy-start(bf16[2,12,12,512]{3,0,2,1:T(2,128)(2,1)} %param.6) | copy-start | bytes 884740
  0.6 22.9 %copy-start.4 = (bf16[2,12,12,512]{3,0,2,1:T(2,128)(2,1)S(1)}, bf16[2,12,12,512]{3,0,2,1:T(2,128)(2,1)}, u32[]{:S(2)}) copy-start(bf16[2,12,12,512]{3,0,2,1:T(2,128)(2,1)} %param.5) | copy-start | bytes 884740
  2.3 31.6 %collective-permute-start.10 = (bf16[2,36,512]{2,1,0:T(8,128)(2,1)S(1)}, bf16[2,36,512]{2,1,0:T(8,128)(2,1)S(1)}, u32[]{:S(2)}, u32[]{:S(2)}) collective-permute-start(bf16[2,36,512]{2,1,0:T(8,128)(2,1)S(1)} %copy.95), channel_id=1, source_target_pairs={{17,0},{18,1},{19,2},{20,3},{21,4},{22,5},{23,6},{24,7},{25,8},{26... | collective-permute-start | bytes 221192 | tf_op jit(solution)/shard_map/ppermute | solution.py:177
  3.6 24.9 %collective-permute-start.8 = (bf16[2,36,512]{2,1,0:T(8,128)(2,1)S(1)}, bf16[2,36,512]{2,1,0:T(8,128)(2,1)S(1)}, u32[]{:S(2)}, u32[]{:S(2)}) collective-permute-start(bf16[2,36,512]{2,1,0:T(8,128)(2,1)S(1)} %copy.95), channel_id=1, source_target_pairs={{1,160},{2,161},{3,162},{4,163},{5,164},{6,165},{7,166},{8,167},{9... | collective-permute-start | bytes 221192 | tf_op jit(solution)/shard_map/ppermute | solution.py:193
  24.0 5.3 %collective-permute-start.5 = (bf16[2,36,512]{2,1,0:T(8,128)(2,1)S(1)}, bf16[2,36,512]{2,1,0:T(8,128)(2,1)S(1)}, u32[]{:S(2)}, u32[]{:S(2)}) collective-permute-start(bf16[2,36,512]{2,1,0:T(8,128)(2,1)S(1)} %copy.91), channel_id=1, source_target_pairs={{0,96},{1,97},{2,98},{3,99},{4,100},{5,101},{6,102},{7,103},{8,104... | collective-permute-start | bytes 221192 | tf_op jit(solution)/shard_map/ppermute | solution.py:193
  25.4 6.5 %collective-permute-start = (bf16[2,36,512]{2,1,0:T(8,128)(2,1)S(1)}, bf16[2,36,512]{2,1,0:T(8,128)(2,1)S(1)}, u32[]{:S(2)}, u32[]{:S(2)}) collective-permute-start(bf16[2,36,512]{2,1,0:T(8,128)(2,1)S(1)} %copy.80), channel_id=1, source_target_pairs={{0,80},{1,81},{2,82},{3,83},{4,84},{5,85},{6,86},{7,87},{8,88},{9,... | collective-permute-start | bytes 221192 | tf_op jit(solution)/shard_map/ppermute | solution.py:193
  26.8 6.4 %collective-permute-start.3 = (bf16[2,36,512]{2,1,0:T(8,128)(2,1)S(1)}, bf16[2,36,512]{2,1,0:T(8,128)(2,1)S(1)}, u32[]{:S(2)}, u32[]{:S(2)}) collective-permute-start(bf16[2,36,512]{2,1,0:T(8,128)(2,1)S(1)} %copy.88), channel_id=1, source_target_pairs={{0,144},{1,145},{2,146},{3,147},{4,148},{5,149},{6,150},{7,151},{8... | collective-permute-start | bytes 221192 | tf_op jit(solution)/shard_map/ppermute | solution.py:193
  28.5 6.0 %collective-permute-start.9 = (bf16[2,36,512]{2,1,0:T(8,128)(2,1)S(1)}, bf16[2,36,512]{2,1,0:T(8,128)(2,1)S(1)}, u32[]{:S(2)}, u32[]{:S(2)}) collective-permute-start(bf16[2,36,512]{2,1,0:T(8,128)(2,1)S(1)} %collective-permute-done.8), channel_id=1, source_target_pairs={{160,496},{161,497},{162,498},{163,499},{164,500},{165,501},{166,5... | collective-permute-start | bytes 221192 | tf_op jit(solution)/shard_map/ppermute | solution.py:193
  29.3 12.1 %collective-permute-start.7 = (bf16[2,36,512]{2,1,0:T(8,128)(2,1)S(1)}, bf16[2,36,512]{2,1,0:T(8,128)(2,1)S(1)}, u32[]{:S(2)}, u32[]{:S(2)}) collective-permute-start(bf16[2,36,512]{2,1,0:T(8,128)(2,1)S(1)} %copy.93), channel_id=1, source_target_pairs={{1,0},{2,1},{3,2},{4,3},{5,4},{6,5},{7,6},{8,7},{9,8},{10,9},{11,1... | collective-permute-start | bytes 221192 | tf_op jit(solution)/shard_map/ppermute | solution.py:209
  31.9 9.4 %collective-permute-start.2 = (bf16[3,2,36,512]{3,2,1,0:T(8,128)(2,1)S(1)}, bf16[3,2,36,512]{3,2,1,0:T(8,128)(2,1)S(1)}, u32[]{:S(2)}, u32[]{:S(2)}) collective-permute-start(bf16[3,2,36,512]{3,2,1,0:T(8,128)(2,1)S(1)} %pad_maximum_fusion), channel_id=1, source_target_pairs={{16,0},{32,16},{48,32},{64,48},{80,64},{96,80},{112,96},{128,112},... | collective-permute-start | bytes 663560 | tf_op jit(solution)/shard_map/ppermute | solution.py:176
  33.2 2.1 %collective-permute-start.6 = (bf16[2,36,512]{2,1,0:T(8,128)(2,1)S(1)}, bf16[2,36,512]{2,1,0:T(8,128)(2,1)S(1)}, u32[]{:S(2)}, u32[]{:S(2)}) collective-permute-start(bf16[2,36,512]{2,1,0:T(8,128)(2,1)S(1)} %collective-permute-done.5), channel_id=1, source_target_pairs={{96,496},{97,497},{98,498},{99,499},{100,500},{101,501},{102,502},... | collective-permute-start | bytes 221192 | tf_op jit(solution)/shard_map/ppermute | solution.py:193
  33.9 1.4 collective-permute-start.1
  34.6 0.7 collective-permute-start.4
  41.4 1.4 copy-start
  41.4 1.5 copy-start.1
  41.4 1.5 copy-start.2
  56.8 5.1 %collective-permute-start.14 = (bf16[16,17,16,128]{3,2,1,0:T(8,128)(2,1)S(1)}, bf16[16,17,16,128]{3,2,1,0:T(8,128)(2,1)S(1)}, u32[]{:S(2)}, u32[]{:S(2)}) collective-permute-start(bf16[16,17,16,128]{3,2,1,0:T(8,128)(2,1)S(1)} %get-tuple-element.9), channel_id=1, source_target_pairs={{0,1},{1,0},{2,3},{3,2},{4,5},{5,4},{6,7},{7,6},{8,9},{9,8},{10,11... | collective-permute-start | bytes 3342344 | tf_op jit(solution)/shard_map/ppermute | solution.py:239
  101.9 27.7 %all-to-all-start.1 = ((bf16[16,2,16,128]{3,2,1,0:T(8,128)(2,1)}), bf16[16,2,16,128]{3,2,1,0:T(8,128)(2,1)S(1)}, u32[]{:S(2)}, u32[]{:S(2)}) async-start(bf16[16,2,16,128]{3,2,1,0:T(8,128)(2,1)} %pad_maximum_fusion.1), calls=%async_computation.1 | async-start | bytes 262144 | tf_op jit(solution)/shard_map/all_to_all | solution.py:244
  111.1 18.5 %collective-permute-start.11 = (bf16[36,512]{1,0:T(8,128)(2,1)S(1)}, bf16[36,512]{1,0:T(8,128)(2,1)S(1)}, u32[]{:S(2)}, u32[]{:S(2)}) collective-permute-start(bf16[36,512]{1,0:T(8,128)(2,1)S(1)} %get-tuple-element.32), channel_id=1, source_target_pairs={{0,17},{1,18},{2,19},{3,20},{4,21},{5,22},{6,23},{7,24},{8,25},{9,... | collective-permute-start | bytes 110600 | tf_op jit(solution)/shard_map/ppermute | solution.py:224
  116.4 13.2 %collective-permute-start.12 = (bf16[36,512]{1,0:T(8,128)(2,1)S(1)}, bf16[36,512]{1,0:T(8,128)(2,1)S(1)}, u32[]{:S(2)}, u32[]{:S(2)}) collective-permute-start(bf16[36,512]{1,0:T(8,128)(2,1)S(1)} %get-tuple-element.39), channel_id=1, source_target_pairs={{0,1},{1,2},{2,3},{3,4},{4,5},{5,6},{6,7},{7,8},{8,9},{9,10},{10,1... | collective-permute-start | bytes 110600 | tf_op jit(solution)/shard_map/ppermute | solution.py:223
  118.4 26.8 %collective-permute-start.13 = (bf16[3,36,512]{2,1,0:T(8,128)(2,1)S(1)}, bf16[3,36,512]{2,1,0:T(8,128)(2,1)S(1)}, u32[]{:S(2)}, u32[]{:S(2)}) collective-permute-start(bf16[3,36,512]{2,1,0:T(8,128)(2,1)S(1)} %pad_maximum_fusion.2), channel_id=1, source_target_pairs={{0,16},{16,32},{32,48},{48,64},{64,80},{80,96},{96,112},{112,128},... | collective-permute-start | bytes 331784 | tf_op jit(solution)/shard_map/ppermute | solution.py:220
  130.3 30.8 %all-to-all-start.2 = ((bf16[32,16,128]{2,1,0:T(8,128)(2,1)}), bf16[32,16,128]{2,1,0:T(8,128)(2,1)S(1)}, u32[]{:S(2)}, u32[]{:S(2)}) async-start(bf16[32,16,128]{2,1,0:T(8,128)(2,1)} %broadcast_in_dim.3), calls=%async_computation.2 | async-start | bytes 262144 | tf_op jit(solution)/shard_map/all_to_all | solution.py:252

commit v2 on v1

v2 whole, which is shorter than its diff:
```python
import functools
import math

import jax
import jax.numpy as jnp
from jax import lax
from jax.experimental import pallas as pl
from jax.experimental.pallas import tpu as pltpu
from jax.sharding import Mesh, PartitionSpec as P

HEADS = 16
HEAD_DIM = 32
WLAT = 6
WLON = 12
WINDOW = 144
TOKENS = 288
BLOCK = 36
GROUP = 4
BF16 = jnp.bfloat16
F32 = jnp.float32
LON = ("zh", "y", "x")
LAT = ("zl", "c")
ALL = LON + LAT
MIDS = ((0, 3), (3, 0), (3, 1), (1, 3))


def nn(a, b):
    return lax.dot_general(a, b, (((1,), (0,)), ((), ())), preferred_element_type=F32)


def nt(a, b):
    return lax.dot_general(a, b, (((1,), (1,)), ((), ())), preferred_element_type=F32)


def tn(a, b):
    return lax.dot_general(a, b, (((0,), (0,)), ((), ())), preferred_element_type=F32)


def attention_group(window, group, last, qkv, d_attn, attended, dqkv):
    feature = HEADS * HEAD_DIM
    width = GROUP * HEAD_DIM
    rows = pl.ds(pl.multiple_of(window * WINDOW, 16), WINDOW)
    at = group * width

    def columns(offset):
        return pl.ds(pl.multiple_of(at + offset, 128), width)

    queries = qkv[rows, columns(0)]
    keys = qkv[rows, columns(feature)]
    values = qkv[rows, columns(2 * feature)]
    grads = d_attn[rows, columns(0)]
    scale = 1.0 / math.sqrt(HEAD_DIM)
    lane_head = lax.broadcasted_iota(jnp.int32, (1, width), 1) // HEAD_DIM
    half = WINDOW // 2
    key_late = lax.broadcasted_iota(jnp.int32, (WINDOW, WINDOW), 0) >= half
    query_late = lax.broadcasted_iota(jnp.int32, (WINDOW, WINDOW), 1) >= half
    masked = jnp.logical_and(last == 1, window == 1)
    allowed = jnp.logical_or(key_late == query_late, jnp.logical_not(masked))

    dkey = jnp.zeros((WINDOW, width), F32)
    dvalue = jnp.zeros((WINDOW, width), F32)
    prob_parts, dscore_parts, key_parts, value_parts = [], [], [], []
    for head in range(GROUP):
        own = (lane_head == head).astype(BF16)
        keys_h = keys * own
        values_h = values * own
        scores = nt(keys_h, queries) * scale
        scores = jnp.where(allowed, scores, -jnp.inf)
        weights = jnp.exp(scores - jnp.max(scores, axis=0, keepdims=True))
        prob = weights * (1.0 / jnp.sum(weights, axis=0, keepdims=True))
        dprob = nt(values_h, grads)
        delta = jnp.sum(prob * dprob, axis=0, keepdims=True)
        dscore = (prob * (dprob - delta) * scale).astype(BF16)
        prob = prob.astype(BF16)
        dkey = dkey + nn(dscore, queries * own)
        dvalue = dvalue + nn(prob, grads * own)
        prob_parts.append(prob)
        dscore_parts.append(dscore)
        key_parts.append(keys_h)
        value_parts.append(values_h)
    prob_all = jnp.concatenate(prob_parts, axis=0)
    dscore_all = jnp.concatenate(dscore_parts, axis=0)
    attended[rows, columns(0)] = tn(prob_all, jnp.concatenate(value_parts, axis=0)).astype(BF16)
    dqkv[rows, columns(0)] = tn(dscore_all, jnp.concatenate(key_parts, axis=0)).astype(BF16)
    dqkv[rows, columns(feature)] = dkey.astype(BF16)
    dqkv[rows, columns(2 * feature)] = dvalue.astype(BF16)


def block_kernel(
    place, x_ref, dy_ref, gain_ref, w_qkv_ref, w_out_ref,
    drolled_ref, back_ref, hidden_ref, dqkv_ref, attended_ref, gain_tile_ref,
    normed_ref, qkv_ref, d_attn_ref,
):
    last = place[0]
    values = x_ref[...].astype(F32)
    centred = values - jnp.mean(values, axis=-1, keepdims=True)
    inverse = lax.rsqrt(jnp.mean(centred * centred, axis=-1, keepdims=True) + 1e-05)
    normed_ref[...] = centred * inverse
    hidden_ref[...] = (normed_ref[...] * gain_ref[...]).astype(BF16)
    qkv_ref[...] = nn(hidden_ref[...], w_qkv_ref[...]).astype(BF16)
    d_attn_ref[...] = nt(dy_ref[...], w_out_ref[...]).astype(BF16)

    groups = HEADS // GROUP

    @pl.loop(0, (TOKENS // WINDOW) * groups)
    def _(step):
        attention_group(
            step // groups, step % groups, last, qkv_ref, d_attn_ref, attended_ref, dqkv_ref
        )

    dhidden = nt(dqkv_ref[...], w_qkv_ref[...])
    normed = normed_ref[...]
    gain_local = jnp.sum(dhidden * normed, axis=0, keepdims=True)
    dnorm = dhidden * gain_ref[...]
    drolled = dy_ref[...].astype(F32) + inverse * (
        dnorm
        - jnp.mean(dnorm, axis=-1, keepdims=True)
        - normed * jnp.mean(dnorm * normed, axis=-1, keepdims=True)
    )
    drolled_ref[...] = drolled.astype(BF16)
    back_ref[0:72, :] = drolled[72:144].astype(BF16)
    back_ref[72:144, :] = drolled[180:252].astype(BF16)

    coarse = gain_local.astype(BF16)
    fine = (gain_local - coarse.astype(F32)).astype(BF16)
    rows = [part[:, 128 * j : 128 * (j + 1)] for part in (coarse, fine) for j in range(4)]
    gain_tile_ref[...] = jnp.concatenate(
        [row.astype(F32) for row in rows] + [jnp.zeros((8, 128), F32)], axis=0
    ).astype(BF16)


def block(place, tokens, grads, norm_gain, w_qkv, w_out):
    feature = HEADS * HEAD_DIM
    vmem = pl.BlockSpec(memory_space=pltpu.VMEM)

    def half(width):
        return jax.ShapeDtypeStruct((TOKENS, width), BF16)

    return pl.pallas_call(
        block_kernel,
        out_shape=(
            half(feature), jax.ShapeDtypeStruct((WINDOW, feature), BF16),
            half(feature), half(3 * feature), half(feature),
            jax.ShapeDtypeStruct((16, 128), BF16),
        ),
        in_specs=[pl.BlockSpec(memory_space=pltpu.SMEM)] + [vmem] * 5,
        out_specs=(vmem,) * 6,
        scratch_shapes=[
            pltpu.VMEM((TOKENS, feature), F32),
            pltpu.VMEM((TOKENS, 3 * feature), BF16),
            pltpu.VMEM((TOKENS, feature), BF16),
        ],
        compiler_params=pltpu.CompilerParams(vmem_limit_bytes=40 * 1024 * 1024),
        cost_estimate=pl.CostEstimate(
            flops=2_000_000_000, bytes_accessed=6_000_000, transcendentals=700_000
        ),
        name="window_block",
    )(place, tokens, grads, norm_gain, w_qkv, w_out)


def weights_kernel(
    place, hidden_ref, dqkv_ref, attended_ref, dy_ref, gain_tile_ref, keep_ref, send_ref, total_ref
):
    core = place[1]
    feature = HEADS * HEAD_DIM
    total_ref[:, 0 : 3 * feature] = tn(hidden_ref[...], dqkv_ref[...]).astype(BF16)
    total_ref[:, 3 * feature : 4 * feature] = tn(attended_ref[...], dy_ref[...]).astype(BF16)

    @pl.loop(0, 16)
    def _(chunk):
        for half, out in ((core, keep_ref), (1 - core, send_ref)):
            start = pl.multiple_of(half * 256 + chunk * 16, 16)
            rows = total_ref[pl.ds(start, 16), :]
            for j in range(16):
                out[chunk, j] = rows[:, 128 * j : 128 * (j + 1)]
            out[chunk, 16] = gain_tile_ref[...]


def weight_terms(place, hidden, dqkv, attended, grads, gain_tile):
    feature = HEADS * HEAD_DIM
    vmem = pl.BlockSpec(memory_space=pltpu.VMEM)
    chunks = jax.ShapeDtypeStruct((16, 17, 16, 128), BF16)
    return pl.pallas_call(
        weights_kernel,
        out_shape=(chunks, chunks),
        in_specs=[pl.BlockSpec(memory_space=pltpu.SMEM)] + [vmem] * 5,
        out_specs=(vmem, vmem),
        scratch_shapes=[pltpu.VMEM((feature, 4 * feature), BF16)],
        compiler_params=pltpu.CompilerParams(vmem_limit_bytes=40 * 1024 * 1024),
        cost_estimate=pl.CostEstimate(
            flops=40_000_000_000, bytes_accessed=100_000_000, transcendentals=0
        ),
        name="weight_terms",
    )(place, hidden, dqkv, attended, grads, gain_tile)


def index(zh, y, x, zl, c):
    return (((zh * 4 + y) * 4 + x) * 8 + zl) * 2 + c


def in_one_piece(work, start):
    once = jnp.minimum(lax.axis_index(LAT) + 1, 1)

    def body(turn, values):
        values, _ = lax.optimization_barrier((values, turn))
        return work(*values)

    return lax.fori_loop(0, once, body, start)


def middle_of(zh, lat):
    zl, c = lat // 2, lat % 2
    y, x = MIDS[(zl % 2) * 2 + c]
    return index(zh, y, x, zl, c)


def fetch(blocks, corner, top):
    out, out_corner, onward = [], [], []
    for zh in range(2):
        for lat in range(16):
            middle, target = middle_of(zh, lat), index(1 - zh, 3, 3, lat // 2, lat % 2)
            out.append((index(zh, 0, 0, lat // 2, lat % 2), middle))
            onward.append((middle, target))
            if lat < 15:
                out_corner.append((index(zh, 0, 0, (lat + 1) // 2, (lat + 1) % 2), middle))
            else:
                out_corner.append((index(zh, 0, 0, 0, 0), target))
    halfway = lax.ppermute(blocks, ALL, out)
    halfway_corner = lax.ppermute(corner, ALL, out_corner)
    halfway, halfway_corner, blocks, corner, top = lax.optimization_barrier(
        (halfway, halfway_corner, blocks, corner, top)
    )
    crossed = [
        lax.ppermute(part, ALL, onward)
        for part in (halfway[:2], jnp.stack([halfway[2], halfway_corner]))
    ]
    inner = [i for i in range(32) if i % 16 < 15]

    def usual(blocks, corner, top):
        return (
            lax.ppermute(blocks, LON, [(i + 1, i) for i in inner]),
            lax.ppermute(
                corner, ALL,
                [((i + 1) * 16 + (j + 1) % 16, i * 16 + j) for i in inner for j in range(16)],
            ),
            lax.ppermute(top, LAT, [((i + 1) % 16, i) for i in range(16)]),
        )

    normal, normal_corner, lat_block = in_one_piece(usual, (blocks, corner, top))
    *crossed, normal, normal_corner, lat_block = lax.optimization_barrier(
        (*crossed, normal, normal_corner, lat_block)
    )
    east = lax.axis_index(LON) % 16 == 15
    last = lax.axis_index(LAT) == 15
    across = (crossed[0][0], crossed[0][1], crossed[1][0])
    arrived = [jnp.where(east, across[k], normal[k]) for k in range(3)]
    over = jnp.where(last, halfway_corner, crossed[1][1])
    return arrived + [jnp.where(east, over, normal_corner)], lat_block


def per_device(block_input, cotangent, norm_gain, w_qkv, w_out):
    half_lat, half_lon = WLAT // 2, WLON // 2
    levels, lat_rows, lon_cols, feature = block_input.shape
    stacked = jnp.stack([block_input, cotangent])

    def part(row, col):
        return stacked[:, :, row : row + half_lat, col : col + half_lon].reshape(2, BLOCK, feature)

    west = jnp.stack([part(row, 0) for row in (3, 6, 9)])
    (p0, p1, p2, corner), lat_block = fetch(west, part(0, 0), part(0, half_lon))
    own = [part(row, half_lon) for row in (3, 6, 9)]
    tokens = jnp.concatenate([own[0], own[1], p0, p1, own[2], p2, corner, lat_block], axis=1)
    last = lax.axis_index(LAT) == 15
    place = jnp.stack([last, lax.axis_index("c")]).astype(jnp.int32)
    drolled, back, hidden, dqkv, attended, gain_tile = block(
        place, tokens[0], tokens[1], norm_gain.reshape(1, feature), w_qkv, w_out
    )

    back_lon = lax.ppermute(back, LON, [(i, (i + 1) % 32) for i in range(32)])

    def sum_in_plane(hidden, dqkv, attended, grads, gain_tile, _):
        keep, send = weight_terms(place, hidden, dqkv, attended, grads, gain_tile)
        other = lax.ppermute(send, "c", [(0, 1), (1, 0)])
        pair = (keep.astype(F32) + other.astype(F32)).astype(BF16)
        plane = lax.all_to_all(pair, ("y", "x"), 0, 0, tiled=True)
        return hidden, dqkv, attended, grads, gain_tile, jnp.sum(plane.astype(F32), axis=0)

    nothing = jnp.zeros((17, 16, 128), F32)
    *_, plane = in_one_piece(
        sum_in_plane, (hidden, dqkv, attended, tokens[1], gain_tile, nothing)
    )
    plane, back_lon = lax.optimization_barrier((plane, back_lon))
    back_lat = lax.ppermute(
        jnp.stack([drolled[252:288], back_lon[108:144]]), LAT,
        [(i, (i + 1) % 16) for i in range(16)],
    )
    gain_part = jnp.broadcast_to(plane[16].astype(BF16), (16, 16, 128))
    column = lax.all_to_all(
        jnp.stack([plane[:16].astype(BF16), gain_part], axis=1), ("zh", "zl"), 0, 0, tiled=True
    )
    column = jnp.sum(column.astype(F32), axis=0)
    gain_rows = column[1]
    gain_grad = (gain_rows[0:4] + gain_rows[4:8]).reshape(feature)
    final = column[0].astype(BF16)
    fan = jnp.broadcast_to(final, (32, 16, 128))
    gathered = lax.all_to_all(fan, ("zh", "zl", "c"), 0, 0, tiled=True)
    gathered = gathered.reshape(16, 2, 16, 128)
    mine = lax.dynamic_index_in_dim(gathered, lax.axis_index("zh"), axis=1, keepdims=False)
    weights = mine.transpose(1, 0, 2).reshape(16, 4 * feature).astype(F32)

    def grid(piece):
        return piece.reshape(levels, half_lat, half_lon, feature)

    rows = [
        (back_lat[1], back_lat[0]),
        (back_lon[0:36], drolled[0:36]),
        (back_lon[36:72], drolled[36:72]),
        (back_lon[72:108], drolled[144:180]),
    ]
    input_grad = jnp.concatenate(
        [jnp.concatenate([grid(west), grid(east)], axis=2) for west, east in rows], axis=1
    )
    return input_grad, weights[:, : 3 * feature], weights[:, 3 * feature :], gain_grad


def solution(mesh):
    fine = Mesh(mesh.devices.reshape(2, 4, 4, 8, 2), ALL)
    grid_spec = P(None, LAT, LON, None)
    return jax.shard_map(
        per_device,
        mesh=fine,
        in_specs=(grid_spec, grid_spec, P(), P(), P()),
        out_specs=(grid_spec, P(LON, None), P(LON, None), P()),
        check_vma=False,
    )
```

time: 163 us -> 150 us (0.920)
  blocking collectives: 38.8 us -> 0 us
  waiting for transfers between devices: 31.2 us -> 41 us
  starting transfers between devices: 68 us -> 76.4 us
  local copies, waits for them, and re-layouts: 5.27 us -> 8.33 us
  other arithmetic: 3.91 us -> 6.37 us
  Pallas kernels: 13.9 us -> 16 us
    all_to_all x1 -> x0, blocking collectives: 38.8 us -> none  [per_device(): plane = lax.all_to_all(pair, ('y', 'x'), 0, 0, tiled=True)]
    all_to_all x0 -> x1, starting transfers between devices: none -> 18.2 us  [sum_in_plane(): plane = lax.all_to_all(pair, ('y', 'x'), 0, 0, tiled=True)]
    all_to_all x0 -> x1, waiting for transfers between devices: none -> 17.1 us  [sum_in_plane(): plane = lax.all_to_all(pair, ('y', 'x'), 0, 0, tiled=True)]
    ppermute x15 -> x10, waiting for transfers between devices: 17.2 us -> 4.65 us  [the longest x1 2.36 us: sum_in_plane(): other = lax.ppermute(send, 'c', [(0, 1), (1, 0)])]
    all_to_all x1, starting transfers between devices: 14.9 us -> 7.66 us  [per_device(): gathered = lax.all_to_all(fan, ('zh', 'zl', 'c'), 0, 0, tiled=True)]
    all_to_all x1, waiting for transfers between devices: 0.01 us -> 5.32 us  [per_device(): lax.all_to_all(jnp.stack([plane[:16].astype(BF16), gain_part], axis=1), (...]
    ppermute x15 -> x10, starting transfers between devices: 43.9 us -> 40.3 us  [the longest x1 13.1 us: usual(): lax.ppermute(top, LAT, [((i + 1) % 16, i) for i in range(16)])]
    pallas_call x1 -> x2, Pallas kernels: 13.9 us -> 16 us  [the longest x1 13.2 us: block(): pl.pallas_call(block_kernel, out_shape=(half(feature), jax.ShapeDtypeStru...]
  transfers between devices with their start and end apart: 17 -> 13, of which waited for: 4 -> 6; matrix products, arithmetic and copies ran while one was open for 2% -> 5% of each run, Pallas kernels for 0% -> 2%
where the time goes in v2:
time: 150 us; the launch traced here: 149 us
  starting transfers between devices  76.4 us (51%)
  waiting for transfers between devices  41 us (27%)
  Pallas kernels  16 us (11%)
  local copies, waits for them, and re-layouts  8.33 us (6%)
  other arithmetic  6.37 us (4%)
    all_to_all x1, starting transfers between devices, sum_in_plane(): plane = lax.all_to_all(pair, ('y', 'x'), 0, 0, tiled=True)  18.2 us
    all_to_all x1, waiting for transfers between devices, sum_in_plane(): plane = lax.all_to_all(pair, ('y', 'x'), 0, 0, tiled=True)  17.1 us
    all_to_all x1, waiting for transfers between devices, per_device(): gathered = lax.all_to_all(fan, ('zh', 'zl', 'c'), 0, 0, tiled=True)  14 us
    pallas_call x1, Pallas kernels, block(): pl.pallas_call(block_kernel, out_shape=(half(feature), jax.ShapeDtypeStru...  13.2 us
    ppermute x1, starting transfers between devices, usual(): lax.ppermute(top, LAT, [((i + 1) % 16, i) for i in range(16)])  13.1 us
    all_to_all x1, starting transfers between devices, per_device(): lax.all_to_all(jnp.stack([plane[:16].astype(BF16), gain_part], axis=1), (...  10.2 us
    all_to_all x1, starting transfers between devices, per_device(): gathered = lax.all_to_all(fan, ('zh', 'zl', 'c'), 0, 0, tiled=True)  7.66 us
    ppermute x1, starting transfers between devices, per_device(): back_lon = lax.ppermute(back, LON, [(i, (i + 1) % 32) for i in range(32)])  6.8 us
  transfers between devices with their start and end apart: 13, of which 6 were waited for; matrix products, arithmetic and copies ran while one was open for 5% of the time, Pallas kernels for 2%

profile of v2, /device:TPU:1, one launch (start us, length us, event | category | flops | bytes accessed | tf_op | source)
XLA Modules:
  0.0 149.3 jit_solution(11989626985725678129)
XLA Ops:
  0.6 1.2 slice_maximum_fusion
  1.8 1.5 %pad_maximum_fusion.3 = (bf16[2,2,3,6,512]{4,1,3,2,0:T(2,128)(2,1)S(1)}, bf16[2,2,3,6,512]{4,1,3,2,0:T(2,128)(2,1)S(1)}, bf16[2,2,3,6,512]{4,1,3,2,0:T(2,128)(2,...) fusion(bf16[1,2,12,12,512]{4,1,3,2,0:T(2,128)(2,1)} %bitcast.53, ...), kind=kLoop, calls=%fused_computation.19 | loop fusion | flops 184320 | bytes 958464 | tf_op jit(solution)/shard_map/stack | solution.py:264
  3.3 0.1 copy.66
  3.4 0.1 copy.64
  3.5 0.1 copy.65
  3.6 5.5 %collective-permute-start.4 = (bf16[3,2,36,512]{3,2,1,0:T(8,128)(2,1)S(1)}, bf16[3,2,36,512]{3,2,1,0:T(8,128)(2,1)S(1)}, u32[]{:S(2)}, u32[]{:S(2)}) collective-permute-start(bf16[3,2,36,512]{3,2,1,0:T(8,128)(2,1)S(1)} %copy_dynamic-update-slice_fusion), channel_id=1, source_target_pairs={{0,48},{1,193},{2,210},{3,115},{4,52},{5,197},{6,214},{7,119},{8,5... | collective-permute-start | bytes 663560 | tf_op jit(solution)/shard_map/ppermute | solution.py:228
  9.1 0.1 copy.70
  9.2 1.6 %collective-permute-start.5 = (bf16[2,36,512]{2,1,0:T(8,128)(2,1)S(1)}, bf16[2,36,512]{2,1,0:T(8,128)(2,1)S(1)}, u32[]{:S(2)}, u32[]{:S(2)}) collective-permute-start(bf16[2,36,512]{2,1,0:T(8,128)(2,1)S(1)} %copy.71), channel_id=1, source_target_pairs={{1,48},{2,193},{3,210},{4,115},{5,52},{6,197},{7,214},{8,119},{9,5... | collective-permute-start | bytes 221192 | tf_op jit(solution)/shard_map/ppermute | solution.py:229
  10.8 0.1 copy.72
  10.8 1.4 collective-permute-done.5
  12.2 0.0 collective-permute-done.4
  12.3 0.7 collective-permute-start.7
  13.0 0.7 collective-permute-start.6
  13.7 0.1 copy.75
  13.8 0.1 copy.62
  13.8 0.1 copy.63
  13.9 0.1 pad_add_fusion.place
  14.0 16.6 %while.34 = (s32[]{:T(128)}, bf16[3,2,36,512]{3,2,1,0:T(8,128)(2,1)S(1)}, bf16[2,36,512]{2,1,0:T(8,128)(2,1)S(1)}, bf16[2,36,512]{2,1,0:T(8,128)(2,1)S(1)}, s32[]{:T(128)}, /*index=5*/s32[]{:T(128)}) while((s32[]{:T(128)}, bf16[3,2,36,512]{3,2,1,0:T(8,128)(2,1)S(1)}, bf16[2,36,512]{2,1,0:T(8,128)(2,1)S(1)}, bf16[2,36,512]{2,1,0:T(8,128)(2,1)S(1)}, ...), condition=%wide.region_1.0_spmd, body=%wide.region_0.0_spmd.sunk | while | flops 2 | bytes 2212029 | solution.py:208
  14.0 1.3 collective-permute-start
  15.3 1.3 collective-permute-start.1
  16.6 13.1 %collective-permute-start.2 = (bf16[2,36,512]{2,1,0:T(8,128)(2,1)S(1)}, bf16[2,36,512]{2,1,0:T(8,128)(2,1)S(1)}, u32[]{:S(2)}, u32[]{:S(2)}) collective-permute-start(bf16[2,36,512]{2,1,0:T(8,128)(2,1)S(1)} %get-tuple-element.299), channel_id=1, source_target_pairs={{1,0},{2,1},{3,2},{4,3},{5,4},{6,5},{7,6},{8,7},{9,8},{10,9},{11,1... | collective-permute-start | bytes 221192 | tf_op jit(solution)/shard_map/while/body/ppermute | solution.py:246
  29.7 0.0 collective-permute-done.1
  29.8 0.9 collective-permute-done.2
  30.6 0.0 collective-permute-done
  30.7 0.0 collective-permute-done.7
  30.7 0.0 collective-permute-done.6
  30.8 0.0 copy-start
  30.8 0.0 copy-start.1
  30.8 0.0 copy-start.2
  30.8 0.7 concatenate.18
  31.6 0.6 copy-done
  32.2 0.1 copy-done.1
  32.3 0.0 copy-done.2
  32.3 13.2 %window_block.1 = (bf16[288,512]{1,0:T(8,128)(2,1)S(1)}, bf16[144,512]{1,0:T(8,128)(2,1)}, bf16[288,512]{1,0:T(8,128)(2,1)S(1)}, bf16[288,1536]{1,0:T(8,128)(2,1...) custom-call(s32[2]{0:T(128)S(1)} %pad_add_fusion.place, bf16[288,512]{1,0:T(8,128)(2,1)S(1)} %get-tuple-element.187.x_ref, ...), custom_call_target="tpu_custom_call" | custom-call | flops 2000000000 | bytes 6000000 | tf_op jit(solution)/shard_map/window_block/pallas_call | solution.py:139
  45.5 6.8 %collective-permute-start.8 = (bf16[144,512]{1,0:T(8,128)(2,1)}, bf16[144,512]{1,0:T(8,128)(2,1)}, u32[]{:S(2)}, u32[]{:S(2)}) collective-permute-start(bf16[144,512]{1,0:T(8,128)(2,1)} %get-tuple-element.128), channel_id=1, source_target_pairs={{0,16},{16,32},{32,48},{48,64},{64,80},{80,96},{96,112},{112,128},... | collective-permute-start | bytes 442376 | tf_op jit(solution)/shard_map/ppermute | solution.py:279
  52.3 0.6 broadcast_in_dim.6
  53.0 46.5 %while.35 = (s32[]{:T(128)}, bf16[288,512]{1,0:T(8,128)(2,1)S(1)}, bf16[288,1536]{1,0:T(8,128)(2,1)}, bf16[288,512]{1,0:T(8,128)(2,1)S(1)}, bf16[288,512]{1,0:T(...) while((s32[]{:T(128)}, bf16[288,512]{1,0:T(8,128)(2,1)S(1)}, ...), condition=%wide.region_4.5_spmd, body=%wide.region_2.4_spmd.sunk | while | flops 40003305472 | bytes 112325040 | solution.py:208
  53.0 2.8 %weight_terms.1 = (bf16[16,17,16,128]{3,2,1,0:T(8,128)(2,1)S(1)}, bf16[16,17,16,128]{3,2,1,0:T(8,128)(2,1)S(1)}) custom-call(s32[2]{0:T(128)S(1)} %get-tuple-element.361.place, bf16[288,512]{1,0:T(8,128)(2,1)S(1)} %get-tuple-element.354.hidden_ref, bf16[288,1536]{1,0:T(8,128)(2,1)} %get-tuple-element.355.dqkv_ref, ...), custom_call_target="tpu_custom_call" | custom-call | flops 40000000000 | bytes 100000000 | tf_op jit(solution)/shard_map/while/body/weight_terms/pallas_call | solution.py:183
  55.8 3.9 %collective-permute-start.3 = (bf16[16,17,16,128]{3,2,1,0:T(8,128)(2,1)S(1)}, bf16[16,17,16,128]{3,2,1,0:T(8,128)(2,1)S(1)}, u32[]{:S(2)}, u32[]{:S(2)}) collective-permute-start(bf16[16,17,16,128]{3,2,1,0:T(8,128)(2,1)S(1)} %get-tuple-element.313), channel_id=1, source_target_pairs={{0,1},{1,0},{2,3},{3,2},{4,5},{5,4},{6,7},{7,6},{8,9},{9,8},{10,11... | collective-permute-start | bytes 3342344 | tf_op jit(solution)/shard_map/while/body/ppermute | solution.py:283
  59.7 2.4 %collective-permute-done.3 = bf16[16,17,16,128]{3,2,1,0:T(8,128)(2,1)S(1)} collective-permute-done((bf16[16,17,16,128]{3,2,1,0:T(8,128)(2,1)S(1)}, bf16[16,17,16,128]{3,2,1,0:T(8,128)(2,1)S(1)}, u32[]{:S(2)}, u32[]{:S(2)}) %collective-permute-start.3) | collective-permute-done | bytes 1114144 | tf_op jit(solution)/shard_map/while/body/ppermute | solution.py:283
  62.0 1.3 add_convert_fusion.2
  63.3 18.2 %all-to-all-start = ((bf16[16,17,16,128]{3,2,1,0:T(8,128)(2,1)}), bf16[16,17,16,128]{3,2,1,0:T(8,128)(2,1)S(1)}, u32[]{:S(2)}, u32[]{:S(2)}) async-start(bf16[16,17,16,128]{3,2,1,0:T(8,128)(2,1)} %add_convert_fusion.2), calls=%async_computation | async-start | bytes 2228224 | tf_op jit(solution)/shard_map/while/body/all_to_all | solution.py:285
  81.6 17.1 %all-to-all-done = bf16[16,17,16,128]{3,2,1,0:T(8,128)(2,1)S(1)} async-done(((bf16[16,17,16,128]{3,2,1,0:T(8,128)(2,1)}), bf16[16,17,16,128]{3,2,1,0:T(8,128)(2,1)S(1)}, u32[]{:S(2)}, u32[]{:S(2)}) %all-to-all-start) | async-done | bytes 1114144 | tf_op jit(solution)/shard_map/while/body/all_to_all | solution.py:285
  98.6 0.8 convert_reduce_fusion.3
  99.4 0.0 collective-permute-done.8
  99.4 0.7 slice_bitcast_fusion.5
  100.1 0.8 slice_bitcast_fusion.2
  101.0 0.7 pad_maximum_fusion.1
  101.6 10.2 %all-to-all-start.1 = ((bf16[16,2,16,128]{3,2,1,0:T(8,128)(2,1)}), bf16[16,2,16,128]{3,2,1,0:T(8,128)(2,1)S(1)}, u32[]{:S(2)}, u32[]{:S(2)}) async-start(bf16[16,2,16,128]{3,2,1,0:T(8,128)(2,1)} %pad_maximum_fusion.1), calls=%async_computation.1 | async-start | bytes 262144 | tf_op jit(solution)/shard_map/all_to_all | solution.py:298
  112.0 0.9 slice_bitcast_fusion.3
  113.0 5.5 %collective-permute-start.9 = (bf16[2,36,512]{2,1,0:T(8,128)(2,1)S(1)}, bf16[2,36,512]{2,1,0:T(8,128)(2,1)S(1)}, u32[]{:S(2)}, u32[]{:S(2)}) collective-permute-start(bf16[2,36,512]{2,1,0:T(8,128)(2,1)S(1)} %pad_maximum_fusion.2), channel_id=1, source_target_pairs={{0,1},{1,2},{2,3},{3,4},{4,5},{5,6},{6,7},{7,8},{8,9},{9,10},{10,1... | collective-permute-start | bytes 221192 | tf_op jit(solution)/shard_map/ppermute | solution.py:293
  118.5 5.3 %all-to-all-done.1 = bf16[16,2,16,128]{3,2,1,0:T(8,128)(2,1)S(1)} async-done(((bf16[16,2,16,128]{3,2,1,0:T(8,128)(2,1)}), bf16[16,2,16,128]{3,2,1,0:T(8,128)(2,1)S(1)}, u32[]{:S(2)}, u32[]{:S(2)}) %all-to-all-start.1) | async-done | bytes 131104 | tf_op jit(solution)/shard_map/all_to_all | solution.py:298
  123.9 0.7 broadcast_in_dim.7
  124.6 7.7 %all-to-all-start.2 = ((bf16[32,16,128]{2,1,0:T(8,128)(2,1)}), bf16[32,16,128]{2,1,0:T(8,128)(2,1)S(1)}, u32[]{:S(2)}, u32[]{:S(2)}) async-start(bf16[32,16,128]{2,1,0:T(8,128)(2,1)} %broadcast_in_dim.7), calls=%async_computation.2 | async-start | bytes 262144 | tf_op jit(solution)/shard_map/all_to_all | solution.py:306
  132.2 0.0 collective-permute-done.9
  132.3 0.1 maximum_maximum_fusion
  132.4 1.0 copy.80
  133.5 0.6 fusion.2
  134.0 14.0 %all-to-all-done.2 = bf16[32,16,128]{2,1,0:T(8,128)(2,1)S(1)} async-done(((bf16[32,16,128]{2,1,0:T(8,128)(2,1)}), bf16[32,16,128]{2,1,0:T(8,128)(2,1)S(1)}, u32[]{:S(2)}, u32[]{:S(2)}) %all-to-all-start.2) | async-done | bytes 131104 | tf_op jit(solution)/shard_map/all_to_all | solution.py:306
  148.1 0.6 slice.175
  148.7 0.6 slice.174
  (33 shorter events, 0.5 us)
Async XLA Ops:
  3.6 8.6 %collective-permute-start.4 = (bf16[3,2,36,512]{3,2,1,0:T(8,128)(2,1)S(1)}, bf16[3,2,36,512]{3,2,1,0:T(8,128)(2,1)S(1)}, u32[]{:S(2)}, u32[]{:S(2)}) collective-permute-start(bf16[3,2,36,512]{3,2,1,0:T(8,128)(2,1)S(1)} %copy_dynamic-update-slice_fusion), channel_id=1, source_target_pairs={{0,48},{1,193},{2,210},{3,115},{4,52},{5,197},{6,214},{7,119},{8,5... | collective-permute-start | bytes 663560 | tf_op jit(solution)/shard_map/ppermute | solution.py:228
  9.2 3.1 %collective-permute-start.5 = (bf16[2,36,512]{2,1,0:T(8,128)(2,1)S(1)}, bf16[2,36,512]{2,1,0:T(8,128)(2,1)S(1)}, u32[]{:S(2)}, u32[]{:S(2)}) collective-permute-start(bf16[2,36,512]{2,1,0:T(8,128)(2,1)S(1)} %copy.71), channel_id=1, source_target_pairs={{1,48},{2,193},{3,210},{4,115},{5,52},{6,197},{7,214},{8,119},{9,5... | collective-permute-start | bytes 221192 | tf_op jit(solution)/shard_map/ppermute | solution.py:229
  12.3 18.4 %collective-permute-start.7 = (bf16[2,2,36,512]{3,2,1,0:T(8,128)(2,1)S(1)}, bf16[2,2,36,512]{3,2,1,0:T(8,128)(2,1)S(1)}, u32[]{:S(2)}, u32[]{:S(2)}) collective-permute-start(bf16[2,2,36,512]{3,2,1,0:T(8,128)(2,1)S(1)} %pad_maximum_fusion), channel_id=1, source_target_pairs={{48,496},{193,497},{210,498},{115,499},{52,500},{197,501},{214,502... | collective-permute-start | bytes 442376 | tf_op jit(solution)/shard_map/ppermute | solution.py:234
  13.0 17.7 %collective-permute-start.6 = (bf16[2,2,36,512]{3,2,1,0:T(8,128)(2,1)S(1)}, bf16[2,2,36,512]{3,2,1,0:T(8,128)(2,1)S(1)}, u32[]{:S(2)}, u32[]{:S(2)}) collective-permute-start(bf16[2,2,36,512]{3,2,1,0:T(8,128)(2,1)S(1)} %slice.124), channel_id=1, source_target_pairs={{48,496},{193,497},{210,498},{115,499},{52,500},{197,501},{214,502... | collective-permute-start | bytes 442376 | tf_op jit(solution)/shard_map/ppermute | solution.py:234
  14.0 16.6 %collective-permute-start = (bf16[3,2,36,512]{3,2,1,0:T(8,128)(2,1)S(1)}, bf16[3,2,36,512]{3,2,1,0:T(8,128)(2,1)S(1)}, u32[]{:S(2)}, u32[]{:S(2)}) collective-permute-start(bf16[3,2,36,512]{3,2,1,0:T(8,128)(2,1)S(1)} %get-tuple-element.297), channel_id=1, source_target_pairs={{16,0},{32,16},{48,32},{64,48},{80,64},{96,80},{112,96},{128,112},... | collective-permute-start | bytes 663560 | tf_op jit(solution)/shard_map/while/body/ppermute | solution.py:241
  15.3 14.4 %collective-permute-start.1 = (bf16[2,36,512]{2,1,0:T(8,128)(2,1)S(1)}, bf16[2,36,512]{2,1,0:T(8,128)(2,1)S(1)}, u32[]{:S(2)}, u32[]{:S(2)}) collective-permute-start(bf16[2,36,512]{2,1,0:T(8,128)(2,1)S(1)} %get-tuple-element.298), channel_id=1, source_target_pairs={{17,0},{18,1},{19,2},{20,3},{21,4},{22,5},{23,6},{24,7},{25,8},{26... | collective-permute-start | bytes 221192 | tf_op jit(solution)/shard_map/while/body/ppermute | solution.py:242
  16.6 14.0 %collective-permute-start.2 = (bf16[2,36,512]{2,1,0:T(8,128)(2,1)S(1)}, bf16[2,36,512]{2,1,0:T(8,128)(2,1)S(1)}, u32[]{:S(2)}, u32[]{:S(2)}) collective-permute-start(bf16[2,36,512]{2,1,0:T(8,128)(2,1)S(1)} %get-tuple-element.299), channel_id=1, source_target_pairs={{1,0},{2,1},{3,2},{4,3},{5,4},{6,5},{7,6},{8,7},{9,8},{10,9},{11,1... | collective-permute-start | bytes 221192 | tf_op jit(solution)/shard_map/while/body/ppermute | solution.py:246
  30.8 1.4 copy-start
  30.8 1.5 %copy-start.1 = (bf16[512,512]{1,0:T(8,128)(2,1)S(1)}, bf16[512,512]{1,0:T(8,128)(2,1)}, u32[]{:S(2)}) copy-start(bf16[512,512]{1,0:T(8,128)(2,1)} %w_out_ref.1) | copy-start | bytes 1572868
  30.8 1.5 %copy-start.2 = (f32[512]{0:T(512)S(1)}, f32[512]{0:T(512)}, u32[]{:S(2)}) copy-start(f32[512]{0:T(512)} %param.11) | copy-start | bytes 6148
  45.5 53.9 %collective-permute-start.8 = (bf16[144,512]{1,0:T(8,128)(2,1)}, bf16[144,512]{1,0:T(8,128)(2,1)}, u32[]{:S(2)}, u32[]{:S(2)}) collective-permute-start(bf16[144,512]{1,0:T(8,128)(2,1)} %get-tuple-element.128), channel_id=1, source_target_pairs={{0,16},{16,32},{32,48},{48,64},{64,80},{80,96},{96,112},{112,128},... | collective-permute-start | bytes 442376 | tf_op jit(solution)/shard_map/ppermute | solution.py:279
  55.8 6.2 %collective-permute-start.3 = (bf16[16,17,16,128]{3,2,1,0:T(8,128)(2,1)S(1)}, bf16[16,17,16,128]{3,2,1,0:T(8,128)(2,1)S(1)}, u32[]{:S(2)}, u32[]{:S(2)}) collective-permute-start(bf16[16,17,16,128]{3,2,1,0:T(8,128)(2,1)S(1)} %get-tuple-element.313), channel_id=1, source_target_pairs={{0,1},{1,0},{2,3},{3,2},{4,5},{5,4},{6,7},{7,6},{8,9},{9,8},{10,11... | collective-permute-start | bytes 3342344 | tf_op jit(solution)/shard_map/while/body/ppermute | solution.py:283
  63.3 35.3 %all-to-all-start = ((bf16[16,17,16,128]{3,2,1,0:T(8,128)(2,1)}), bf16[16,17,16,128]{3,2,1,0:T(8,128)(2,1)S(1)}, u32[]{:S(2)}, u32[]{:S(2)}) async-start(bf16[16,17,16,128]{3,2,1,0:T(8,128)(2,1)} %add_convert_fusion.2), calls=%async_computation | async-start | bytes 2228224 | tf_op jit(solution)/shard_map/while/body/all_to_all | solution.py:285
  101.6 22.2 %all-to-all-start.1 = ((bf16[16,2,16,128]{3,2,1,0:T(8,128)(2,1)}), bf16[16,2,16,128]{3,2,1,0:T(8,128)(2,1)S(1)}, u32[]{:S(2)}, u32[]{:S(2)}) async-start(bf16[16,2,16,128]{3,2,1,0:T(8,128)(2,1)} %pad_maximum_fusion.1), calls=%async_computation.1 | async-start | bytes 262144 | tf_op jit(solution)/shard_map/all_to_all | solution.py:298
  113.0 19.2 %collective-permute-start.9 = (bf16[2,36,512]{2,1,0:T(8,128)(2,1)S(1)}, bf16[2,36,512]{2,1,0:T(8,128)(2,1)S(1)}, u32[]{:S(2)}, u32[]{:S(2)}) collective-permute-start(bf16[2,36,512]{2,1,0:T(8,128)(2,1)S(1)} %pad_maximum_fusion.2), channel_id=1, source_target_pairs={{0,1},{1,2},{2,3},{3,4},{4,5},{5,6},{6,7},{7,8},{8,9},{9,10},{10,1... | collective-permute-start | bytes 221192 | tf_op jit(solution)/shard_map/ppermute | solution.py:293
  124.6 23.5 %all-to-all-start.2 = ((bf16[32,16,128]{2,1,0:T(8,128)(2,1)}), bf16[32,16,128]{2,1,0:T(8,128)(2,1)S(1)}, u32[]{:S(2)}, u32[]{:S(2)}) async-start(bf16[32,16,128]{2,1,0:T(8,128)(2,1)} %broadcast_in_dim.7), calls=%async_computation.2 | async-start | bytes 262144 | tf_op jit(solution)/shard_map/all_to_all | solution.py:306

commit v3 on v2

v3 whole, which is shorter than its diff:
```python
import functools
import math

import jax
import jax.numpy as jnp
from jax import lax
from jax.experimental import pallas as pl
from jax.experimental.pallas import tpu as pltpu
from jax.sharding import Mesh, PartitionSpec as P

HEADS = 16
HEAD_DIM = 32
WLAT = 6
WLON = 12
WINDOW = 144
TOKENS = 288
HALF = 72
EXTRA = 80
ALL_TOKENS = TOKENS + EXTRA
BLOCK = 36
GROUP = 4
BF16 = jnp.bfloat16
F32 = jnp.float32
LON = ("zh", "y", "x")
LAT = ("zl", "c")
ALL = LON + LAT
MIDS = ((0, 3), (3, 0), (3, 1), (1, 3), (2, 0), (0, 2), (1, 0), (2, 3))


def nn(a, b):
    return lax.dot_general(a, b, (((1,), (0,)), ((), ())), preferred_element_type=F32)


def nt(a, b):
    return lax.dot_general(a, b, (((1,), (1,)), ((), ())), preferred_element_type=F32)


def tn(a, b):
    return lax.dot_general(a, b, (((0,), (0,)), ((), ())), preferred_element_type=F32)


def attention_group(start, size, masked, group, qkv, d_attn, attended, dqkv):
    feature = HEADS * HEAD_DIM
    width = GROUP * HEAD_DIM
    rows = pl.ds(start, size)
    at = group * width

    def columns(offset):
        return pl.ds(pl.multiple_of(at + offset, 128), width)

    queries = qkv[rows, columns(0)]
    keys = qkv[rows, columns(feature)]
    values = qkv[rows, columns(2 * feature)]
    grads = d_attn[rows, columns(0)]
    scale = 1.0 / math.sqrt(HEAD_DIM)
    lane_head = lax.broadcasted_iota(jnp.int32, (1, width), 1) // HEAD_DIM
    key_late = lax.broadcasted_iota(jnp.int32, (size, size), 0) >= HALF
    query_late = lax.broadcasted_iota(jnp.int32, (size, size), 1) >= HALF
    allowed = jnp.logical_or(key_late == query_late, jnp.logical_not(masked))

    own = [(lane_head == head).astype(BF16) for head in range(GROUP)]
    key_stack = jnp.concatenate([keys * mask for mask in own], axis=0)
    value_stack = jnp.concatenate([values * mask for mask in own], axis=0)
    scores_all = nt(key_stack, queries)
    dprob_all = nt(value_stack, grads)
    prob_parts, dscore_parts = [], []
    for head in range(GROUP):
        part = slice(head * size, (head + 1) * size)
        scores = jnp.where(allowed, scores_all[part] * (scale * math.log2(math.e)), -jnp.inf)
        weights = jnp.exp2(scores - jnp.max(scores, axis=0, keepdims=True))
        prob = weights * (1.0 / jnp.sum(weights, axis=0, keepdims=True))
        dprob = dprob_all[part]
        delta = jnp.sum(prob * dprob, axis=0, keepdims=True)
        dscore_parts.append((prob * (dprob - delta) * scale).astype(BF16))
        prob_parts.append(prob.astype(BF16))
    prob_all = jnp.concatenate(prob_parts, axis=0)
    dscore_all = jnp.concatenate(dscore_parts, axis=0)

    def own_columns(stack):
        picked = stack[0:size]
        for head in range(1, GROUP):
            picked = jnp.where(lane_head == head, stack[head * size : (head + 1) * size], picked)
        return picked.astype(BF16)

    attended[rows, columns(0)] = tn(prob_all, value_stack).astype(BF16)
    dqkv[rows, columns(0)] = tn(dscore_all, key_stack).astype(BF16)
    dqkv[rows, columns(feature)] = own_columns(nn(dscore_all, queries))
    dqkv[rows, columns(2 * feature)] = own_columns(nn(prob_all, grads))


def block_kernel(
    place, x_ref, dy_ref, gain_ref, w_qkv_ref, w_out_ref,
    drolled_ref, back_ref, hidden_ref, dqkv_ref, attended_ref, gain_tile_ref,
    normed_ref, inverse_ref, qkv_ref, d_attn_ref, gain_sum_ref,
):
    first = place[0]
    last = place[1]
    feature = HEADS * HEAD_DIM
    regular = pl.ds(0, TOKENS)
    extra = pl.ds(TOKENS, EXTRA)

    def project(rows):
        values = x_ref[rows, :].astype(F32)
        centred = values - jnp.mean(values, axis=-1, keepdims=True)
        inverse = lax.rsqrt(jnp.mean(centred * centred, axis=-1, keepdims=True) + 1e-05)
        normed = centred * inverse
        normed_ref[rows, :] = normed
        inverse_ref[rows, :] = jnp.broadcast_to(inverse, (inverse.shape[0], 128))
        hidden = (normed * gain_ref[...]).astype(BF16)
        hidden_ref[rows, :] = hidden
        qkv_ref[rows, :] = nn(hidden, w_qkv_ref[...]).astype(BF16)
        d_attn_ref[rows, :] = nt(dy_ref[rows, :], w_out_ref[...]).astype(BF16)

    def finish(rows):
        dhidden = nt(dqkv_ref[rows, :], w_qkv_ref[...])
        normed = normed_ref[rows, :]
        dnorm = dhidden * gain_ref[...]
        drolled = dy_ref[rows, :].astype(F32) + inverse_ref[rows, 0:1] * (
            dnorm
            - jnp.mean(dnorm, axis=-1, keepdims=True)
            - normed * jnp.mean(dnorm * normed, axis=-1, keepdims=True)
        )
        drolled_ref[rows, :] = drolled.astype(BF16)
        return drolled, jnp.sum(dhidden * normed, axis=0, keepdims=True)

    @pl.when(first == 1)
    def _():
        project(pl.ds(0, ALL_TOKENS))

    @pl.when(first == 0)
    def _():
        project(regular)
        hidden_ref[extra, :] = jnp.zeros((EXTRA, feature), BF16)
        attended_ref[extra, :] = jnp.zeros((EXTRA, feature), BF16)
        dqkv_ref[extra, :] = jnp.zeros((EXTRA, 3 * feature), BF16)
        drolled_ref[extra, :] = jnp.zeros((EXTRA, feature), BF16)

    groups = HEADS // GROUP

    @pl.loop(0, (TOKENS // WINDOW) * groups)
    def _(step):
        window = step // groups
        attention_group(
            pl.multiple_of(window * WINDOW, 16), WINDOW,
            jnp.logical_and(last == 1, window == 1), step % groups,
            qkv_ref, d_attn_ref, attended_ref, dqkv_ref,
        )

    def hand_back(drolled):
        back_ref[0:72, :] = drolled[72:144].astype(BF16)
        back_ref[72:144, :] = drolled[180:252].astype(BF16)

    @pl.when(first == 0)
    def _():
        drolled, gain_sum = finish(regular)
        gain_sum_ref[...] = gain_sum
        hand_back(drolled)
        back_ref[144:180, :] = jnp.zeros((BLOCK, feature), BF16)

    @pl.when(first == 1)
    def _():
        @pl.loop(0, groups)
        def _(group):
            attention_group(
                TOKENS, EXTRA, first == 1, group, qkv_ref, d_attn_ref, attended_ref, dqkv_ref
            )

        drolled, gain_sum = finish(pl.ds(0, ALL_TOKENS))
        gain_sum_ref[...] = gain_sum
        hand_back(drolled)
        back_ref[144:180, :] = drolled[324:360].astype(BF16)

    gain_local = gain_sum_ref[...]
    coarse = gain_local.astype(BF16)
    fine = (gain_local - coarse.astype(F32)).astype(BF16)
    rows = [part[:, 128 * j : 128 * (j + 1)] for part in (coarse, fine) for j in range(4)]
    gain_tile_ref[...] = jnp.concatenate(
        [row.astype(F32) for row in rows] + [jnp.zeros((8, 128), F32)], axis=0
    ).astype(BF16)


def block(place, tokens, grads, norm_gain, w_qkv, w_out):
    feature = HEADS * HEAD_DIM
    vmem = pl.BlockSpec(memory_space=pltpu.VMEM)

    def half(rows, width):
        return jax.ShapeDtypeStruct((rows, width), BF16)

    return pl.pallas_call(
        block_kernel,
        out_shape=(
            half(ALL_TOKENS, feature), half(5 * BLOCK, feature),
            half(ALL_TOKENS, feature), half(ALL_TOKENS, 3 * feature), half(ALL_TOKENS, feature),
            half(16, 128),
        ),
        in_specs=[pl.BlockSpec(memory_space=pltpu.SMEM)] + [vmem] * 5,
        out_specs=(vmem,) * 6,
        scratch_shapes=[
            pltpu.VMEM((ALL_TOKENS, feature), F32),
            pltpu.VMEM((ALL_TOKENS, 128), F32),
            pltpu.VMEM((ALL_TOKENS, 3 * feature), BF16),
            pltpu.VMEM((ALL_TOKENS, feature), BF16),
            pltpu.VMEM((1, feature), F32),
        ],
        compiler_params=pltpu.CompilerParams(vmem_limit_bytes=40 * 1024 * 1024),
        cost_estimate=pl.CostEstimate(
            flops=2_000_000_000, bytes_accessed=6_000_000, transcendentals=700_000
        ),
        name="window_block",
    )(place, tokens, grads, norm_gain, w_qkv, w_out)


def weights_kernel(
    place, hidden_ref, dqkv_ref, attended_ref, dy_ref, gain_tile_ref, keep_ref, send_ref, total_ref
):
    core = place[2]
    feature = HEADS * HEAD_DIM
    total_ref[:, 0 : 3 * feature] = tn(hidden_ref[...], dqkv_ref[...]).astype(BF16)
    total_ref[:, 3 * feature : 4 * feature] = tn(attended_ref[...], dy_ref[...]).astype(BF16)

    @pl.loop(0, 16)
    def _(chunk):
        for half, out in ((core, keep_ref), (1 - core, send_ref)):
            start = pl.multiple_of(half * 256 + chunk * 16, 16)
            rows = total_ref[pl.ds(start, 16), :]
            for j in range(16):
                out[chunk, j] = rows[:, 128 * j : 128 * (j + 1)]
            out[chunk, 16] = gain_tile_ref[...]


def weight_terms(place, hidden, dqkv, attended, grads, gain_tile):
    feature = HEADS * HEAD_DIM
    vmem = pl.BlockSpec(memory_space=pltpu.VMEM)
    chunks = jax.ShapeDtypeStruct((16, 17, 16, 128), BF16)
    return pl.pallas_call(
        weights_kernel,
        out_shape=(chunks, chunks),
        in_specs=[pl.BlockSpec(memory_space=pltpu.SMEM)] + [vmem] * 5,
        out_specs=(vmem, vmem),
        scratch_shapes=[pltpu.VMEM((feature, 4 * feature), BF16)],
        compiler_params=pltpu.CompilerParams(vmem_limit_bytes=40 * 1024 * 1024),
        cost_estimate=pl.CostEstimate(
            flops=40_000_000_000, bytes_accessed=100_000_000, transcendentals=0
        ),
        name="weight_terms",
    )(place, hidden, dqkv, attended, grads, gain_tile)


def small_call(body, name, out_shape, *operands, place=None):
    vmem = pl.BlockSpec(memory_space=pltpu.VMEM)
    many = isinstance(out_shape, tuple)
    head = () if place is None else (place,)
    return pl.pallas_call(
        body,
        out_shape=out_shape,
        in_specs=[pl.BlockSpec(memory_space=pltpu.SMEM)] * len(head) + [vmem] * len(operands),
        out_specs=(vmem,) * len(out_shape) if many else vmem,
        compiler_params=pltpu.CompilerParams(vmem_limit_bytes=16 * 1024 * 1024),
        name=name,
    )(*head, *operands)


def pair_kernel(keep_ref, other_ref, out_ref):
    @pl.loop(0, 16)
    def _(chunk):
        for j in range(17):
            total = keep_ref[chunk, j].astype(F32) + other_ref[chunk, j].astype(F32)
            out_ref[chunk, j] = total.astype(BF16)


def plane_kernel(parts_ref, out_ref):
    gain = parts_ref[0, 16].astype(F32)
    for chunk in range(1, 16):
        gain = gain + parts_ref[chunk, 16].astype(F32)

    @pl.loop(0, 16)
    def _(j):
        total = parts_ref[0, j].astype(F32)
        for chunk in range(1, 16):
            total = total + parts_ref[chunk, j].astype(F32)
        out_ref[j, 0] = total.astype(BF16)
        out_ref[j, 1] = gain.astype(BF16)


def column_kernel(parts_ref, fan_ref, gain_ref):
    total = parts_ref[0, 0].astype(F32)
    gain = parts_ref[0, 1].astype(F32)
    for z in range(1, 16):
        total = total + parts_ref[z, 0].astype(F32)
        gain = gain + parts_ref[z, 1].astype(F32)
    total = total.astype(BF16)
    for peer in range(32):
        fan_ref[peer] = total
    gain_ref[...] = gain[0:4] + gain[4:8]


def spread_kernel(place, tiles_ref, qkv_ref, out_ref):
    half = place[3]
    for z in range(16):
        tile = tiles_ref[z, half].astype(F32)
        if z < 12:
            qkv_ref[:, 128 * z : 128 * (z + 1)] = tile
        else:
            out_ref[:, 128 * (z - 12) : 128 * (z - 11)] = tile


def index(zh, y, x, zl, c):
    return (((zh * 4 + y) * 4 + x) * 8 + zl) * 2 + c


def in_one_piece(work, start):
    once = jnp.minimum(lax.axis_index(LAT) + 1, 1)

    def body(turn, values):
        values, _ = lax.optimization_barrier((values, turn))
        return work(*values)

    return lax.fori_loop(0, once, body, start)


def middle_of(zh, lat):
    zl, c = lat // 2, lat % 2
    y, x = MIDS[zl]
    z = (zh * 8 + zl + 1 - 2 * c) % 16
    return index(z // 8, y, x, z % 8, c)


def fetch(blocks, corner, top, first_block):
    out, out_corner, onward = [], [], []
    for zh in range(2):
        for lat in range(16):
            middle, target = middle_of(zh, lat), index(1 - zh, 3, 3, lat // 2, lat % 2)
            out.append((index(zh, 0, 0, lat // 2, lat % 2), middle))
            onward.append((middle, target))
            if lat < 15:
                out_corner.append((index(zh, 0, 0, (lat + 1) // 2, (lat + 1) % 2), middle))
    halfway = lax.ppermute(blocks, ALL, out)
    halfway_corner = lax.ppermute(corner, ALL, out_corner)
    halfway, halfway_corner, blocks, corner, top, first_block = lax.optimization_barrier(
        (halfway, halfway_corner, blocks, corner, top, first_block)
    )
    crossed = lax.ppermute(jnp.concatenate([halfway, halfway_corner[None]]), ALL, onward)
    inner = [i for i in range(32) if i % 16 < 15]

    def usual(blocks, corner, top, first_block):
        return (
            lax.ppermute(blocks, LON, [(i + 1, i) for i in inner]),
            lax.ppermute(
                corner, ALL, [((i + 1) * 16 + j + 1, i * 16 + j) for i in inner for j in range(15)]
            ),
            lax.ppermute(top, LAT, [(j + 1, j) for j in range(15)]),
            lax.ppermute(first_block, ALL, [((i + 1) % 32 * 16, i * 16) for i in range(32)]),
        )

    usual_blocks = in_one_piece(usual, (blocks, corner, top, first_block))
    crossed, normal, normal_corner, lat_block, extra = lax.optimization_barrier(
        (crossed, *usual_blocks)
    )
    east = lax.axis_index(LON) % 16 == 15
    arrived = [jnp.where(east, crossed[k], normal[k]) for k in range(3)]
    return arrived + [jnp.where(east, crossed[3], normal_corner)], lat_block, extra


def per_device(block_input, cotangent, norm_gain, w_qkv, w_out):
    half_lat, half_lon = WLAT // 2, WLON // 2
    levels, lat_rows, lon_cols, feature = block_input.shape
    stacked = jnp.stack([block_input, cotangent])

    def part(row, col):
        return stacked[:, :, row : row + half_lat, col : col + half_lon].reshape(2, BLOCK, feature)

    west = jnp.stack([part(row, 0) for row in (3, 6, 9)])
    (p0, p1, p2, corner), lat_block, extra = fetch(
        west, part(0, 0), part(0, half_lon), part(0, 0)
    )
    own = [part(row, half_lon) for row in (3, 6, 9, 0)]
    none = jnp.zeros((2, EXTRA - HALF, feature), BF16)
    tokens = jnp.concatenate(
        [own[0], own[1], p0, p1, own[2], p2, corner, lat_block, own[3], extra, none], axis=1
    )
    lat = lax.axis_index(LAT)
    first = lat == 0
    place = jnp.stack([first, lat == 15, lax.axis_index("c"), lax.axis_index("zh")])
    place = place.astype(jnp.int32)
    drolled, back, hidden, dqkv, attended, gain_tile = block(
        place, tokens[0], tokens[1], norm_gain.reshape(1, feature), w_qkv, w_out
    )

    back_lon = lax.ppermute(back, LON, [(i, (i + 1) % 32) for i in range(32)])

    def sum_in_plane(hidden, dqkv, attended, grads, gain_tile, _):
        keep, send = weight_terms(place, hidden, dqkv, attended, grads, gain_tile)
        other = lax.ppermute(send, "c", [(0, 1), (1, 0)])
        pair = small_call(
            pair_kernel, "pair_sum", jax.ShapeDtypeStruct(keep.shape, BF16), keep, other
        )
        plane = lax.all_to_all(pair, ("y", "x"), 0, 0, tiled=True)
        plane = small_call(
            plane_kernel, "plane_sum", jax.ShapeDtypeStruct((16, 2, 16, 128), BF16), plane
        )
        return hidden, dqkv, attended, grads, gain_tile, plane

    nothing = jnp.zeros((16, 2, 16, 128), BF16)
    *_, plane = in_one_piece(
        sum_in_plane, (hidden, dqkv, attended, tokens[1], gain_tile, nothing)
    )
    plane, back_lon = lax.optimization_barrier((plane, back_lon))
    back_lat = lax.ppermute(
        jnp.stack([drolled[252:288], back_lon[108:144]]), LAT, [(j, j + 1) for j in range(15)]
    )
    column = lax.all_to_all(plane, ("zh", "zl"), 0, 0, tiled=True)
    fan, gain_rows = small_call(
        column_kernel, "column_sum",
        (jax.ShapeDtypeStruct((32, 16, 128), BF16), jax.ShapeDtypeStruct((4, 128), F32)),
        column,
    )
    gain_grad = gain_rows.reshape(feature)
    gathered = lax.all_to_all(fan, ("zh", "zl", "c"), 0, 0, tiled=True)
    qkv_grad, out_grad = small_call(
        spread_kernel, "spread",
        (
            jax.ShapeDtypeStruct((16, 3 * feature), F32),
            jax.ShapeDtypeStruct((16, feature), F32),
        ),
        gathered.reshape(16, 2, 16, 128), place=place,
    )

    def grid(piece):
        return piece.reshape(levels, half_lat, half_lon, feature)

    rows = [
        (jnp.where(first, back_lon[144:180], back_lat[1]), jnp.where(first, drolled[288:324], back_lat[0])),
        (back_lon[0:36], drolled[0:36]),
        (back_lon[36:72], drolled[36:72]),
        (back_lon[72:108], drolled[144:180]),
    ]
    input_grad = jnp.concatenate(
        [jnp.concatenate([grid(west), grid(east)], axis=2) for west, east in rows], axis=1
    )
    return input_grad, qkv_grad, out_grad, gain_grad


def solution(mesh):
    fine = Mesh(mesh.devices.reshape(2, 4, 4, 8, 2), ALL)
    grid_spec = P(None, LAT, LON, None)
    return jax.shard_map(
        per_device,
        mesh=fine,
        in_specs=(grid_spec, grid_spec, P(), P(), P()),
        out_specs=(grid_spec, P(LON, None), P(LON, None), P()),
        check_vma=False,
    )
```

time: 150 us -> 141 us (0.940)
  starting transfers between devices: 76.4 us -> 65.5 us
  waiting for transfers between devices: 41 us -> 46.2 us
  local copies, waits for them, and re-layouts: 8.33 us -> 5.35 us
  other arithmetic: 6.37 us -> 3.91 us
  Pallas kernels: 16 us -> 17.8 us
    ppermute x5, starting transfers between devices: 21.3 us -> 8.1 us  [the longest x1 3.54 us: per_device(): lax.ppermute(jnp.stack([drolled[252:288], back_lon[108:144]]), LAT, [(j,...]
    ppermute x1, starting transfers between devices: 5.48 us -> 14.2 us  [fetch(): halfway = lax.ppermute(blocks, ALL, out)]
    all_to_all x1, waiting for transfers between devices: 14 us -> 6.22 us  [per_device(): gathered = lax.all_to_all(fan, ('zh', 'zl', 'c'), 0, 0, tiled=True)]
    ppermute x5, waiting for transfers between devices: 0.89 us -> 7.71 us  [the longest x1 3.97 us: usual(): lax.ppermute(corner, ALL, [((i + 1) * 16 + j + 1, i * 16 + j) for i in in...]
    all_to_all x1, waiting for transfers between devices: 5.32 us -> 11.2 us  [per_device(): column = lax.all_to_all(plane, ('zh', 'zl'), 0, 0, tiled=True)]
    all_to_all x1, starting transfers between devices: 18.2 us -> 13 us  [sum_in_plane(): plane = lax.all_to_all(pair, ('y', 'x'), 0, 0, tiled=True)]
    ppermute x1, starting transfers between devices: 6.8 us -> 4.41 us  [per_device(): back_lon = lax.ppermute(back, LON, [(i, (i + 1) % 32) for i in range(32)])]
    pallas_call x1 -> x5, Pallas kernels: 13.2 us -> 14.9 us  [the longest x1 10.7 us: block(): pl.pallas_call(block_kernel, out_shape=(half(ALL_TOKENS, feature), half(5...]
  transfers between devices with their start and end apart: 13 -> 13, of which waited for: 6 -> 8; matrix products, arithmetic and copies ran while one was open for 5% -> 3% of each run, Pallas kernels for 2% -> 4%
where the time goes in v3:
time: 141 us; the launch traced here: 140 us
  starting transfers between devices  65.5 us (46%)
  waiting for transfers between devices  46.2 us (33%)
  Pallas kernels  17.8 us (13%)
  local copies, waits for them, and re-layouts  5.35 us (4%)
  other arithmetic  3.91 us (3%)
    all_to_all x1, waiting for transfers between devices, sum_in_plane(): plane = lax.all_to_all(pair, ('y', 'x'), 0, 0, tiled=True)  17.1 us
    ppermute x1, starting transfers between devices, fetch(): halfway = lax.ppermute(blocks, ALL, out)  14.2 us
    all_to_all x1, starting transfers between devices, sum_in_plane(): plane = lax.all_to_all(pair, ('y', 'x'), 0, 0, tiled=True)  13 us
    all_to_all x1, waiting for transfers between devices, per_device(): column = lax.all_to_all(plane, ('zh', 'zl'), 0, 0, tiled=True)  11.2 us
    pallas_call x1, Pallas kernels, block(): pl.pallas_call(block_kernel, out_shape=(half(ALL_TOKENS, feature), half(5...  10.7 us
    all_to_all x1, starting transfers between devices, per_device(): column = lax.all_to_all(plane, ('zh', 'zl'), 0, 0, tiled=True)  10 us
    all_to_all x1, starting transfers between devices, per_device(): gathered = lax.all_to_all(fan, ('zh', 'zl', 'c'), 0, 0, tiled=True)  7.71 us
    all_to_all x1, waiting for transfers between devices, per_device(): gathered = lax.all_to_all(fan, ('zh', 'zl', 'c'), 0, 0, tiled=True)  6.22 us
  transfers between devices with their start and end apart: 13, of which 8 were waited for; matrix products, arithmetic and copies ran while one was open for 3% of the time, Pallas kernels for 4%

profile of v3, /device:TPU:1, one launch (start us, length us, event | category | flops | bytes accessed | tf_op | source)
XLA Modules:
  0.0 139.9 jit_solution(9944777116800909794)
XLA Ops:
  0.6 1.2 slice_maximum_fusion
  1.8 1.5 %pad_maximum_fusion.2 = (bf16[2,2,3,6,512]{4,1,3,2,0:T(2,128)(2,1)S(1)}, bf16[2,2,3,6,512]{4,1,3,2,0:T(2,128)(2,1)S(1)}, bf16[2,2,3,6,512]{4,1,3,2,0:T(2,128)(2,...) fusion(bf16[1,2,12,12,512]{4,1,3,2,0:T(2,128)(2,1)} %bitcast.45, ...), kind=kLoop, calls=%fused_computation.12 | loop fusion | flops 184320 | bytes 958464 | tf_op jit(solution)/shard_map/stack | solution.py:367
  3.3 0.1 copy.29
  3.4 0.1 copy.27
  3.5 0.1 copy.28
  3.6 14.2 %collective-permute-start.5 = (bf16[3,2,36,512]{3,2,1,0:T(8,128)(2,1)S(1)}, bf16[3,2,36,512]{3,2,1,0:T(8,128)(2,1)S(1)}, u32[]{:S(2)}, u32[]{:S(2)}) collective-permute-start(bf16[3,2,36,512]{3,2,1,0:T(8,128)(2,1)S(1)} %copy_dynamic-update-slice_fusion), channel_id=1, source_target_pairs={{0,50},{1,319},{2,196},{3,193},{4,214},{5,211},{6,120},{7,117},{8,... | collective-permute-start | bytes 663560 | tf_op jit(solution)/shard_map/ppermute | solution.py:337
  17.8 0.1 copy.33
  17.8 1.3 collective-permute-start.6
  19.1 0.1 copy.35
  19.2 1.4 collective-permute-done.6
  20.6 0.3 collective-permute-done.5
  20.9 0.7 collective-permute-start.7
  21.6 0.1 copy.39
  21.7 0.1 copy.25
  21.8 0.1 copy.26
  21.9 0.1 pad_add_fusion.place
  22.0 9.3 %while.36 = (s32[]{:T(128)}, bf16[3,2,36,512]{3,2,1,0:T(8,128)(2,1)S(1)}, bf16[2,36,512]{2,1,0:T(8,128)(2,1)S(1)}, bf16[2,36,512]{2,1,0:T(8,128)(2,1)S(1)}, bf16...) while((s32[]{:T(128)}, bf16[3,2,36,512]{3,2,1,0:T(8,128)(2,1)S(1)}, bf16[2,36,512]{2,1,0:T(8,128)(2,1)S(1)}, ...), condition=%wide.region_1.0_spmd, body=%wide.region_0.0_spmd.sunk | while | flops 2 | bytes 2654445 | solution.py:318
  22.1 1.3 collective-permute-start
  23.4 1.3 collective-permute-start.1
  24.7 1.9 %collective-permute-start.2 = (bf16[2,36,512]{2,1,0:T(8,128)(2,1)S(1)}, bf16[2,36,512]{2,1,0:T(8,128)(2,1)S(1)}, u32[]{:S(2)}, u32[]{:S(2)}) collective-permute-start(bf16[2,36,512]{2,1,0:T(8,128)(2,1)S(1)} %get-tuple-element.311), channel_id=1, source_target_pairs={{1,0},{2,1},{3,2},{4,3},{5,4},{6,5},{7,6},{8,7},{9,8},{10,9},{11,1... | collective-permute-start | bytes 221192 | tf_op jit(solution)/shard_map/while/body/ppermute | solution.py:351
  26.6 0.7 collective-permute-start.3
  27.3 4.0 %collective-permute-done.1 = bf16[2,36,512]{2,1,0:T(8,128)(2,1)S(1)} collective-permute-done((bf16[2,36,512]{2,1,0:T(8,128)(2,1)S(1)}, bf16[2,36,512]{2,1,0:T(8,128)(2,1)S(1)}, u32[]{:S(2)}, u32[]{:S(2)}) %collective-permute-start.1) | collective-permute-done | bytes 73760 | tf_op jit(solution)/shard_map/while/body/ppermute | solution.py:348
  31.2 0.0 collective-permute-done.2
  31.3 0.0 collective-permute-done.3
  31.3 0.0 collective-permute-done
  31.3 0.0 collective-permute-done.7
  31.4 0.0 copy-start
  31.4 0.9 concatenate.22
  32.3 0.0 copy-start.1
  32.3 0.0 copy-start.2
  32.3 0.1 slice_bitcast_fusion
  32.4 0.4 copy-done
  32.8 0.7 copy-done.1
  33.5 0.0 copy-done.2
  33.5 10.7 %window_block.1 = (bf16[368,512]{1,0:T(8,128)(2,1)S(1)}, bf16[180,512]{1,0:T(8,128)(2,1)}, bf16[368,512]{1,0:T(8,128)(2,1)S(1)}, bf16[368,1536]{1,0:T(8,128)(2,1...) custom-call(s32[4]{0:T(128)S(1)} %pad_add_fusion.place, bf16[368,512]{1,0:T(8,128)(2,1)S(1)} %get-tuple-element.190.x_ref, ...), custom_call_target="tpu_custom_call" | custom-call | flops 2000000000 | bytes 6000000 | tf_op jit(solution)/shard_map/window_block/pallas_call | solution.py:189
  44.2 4.4 %collective-permute-start.8 = (bf16[180,512]{1,0:T(8,128)(2,1)}, bf16[180,512]{1,0:T(8,128)(2,1)}, u32[]{:S(2)}, u32[]{:S(2)}) collective-permute-start(bf16[180,512]{1,0:T(8,128)(2,1)} %get-tuple-element.141), channel_id=1, source_target_pairs={{0,16},{16,32},{32,48},{48,64},{64,80},{80,96},{96,112},{112,128},... | collective-permute-start | bytes 552968 | tf_op jit(solution)/shard_map/ppermute | solution.py:389
  48.6 0.7 broadcast_in_dim.11
  49.3 43.2 %while.37 = (s32[]{:T(128)}, bf16[368,512]{1,0:T(8,128)(2,1)S(1)}, bf16[368,1536]{1,0:T(8,128)(2,1)}, bf16[368,512]{1,0:T(8,128)(2,1)S(1)}, bf16[368,512]{1,0:T(...) while((s32[]{:T(128)}, bf16[368,512]{1,0:T(8,128)(2,1)S(1)}, ...), condition=%wide.region_3.4_spmd, body=%wide.region_2.3_spmd.sunk | while | flops 40000000000 | bytes 107798960 | solution.py:318
  49.3 2.9 %weight_terms.1 = (bf16[16,17,16,128]{3,2,1,0:T(8,128)(2,1)S(1)}, bf16[16,17,16,128]{3,2,1,0:T(8,128)(2,1)S(1)}) custom-call(s32[4]{0:T(128)S(1)} %get-tuple-element.377.place, bf16[368,512]{1,0:T(8,128)(2,1)S(1)} %get-tuple-element.370.hidden_ref, bf16[368,1536]{1,0:T(8,128)(2,1)} %get-tuple-element.371.dqkv_ref, ...), custom_call_target="tpu_custom_call" | custom-call | flops 40000000000 | bytes 100000000 | tf_op jit(solution)/shard_map/while/body/weight_terms/pallas_call | solution.py:235
  52.2 5.5 %collective-permute-start.4 = (bf16[16,17,16,128]{3,2,1,0:T(8,128)(2,1)S(1)}, bf16[16,17,16,128]{3,2,1,0:T(8,128)(2,1)S(1)}, u32[]{:S(2)}, u32[]{:S(2)}) collective-permute-start(bf16[16,17,16,128]{3,2,1,0:T(8,128)(2,1)S(1)} %get-tuple-element.327), channel_id=1, source_target_pairs={{0,1},{1,0},{2,3},{3,2},{4,5},{5,4},{6,7},{7,6},{8,9},{9,8},{10,11... | collective-permute-start | bytes 3342344 | tf_op jit(solution)/shard_map/while/body/ppermute | solution.py:393
  57.8 2.4 %collective-permute-done.4.other_ref = bf16[16,17,16,128]{3,2,1,0:T(8,128)(2,1)S(1)} collective-permute-done((bf16[16,17,16,128]{3,2,1,0:T(8,128)(2,1)S(1)}, bf16[16,17,16,128]{3,2,1,0:T(8,128)(2,1)S(1)}, u32[]{:S(2)}, u32[]{:S(2)}) %collective-permute-start.4) | collective-permute-done | bytes 1114144 | tf_op jit(solution)/shard_map/while/body/ppermute | solution.py:393
  60.1 1.3 pair_sum.1
  61.4 13.0 %all-to-all-start = ((bf16[16,17,16,128]{3,2,1,0:T(8,128)(2,1)}), bf16[16,17,16,128]{3,2,1,0:T(8,128)(2,1)S(1)}, u32[]{:S(2)}, u32[]{:S(2)}) async-start(bf16[16,17,16,128]{3,2,1,0:T(8,128)(2,1)} %pair_sum.1), calls=%async_computation | async-start | bytes 2228224 | tf_op jit(solution)/shard_map/while/body/all_to_all | solution.py:397
  74.4 17.1 %all-to-all-done.parts_ref = bf16[16,17,16,128]{3,2,1,0:T(8,128)(2,1)S(1)} async-done(((bf16[16,17,16,128]{3,2,1,0:T(8,128)(2,1)}), bf16[16,17,16,128]{3,2,1,0:T(8,128)(2,1)S(1)}, u32[]{:S(2)}, u32[]{:S(2)}) %all-to-all-start) | async-done | bytes 1114144 | tf_op jit(solution)/shard_map/while/body/all_to_all | solution.py:397
  91.5 1.0 plane_sum.1
  92.5 0.0 collective-permute-done.8
  92.5 10.0 %all-to-all-start.1 = ((bf16[16,2,16,128]{3,2,1,0:T(8,128)(2,1)}), bf16[16,2,16,128]{3,2,1,0:T(8,128)(2,1)S(1)}, u32[]{:S(2)}, u32[]{:S(2)}) async-start(bf16[16,2,16,128]{3,2,1,0:T(8,128)(2,1)} %get-tuple-element.144), calls=%async_computation.1 | async-start | bytes 262144 | tf_op jit(solution)/shard_map/all_to_all | solution.py:411
  102.5 0.8 slice_bitcast_fusion.4
  103.3 11.2 %all-to-all-done.1.parts_ref = bf16[16,2,16,128]{3,2,1,0:T(8,128)(2,1)S(1)} async-done(((bf16[16,2,16,128]{3,2,1,0:T(8,128)(2,1)}), bf16[16,2,16,128]{3,2,1,0:T(8,128)(2,1)S(1)}, u32[]{:S(2)}, u32[]{:S(2)}) %all-to-all-start.1) | async-done | bytes 131104 | tf_op jit(solution)/shard_map/all_to_all | solution.py:411
  114.5 0.7 column_sum.1
  115.2 7.7 %all-to-all-start.2 = ((bf16[32,16,128]{2,1,0:T(8,128)(2,1)}), bf16[32,16,128]{2,1,0:T(8,128)(2,1)S(1)}, u32[]{:S(2)}, u32[]{:S(2)}) async-start(bf16[32,16,128]{2,1,0:T(8,128)(2,1)} %get-tuple-element.145), calls=%async_computation.2 | async-start | bytes 262144 | tf_op jit(solution)/shard_map/all_to_all | solution.py:418
  122.9 3.5 %collective-permute-start.9 = (bf16[2,36,512]{2,1,0:T(8,128)(2,1)S(1)}, bf16[2,36,512]{2,1,0:T(8,128)(2,1)S(1)}, u32[]{:S(2)}, u32[]{:S(2)}) collective-permute-start(bf16[2,36,512]{2,1,0:T(8,128)(2,1)S(1)} %pad_maximum_fusion.1), channel_id=1, source_target_pairs={{0,1},{1,2},{2,3},{3,4},{4,5},{5,6},{6,7},{7,8},{8,9},{9,10},{10,1... | collective-permute-start | bytes 221192 | tf_op jit(solution)/shard_map/ppermute | solution.py:408
  126.5 3.7 %collective-permute-done.9 = bf16[2,36,512]{2,1,0:T(8,128)(2,1)S(1)} collective-permute-done((bf16[2,36,512]{2,1,0:T(8,128)(2,1)S(1)}, bf16[2,36,512]{2,1,0:T(8,128)(2,1)S(1)}, u32[]{:S(2)}, u32[]{:S(2)}) %collective-permute-start.9) | collective-permute-done | bytes 73760 | tf_op jit(solution)/shard_map/ppermute | solution.py:408
  130.2 0.9 fusion.1
  131.3 0.1 maximum_maximum_fusion
  131.5 1.0 copy.44
  132.5 6.2 %all-to-all-done.2 = bf16[32,16,128]{2,1,0:T(8,128)(2,1)S(1)} async-done(((bf16[32,16,128]{2,1,0:T(8,128)(2,1)}), bf16[32,16,128]{2,1,0:T(8,128)(2,1)S(1)}, u32[]{:S(2)}, u32[]{:S(2)}) %all-to-all-start.2) | async-done | bytes 131104 | tf_op jit(solution)/shard_map/all_to_all | solution.py:418
  138.7 1.2 spread.1
  (29 shorter events, 0.4 us)
Async XLA Ops:
  3.6 17.3 %collective-permute-start.5 = (bf16[3,2,36,512]{3,2,1,0:T(8,128)(2,1)S(1)}, bf16[3,2,36,512]{3,2,1,0:T(8,128)(2,1)S(1)}, u32[]{:S(2)}, u32[]{:S(2)}) collective-permute-start(bf16[3,2,36,512]{3,2,1,0:T(8,128)(2,1)S(1)} %copy_dynamic-update-slice_fusion), channel_id=1, source_target_pairs={{0,50},{1,319},{2,196},{3,193},{4,214},{5,211},{6,120},{7,117},{8,... | collective-permute-start | bytes 663560 | tf_op jit(solution)/shard_map/ppermute | solution.py:337
  17.8 2.8 %collective-permute-start.6 = (bf16[2,36,512]{2,1,0:T(8,128)(2,1)S(1)}, bf16[2,36,512]{2,1,0:T(8,128)(2,1)S(1)}, u32[]{:S(2)}, u32[]{:S(2)}) collective-permute-start(bf16[2,36,512]{2,1,0:T(8,128)(2,1)S(1)} %copy.34), channel_id=1, source_target_pairs={{1,50},{2,319},{3,196},{4,193},{5,214},{6,211},{7,120},{8,117},{9,... | collective-permute-start | bytes 221192 | tf_op jit(solution)/shard_map/ppermute | solution.py:338
  20.9 10.4 %collective-permute-start.7 = (bf16[4,2,36,512]{3,2,1,0:T(8,128)(2,1)S(1)}, bf16[4,2,36,512]{3,2,1,0:T(8,128)(2,1)S(1)}, u32[]{:S(2)}, u32[]{:S(2)}) collective-permute-start(bf16[4,2,36,512]{3,2,1,0:T(8,128)(2,1)S(1)} %pad_maximum_fusion), channel_id=1, source_target_pairs={{50,496},{319,497},{196,498},{193,499},{214,500},{211,501},{120,50... | collective-permute-start | bytes 884744 | tf_op jit(solution)/shard_map/ppermute | solution.py:342
  22.1 9.2 %collective-permute-start = (bf16[3,2,36,512]{3,2,1,0:T(8,128)(2,1)S(1)}, bf16[3,2,36,512]{3,2,1,0:T(8,128)(2,1)S(1)}, u32[]{:S(2)}, u32[]{:S(2)}) collective-permute-start(bf16[3,2,36,512]{3,2,1,0:T(8,128)(2,1)S(1)} %get-tuple-element.309), channel_id=1, source_target_pairs={{16,0},{32,16},{48,32},{64,48},{80,64},{96,80},{112,96},{128,112},... | collective-permute-start | bytes 663560 | tf_op jit(solution)/shard_map/while/body/ppermute | solution.py:347
  23.4 7.9 %collective-permute-start.1 = (bf16[2,36,512]{2,1,0:T(8,128)(2,1)S(1)}, bf16[2,36,512]{2,1,0:T(8,128)(2,1)S(1)}, u32[]{:S(2)}, u32[]{:S(2)}) collective-permute-start(bf16[2,36,512]{2,1,0:T(8,128)(2,1)S(1)} %get-tuple-element.310), channel_id=1, source_target_pairs={{17,0},{18,1},{19,2},{20,3},{21,4},{22,5},{23,6},{24,7},{25,8},{26... | collective-permute-start | bytes 221192 | tf_op jit(solution)/shard_map/while/body/ppermute | solution.py:348
  24.7 6.6 %collective-permute-start.2 = (bf16[2,36,512]{2,1,0:T(8,128)(2,1)S(1)}, bf16[2,36,512]{2,1,0:T(8,128)(2,1)S(1)}, u32[]{:S(2)}, u32[]{:S(2)}) collective-permute-start(bf16[2,36,512]{2,1,0:T(8,128)(2,1)S(1)} %get-tuple-element.311), channel_id=1, source_target_pairs={{1,0},{2,1},{3,2},{4,3},{5,4},{6,5},{7,6},{8,7},{9,8},{10,9},{11,1... | collective-permute-start | bytes 221192 | tf_op jit(solution)/shard_map/while/body/ppermute | solution.py:351
  26.6 4.7 %collective-permute-start.3 = (bf16[2,36,512]{2,1,0:T(8,128)(2,1)S(1)}, bf16[2,36,512]{2,1,0:T(8,128)(2,1)S(1)}, u32[]{:S(2)}, u32[]{:S(2)}) collective-permute-start(bf16[2,36,512]{2,1,0:T(8,128)(2,1)S(1)} %get-tuple-element.312), channel_id=1, source_target_pairs={{16,0},{32,16},{48,32},{64,48},{80,64},{96,80},{112,96},{128,112},... | collective-permute-start | bytes 221192 | tf_op jit(solution)/shard_map/while/body/ppermute | solution.py:352
  31.4 1.4 %copy-start = (bf16[512,1536]{1,0:T(8,128)(2,1)S(1)}, bf16[512,1536]{1,0:T(8,128)(2,1)}, u32[]{:S(2)}) copy-start(bf16[512,1536]{1,0:T(8,128)(2,1)} %w_qkv_ref.1) | copy-start | bytes 4718596
  32.3 1.2 copy-start.1
  32.3 1.2 copy-start.2
  44.2 48.3 %collective-permute-start.8 = (bf16[180,512]{1,0:T(8,128)(2,1)}, bf16[180,512]{1,0:T(8,128)(2,1)}, u32[]{:S(2)}, u32[]{:S(2)}) collective-permute-start(bf16[180,512]{1,0:T(8,128)(2,1)} %get-tuple-element.141), channel_id=1, source_target_pairs={{0,16},{16,32},{32,48},{48,64},{64,80},{80,96},{96,112},{112,128},... | collective-permute-start | bytes 552968 | tf_op jit(solution)/shard_map/ppermute | solution.py:389
  52.2 7.9 %collective-permute-start.4 = (bf16[16,17,16,128]{3,2,1,0:T(8,128)(2,1)S(1)}, bf16[16,17,16,128]{3,2,1,0:T(8,128)(2,1)S(1)}, u32[]{:S(2)}, u32[]{:S(2)}) collective-permute-start(bf16[16,17,16,128]{3,2,1,0:T(8,128)(2,1)S(1)} %get-tuple-element.327), channel_id=1, source_target_pairs={{0,1},{1,0},{2,3},{3,2},{4,5},{5,4},{6,7},{7,6},{8,9},{9,8},{10,11... | collective-permute-start | bytes 3342344 | tf_op jit(solution)/shard_map/while/body/ppermute | solution.py:393
  61.4 30.1 %all-to-all-start = ((bf16[16,17,16,128]{3,2,1,0:T(8,128)(2,1)}), bf16[16,17,16,128]{3,2,1,0:T(8,128)(2,1)S(1)}, u32[]{:S(2)}, u32[]{:S(2)}) async-start(bf16[16,17,16,128]{3,2,1,0:T(8,128)(2,1)} %pair_sum.1), calls=%async_computation | async-start | bytes 2228224 | tf_op jit(solution)/shard_map/while/body/all_to_all | solution.py:397
  92.5 22.0 %all-to-all-start.1 = ((bf16[16,2,16,128]{3,2,1,0:T(8,128)(2,1)}), bf16[16,2,16,128]{3,2,1,0:T(8,128)(2,1)S(1)}, u32[]{:S(2)}, u32[]{:S(2)}) async-start(bf16[16,2,16,128]{3,2,1,0:T(8,128)(2,1)} %get-tuple-element.144), calls=%async_computation.1 | async-start | bytes 262144 | tf_op jit(solution)/shard_map/all_to_all | solution.py:411
  115.2 23.5 %all-to-all-start.2 = ((bf16[32,16,128]{2,1,0:T(8,128)(2,1)}), bf16[32,16,128]{2,1,0:T(8,128)(2,1)S(1)}, u32[]{:S(2)}, u32[]{:S(2)}) async-start(bf16[32,16,128]{2,1,0:T(8,128)(2,1)} %get-tuple-element.145), calls=%async_computation.2 | async-start | bytes 262144 | tf_op jit(solution)/shard_map/all_to_all | solution.py:418
  122.9 7.3 %collective-permute-start.9 = (bf16[2,36,512]{2,1,0:T(8,128)(2,1)S(1)}, bf16[2,36,512]{2,1,0:T(8,128)(2,1)S(1)}, u32[]{:S(2)}, u32[]{:S(2)}) collective-permute-start(bf16[2,36,512]{2,1,0:T(8,128)(2,1)S(1)} %pad_maximum_fusion.1), channel_id=1, source_target_pairs={{0,1},{1,2},{2,3},{3,4},{4,5},{5,6},{6,7},{7,8},{8,9},{9,10},{10,1... | collective-permute-start | bytes 221192 | tf_op jit(solution)/shard_map/ppermute | solution.py:408

commit v4 on v3

v4 whole, which is shorter than its diff:
```python
import functools
import math

import jax
import jax.numpy as jnp
from jax import lax
from jax.experimental import pallas as pl
from jax.experimental.pallas import tpu as pltpu
from jax.sharding import Mesh, PartitionSpec as P

HEADS = 16
HEAD_DIM = 32
WLAT = 6
WLON = 12
WINDOW = 144
TOKENS = 288
HALF = 72
EXTRA = 80
ALL_TOKENS = TOKENS + EXTRA
BLOCK = 36
GROUP = 4
BF16 = jnp.bfloat16
F32 = jnp.float32
LON = ("zh", "y", "x")
LAT = ("zq", "zb", "c")
ALONG_Z = ("zh", "zq", "zb")
ALL = LON + LAT
MIDS = ((0, 3), (3, 0), (3, 1), (1, 3), (2, 0), (0, 2), (1, 0), (2, 3))


def nn(a, b):
    return lax.dot_general(a, b, (((1,), (0,)), ((), ())), preferred_element_type=F32)


def nt(a, b):
    return lax.dot_general(a, b, (((1,), (1,)), ((), ())), preferred_element_type=F32)


def tn(a, b):
    return lax.dot_general(a, b, (((0,), (0,)), ((), ())), preferred_element_type=F32)


def attention_group(start, size, masked, group, qkv, d_attn, attended_t, dqkv):
    feature = HEADS * HEAD_DIM
    width = GROUP * HEAD_DIM
    rows = pl.ds(start, size)
    at = group * width

    def columns(offset):
        return pl.ds(pl.multiple_of(at + offset, 128), width)

    queries = qkv[rows, columns(0)]
    keys = qkv[rows, columns(feature)]
    values = qkv[rows, columns(2 * feature)]
    grads = d_attn[rows, columns(0)]
    scale = 1.0 / math.sqrt(HEAD_DIM)
    lane_head = lax.broadcasted_iota(jnp.int32, (1, width), 1) // HEAD_DIM
    key_late = lax.broadcasted_iota(jnp.int32, (size, size), 0) >= HALF
    query_late = lax.broadcasted_iota(jnp.int32, (size, size), 1) >= HALF
    allowed = jnp.logical_or(key_late == query_late, jnp.logical_not(masked))

    own = [(lane_head == head).astype(BF16) for head in range(GROUP)]
    key_stack = jnp.concatenate([keys * mask for mask in own], axis=0)
    value_stack = jnp.concatenate([values * mask for mask in own], axis=0)
    scores_all = nt(key_stack, queries)
    dprob_all = nt(value_stack, grads)
    prob_parts, dscore_parts = [], []
    for head in range(GROUP):
        part = slice(head * size, (head + 1) * size)
        scores = jnp.where(allowed, scores_all[part] * (scale * math.log2(math.e)), -jnp.inf)
        weights = jnp.exp2(scores - jnp.max(scores, axis=0, keepdims=True))
        prob = weights * (1.0 / jnp.sum(weights, axis=0, keepdims=True))
        dprob = dprob_all[part]
        delta = jnp.sum(prob * dprob, axis=0, keepdims=True)
        dscore_parts.append((prob * (dprob - delta) * scale).astype(BF16))
        prob_parts.append(prob.astype(BF16))
    prob_all = jnp.concatenate(prob_parts, axis=0)
    dscore_all = jnp.concatenate(dscore_parts, axis=0)

    def own_columns(stack):
        picked = stack[0:size]
        for head in range(1, GROUP):
            picked = jnp.where(lane_head == head, stack[head * size : (head + 1) * size], picked)
        return picked.astype(BF16)

    def turned(array):
        return array.astype(F32).T.astype(BF16)

    def by_head(heads_t, parts):
        return jnp.concatenate(
            [
                nn(heads_t[head * HEAD_DIM : (head + 1) * HEAD_DIM], parts[head])
                for head in range(GROUP)
            ],
            axis=0,
        )

    attended_t[pl.ds(pl.multiple_of(at, 128), width), :] = by_head(
        turned(values), prob_parts
    ).astype(BF16)
    dqkv[rows, columns(0)] = by_head(turned(keys), dscore_parts).T.astype(BF16)
    dqkv[rows, columns(feature)] = own_columns(nn(dscore_all, queries))
    dqkv[rows, columns(2 * feature)] = own_columns(nn(prob_all, grads))


def block_kernel(
    place, own_ref, usual_ref, usual_corner_ref, crossed_ref, lat_ref, extra_ref,
    gain_ref, w_qkv_ref, w_out_ref,
    drolled_ref, back_ref, dy_ref, hidden_ref, dqkv_ref, attended_ref, attended_extra_ref,
    gain_tile_ref, nothing_ref,
    x_ref, dy_wide_ref, normed_ref, inverse_ref, qkv_ref, d_attn_ref,
):
    first = place[0]
    last = place[1]
    east = place[3] == 1
    feature = HEADS * HEAD_DIM
    regular = pl.ds(0, TOKENS)
    extra = pl.ds(TOKENS, EXTRA)

    for kind, ref in ((0, x_ref), (1, dy_wide_ref)):

        def fetched(k, usual):
            return jnp.where(east, crossed_ref[k, kind].astype(F32), usual.astype(F32))

        blocks = (
            own_ref[0, kind], own_ref[1, kind], fetched(0, usual_ref[0, kind]),
            fetched(1, usual_ref[1, kind]), own_ref[2, kind], fetched(2, usual_ref[2, kind]),
            fetched(3, usual_corner_ref[kind]), lat_ref[kind], own_ref[3, kind], extra_ref[kind],
        )
        for at, part in enumerate(blocks):
            ref[at * BLOCK : (at + 1) * BLOCK, :] = part.astype(F32)
        ref[TOKENS + HALF :, :] = jnp.zeros((EXTRA - HALF, feature), F32)
    dy_ref[...] = dy_wide_ref[...].astype(BF16)

    def project(rows):
        values = x_ref[rows, :]
        centred = values - jnp.mean(values, axis=-1, keepdims=True)
        inverse = lax.rsqrt(jnp.mean(centred * centred, axis=-1, keepdims=True) + 1e-05)
        normed = centred * inverse
        normed_ref[rows, :] = normed
        inverse_ref[rows, :] = jnp.broadcast_to(inverse, (inverse.shape[0], 128))
        hidden = (normed * gain_ref[...]).astype(BF16)
        hidden_ref[rows, :] = hidden
        qkv_ref[rows, :] = nn(hidden, w_qkv_ref[...]).astype(BF16)
        d_attn_ref[rows, :] = nt(dy_ref[rows, :], w_out_ref[...]).astype(BF16)

    def finish(rows):
        dhidden = nt(dqkv_ref[rows, :], w_qkv_ref[...])
        normed = normed_ref[rows, :]
        dnorm = dhidden * gain_ref[...]
        drolled = dy_wide_ref[rows, :] + inverse_ref[rows, 0:1] * (
            dnorm
            - jnp.mean(dnorm, axis=-1, keepdims=True)
            - normed * jnp.mean(dnorm * normed, axis=-1, keepdims=True)
        )
        drolled_ref[rows, :] = drolled.astype(BF16)
        back_ref[0:72, :] = drolled[72:144].astype(BF16)
        back_ref[72:144, :] = drolled[180:252].astype(BF16)
        if drolled.shape[0] > TOKENS:
            back_ref[144:180, :] = drolled[324:360].astype(BF16)
        else:
            back_ref[144:180, :] = jnp.zeros((BLOCK, feature), BF16)

        gain_local = jnp.sum(dhidden * normed, axis=0, keepdims=True)
        coarse = gain_local.astype(BF16)
        fine = (gain_local - coarse.astype(F32)).astype(BF16)
        parts = [part[:, 128 * j : 128 * (j + 1)] for part in (coarse, fine) for j in range(4)]
        gain_tile_ref[...] = jnp.concatenate(
            [part.astype(F32) for part in parts], axis=0
        ).astype(BF16)

    groups = HEADS // GROUP

    def attention(windows):
        @pl.loop(0, windows * groups)
        def _(step):
            window = step // groups
            attention_group(
                pl.multiple_of(window * WINDOW, 16), WINDOW,
                jnp.logical_and(last == 1, window == 1), step % groups,
                qkv_ref, d_attn_ref, attended_ref.at[window], dqkv_ref,
            )

    @pl.when(first == 0)
    def _():
        project(regular)
        attention(TOKENS // WINDOW)
        finish(regular)
        hidden_ref[extra, :] = jnp.zeros((EXTRA, feature), BF16)
        attended_extra_ref[...] = jnp.zeros((feature, EXTRA), BF16)
        dqkv_ref[extra, :] = jnp.zeros((EXTRA, 3 * feature), BF16)
        drolled_ref[extra, :] = jnp.zeros((EXTRA, feature), BF16)

    @pl.when(first == 1)
    def _():
        project(pl.ds(0, ALL_TOKENS))
        attention(TOKENS // WINDOW)

        @pl.loop(0, groups)
        def _(group):
            attention_group(
                TOKENS, EXTRA, first == 1, group,
                qkv_ref, d_attn_ref, attended_extra_ref, dqkv_ref,
            )

        finish(pl.ds(0, ALL_TOKENS))

    nothing_ref[...] = jnp.zeros(nothing_ref.shape, BF16)


def block(place, *operands):
    feature = HEADS * HEAD_DIM
    vmem = pl.BlockSpec(memory_space=pltpu.VMEM)

    def half(*shape):
        return jax.ShapeDtypeStruct(shape, BF16)

    return pl.pallas_call(
        block_kernel,
        out_shape=(
            half(ALL_TOKENS, feature), half(5 * BLOCK, feature), half(ALL_TOKENS, feature),
            half(ALL_TOKENS, feature), half(ALL_TOKENS, 3 * feature),
            half(TOKENS // WINDOW, feature, WINDOW), half(feature, EXTRA),
            half(8, 128), half(16, 72, 128),
        ),
        in_specs=[pl.BlockSpec(memory_space=pltpu.SMEM)] + [vmem] * len(operands),
        out_specs=(vmem,) * 9,
        scratch_shapes=[
            pltpu.VMEM((ALL_TOKENS, feature), F32),
            pltpu.VMEM((ALL_TOKENS, feature), F32),
            pltpu.VMEM((ALL_TOKENS, feature), F32),
            pltpu.VMEM((ALL_TOKENS, 128), F32),
            pltpu.VMEM((ALL_TOKENS, 3 * feature), BF16),
            pltpu.VMEM((ALL_TOKENS, feature), BF16),
        ],
        compiler_params=pltpu.CompilerParams(vmem_limit_bytes=40 * 1024 * 1024),
        cost_estimate=pl.CostEstimate(
            flops=2_000_000_000, bytes_accessed=6_000_000, transcendentals=700_000
        ),
        name="window_block",
    )(place, *operands)


def weights_kernel(
    place, hidden_ref, dqkv_ref, attended_ref, attended_extra_ref, dy_ref, gain_tile_ref,
    keep_ref, send_ref, total_ref,
):
    core = place[2]
    feature = HEADS * HEAD_DIM
    total_ref[:, 0 : 3 * feature] = tn(hidden_ref[...], dqkv_ref[...]).astype(BF16)
    out_total = nn(attended_extra_ref[...], dy_ref[TOKENS:, :])
    for window in range(TOKENS // WINDOW):
        rows = slice(window * WINDOW, (window + 1) * WINDOW)
        out_total = out_total + nn(attended_ref[window], dy_ref[rows, :])
    total_ref[:, 3 * feature :] = out_total.astype(BF16)
    for lon in range(16):
        for ref in (keep_ref, send_ref):
            ref[lon, 0, 128:136] = gain_tile_ref[...]
            ref[lon, 1, 128:136] = gain_tile_ref[...]

    def deal(halves):
        @pl.loop(0, 16)
        def _(lon):
            for zh in range(2):
                start = pl.multiple_of(zh * 256 + lon * 16, 16)
                rows = total_ref[pl.ds(start, 16), :]
                for j in range(16):
                    tile = (zh * 4 + j % 4) * 16
                    halves[j // 8][lon, j % 8 // 4, tile : tile + 16] = rows[:, 128 * j : 128 * (j + 1)]

    @pl.when(core == 0)
    def _():
        deal((keep_ref, send_ref))

    @pl.when(core == 1)
    def _():
        deal((send_ref, keep_ref))


def weight_terms(place, *operands):
    feature = HEADS * HEAD_DIM
    vmem = pl.BlockSpec(memory_space=pltpu.VMEM)
    dealt = jax.ShapeDtypeStruct((16, 2, 136, 128), BF16)
    return pl.pallas_call(
        weights_kernel,
        out_shape=(dealt, dealt),
        in_specs=[pl.BlockSpec(memory_space=pltpu.SMEM)] + [vmem] * len(operands),
        out_specs=(vmem, vmem),
        scratch_shapes=[pltpu.VMEM((feature, 4 * feature), BF16)],
        compiler_params=pltpu.CompilerParams(vmem_limit_bytes=40 * 1024 * 1024),
        cost_estimate=pl.CostEstimate(
            flops=700_000_000, bytes_accessed=4_000_000, transcendentals=0
        ),
        name="weight_terms",
    )(place, *operands)


def small_call(body, name, out_shape, *operands, place=None):
    vmem = pl.BlockSpec(memory_space=pltpu.VMEM)
    many = isinstance(out_shape, tuple)
    head = () if place is None else (place,)
    return pl.pallas_call(
        body,
        out_shape=out_shape,
        in_specs=[pl.BlockSpec(memory_space=pltpu.SMEM)] * len(head) + [vmem] * len(operands),
        out_specs=(vmem,) * len(out_shape) if many else vmem,
        compiler_params=pltpu.CompilerParams(vmem_limit_bytes=8 * 1024 * 1024),
        name=name,
    )(*head, *operands)


def pack_kernel(x_ref, dy_ref, west_ref, corner_ref, top_ref, own_ref, wide_ref):
    for kind, ref in ((0, x_ref), (1, dy_ref)):
        for band in range(4):
            for side in range(2):
                at = (kind * 4 + band) * 2 + side
                for i in range(BLOCK // 2):
                    pair = ref[band * 3 + i // 6, side * 6 + i % 6]
                    wide_ref[at, 2 * i : 2 * i + 2, :] = pair.astype(F32)
                part = wide_ref[at].astype(BF16)
                if side == 1:
                    own_ref[(band + 3) % 4, kind] = part
                    if band == 0:
                        top_ref[kind] = part
                elif band == 0:
                    corner_ref[kind] = part
                else:
                    west_ref[band - 1, kind] = part


def pack(block_input, cotangent):
    feature = block_input.shape[-1]
    vmem = pl.BlockSpec(memory_space=pltpu.VMEM)

    def blocks(*lead):
        return jax.ShapeDtypeStruct((*lead, 2, BLOCK, feature), BF16)

    return pl.pallas_call(
        pack_kernel,
        out_shape=(blocks(3), blocks(), blocks(), blocks(4)),
        in_specs=[vmem] * 2,
        out_specs=(vmem,) * 4,
        scratch_shapes=[pltpu.VMEM((16, BLOCK, feature), F32)],
        compiler_params=pltpu.CompilerParams(vmem_limit_bytes=16 * 1024 * 1024),
        name="pack",
    )(block_input.transpose(1, 2, 0, 3), cotangent.transpose(1, 2, 0, 3))


def pair_kernel(keep_ref, other_ref, out_ref):
    @pl.loop(0, 32)
    def _(chunk):
        total = keep_ref[chunk].astype(F32) + other_ref[chunk].astype(F32)
        out_ref[chunk] = total.astype(BF16)


def plane_kernel(parts_ref, out_ref):
    def total(rows):
        terms = parts_ref[0, rows].astype(F32)
        for chunk in range(1, 32):
            terms = terms + parts_ref[chunk, rows].astype(F32)
        return terms.astype(BF16)

    gain = total(slice(128, 136))
    for z in range(16):
        out_ref[z, 64:72] = gain

    for zh in range(2):
        tiles = total(slice(zh * 64, zh * 64 + 64))
        for zl in range(8):
            out_ref[zh * 8 + zl, 0:64] = tiles


def column_kernel(parts_ref, half_ref, gain_ref):
    for side in range(2):
        total = parts_ref[side, 0:64].astype(F32)
        for z in range(2 + side, 16, 2):
            total = total + parts_ref[z, 0:64].astype(F32)
        half_ref[side * 64 : side * 64 + 64] = total.astype(BF16)
    gain = parts_ref[0, 64:72].astype(F32)
    for z in range(2, 16, 2):
        gain = gain + parts_ref[z, 64:72].astype(F32)
    gain_ref[...] = gain[0:4] + gain[4:8]


def spread_kernel(place, own_ref, other_ref, qkv_ref, out_ref):
    core = place[2]
    for j in range(16):
        rows = slice(j % 8 * 16, j % 8 * 16 + 16)
        own, other = own_ref[rows].astype(F32), other_ref[rows].astype(F32)
        tile = jnp.where(core == j // 8, own, other)
        if j < 12:
            qkv_ref[:, 128 * j : 128 * (j + 1)] = tile
        else:
            out_ref[:, 128 * (j - 12) : 128 * (j - 11)] = tile


def index(zh, y, x, zl, c):
    return (((zh * 4 + y) * 4 + x) * 8 + zl) * 2 + c


def in_one_piece(work, start):
    once = jnp.minimum(lax.axis_index(LAT) + 1, 1)

    def body(turn, values):
        values, _ = lax.optimization_barrier((values, turn))
        return work(*values)

    return lax.fori_loop(0, once, body, start)


def middle_of(zh, lat):
    zl, c = lat // 2, lat % 2
    y, x = MIDS[zl]
    z = (zh * 8 + zl + 1 - 2 * c) % 16
    return index(z // 8, y, x, z % 8, c)


def fetch(blocks, corner, top, first_block):
    out, out_corner, onward = [], [], []
    for zh in range(2):
        for lat in range(16):
            middle, target = middle_of(zh, lat), index(1 - zh, 3, 3, lat // 2, lat % 2)
            out.append((index(zh, 0, 0, lat // 2, lat % 2), middle))
            onward.append((middle, target))
            if lat < 15:
                out_corner.append((index(zh, 0, 0, (lat + 1) // 2, (lat + 1) % 2), middle))
    halfway = lax.ppermute(blocks, ALL, out)
    halfway_corner = lax.ppermute(corner, ALL, out_corner)
    halfway, halfway_corner, blocks, corner, top, first_block = lax.optimization_barrier(
        (halfway, halfway_corner, blocks, corner, top, first_block)
    )
    crossed = lax.ppermute(jnp.concatenate([halfway, halfway_corner[None]]), ALL, onward)
    inner = [i for i in range(32) if i % 16 < 15]

    def usual(blocks, corner, top, first_block):
        return (
            lax.ppermute(blocks, LON, [(i + 1, i) for i in inner]),
            lax.ppermute(
                corner, ALL, [((i + 1) * 16 + j + 1, i * 16 + j) for i in inner for j in range(15)]
            ),
            lax.ppermute(top, LAT, [(j + 1, j) for j in range(15)]),
            lax.ppermute(first_block, ALL, [((i + 1) % 32 * 16, i * 16) for i in range(32)]),
        )

    usual_blocks = in_one_piece(usual, (blocks, corner, top, first_block))
    normal, normal_corner, lat_block, extra = usual_blocks
    return normal, normal_corner, crossed, lat_block, extra


def per_device(block_input, cotangent, norm_gain, w_qkv, w_out):
    half_lat, half_lon = WLAT // 2, WLON // 2
    levels, lat_rows, lon_cols, feature = block_input.shape
    west, corner, top, own = pack(block_input, cotangent)
    fetched = fetch(west, corner, top, corner)
    lat = lax.axis_index(LAT)
    first = lat == 0
    east = lax.axis_index(LON) % 16 == 15
    place = jnp.stack([first, lat == 15, lax.axis_index("c"), east]).astype(jnp.int32)
    drolled, back, grads, hidden, dqkv, *attended, gain_tile, nothing = block(
        place, own, *fetched, norm_gain.reshape(1, feature), w_qkv, w_out
    )

    back_lon = lax.ppermute(back, LON, [(i, (i + 1) % 32) for i in range(32)])

    def sum_in_planes(*operands):
        keep, send = weight_terms(place, *operands[:-1])
        other = lax.ppermute(send, "c", [(0, 1), (1, 0)])
        pair = small_call(
            pair_kernel, "pair_sum", jax.ShapeDtypeStruct((32, 136, 128), BF16),
            keep.reshape(32, 136, 128), other.reshape(32, 136, 128),
        )
        plane = lax.all_to_all(pair, ("y", "x", "zb"), 0, 0, tiled=True)
        plane = small_call(
            plane_kernel, "plane_sum", jax.ShapeDtypeStruct((16, 72, 128), BF16), plane
        )
        return *operands[:-1], plane

    *_, plane = in_one_piece(
        sum_in_planes, (hidden, dqkv, *attended, grads, gain_tile, nothing)
    )
    plane, back_lon = lax.optimization_barrier((plane, back_lon))
    back_lat = lax.ppermute(
        jnp.stack([drolled[252:288], back_lon[108:144]]), LAT, [(j, j + 1) for j in range(15)]
    )
    column = lax.all_to_all(plane, ALONG_Z, 0, 0, tiled=True)
    def grid(piece):
        return piece.reshape(half_lat, half_lon, levels, feature)

    rows = [
        (jnp.where(first, back_lon[144:180], back_lat[1]), jnp.where(first, drolled[288:324], back_lat[0])),
        (back_lon[0:36], drolled[0:36]),
        (back_lon[36:72], drolled[36:72]),
        (back_lon[72:108], drolled[144:180]),
    ]
    input_grad = jnp.concatenate(
        [jnp.concatenate([grid(west), grid(east)], axis=1) for west, east in rows], axis=0
    )
    column, input_grad = lax.optimization_barrier((column, input_grad))
    half, gain_rows = small_call(
        column_kernel, "column_sum",
        (jax.ShapeDtypeStruct((128, 128), BF16), jax.ShapeDtypeStruct((4, 128), F32)),
        column,
    )
    gain_grad = gain_rows.reshape(feature)
    other_half = lax.ppermute(half, "c", [(0, 1), (1, 0)])
    qkv_grad, out_grad = small_call(
        spread_kernel, "spread",
        (
            jax.ShapeDtypeStruct((16, 3 * feature), F32),
            jax.ShapeDtypeStruct((16, feature), F32),
        ),
        half, other_half, place=place,
    )

    input_grad = input_grad.transpose(2, 0, 1, 3)
    return input_grad, qkv_grad, out_grad, gain_grad


def solution(mesh):
    fine = Mesh(mesh.devices.reshape(2, 4, 4, 4, 2, 2), ALL)
    grid_spec = P(None, LAT, LON, None)
    return jax.shard_map(
        per_device,
        mesh=fine,
        in_specs=(grid_spec, grid_spec, P(), P(), P()),
        out_specs=(grid_spec, P(LON, None), P(LON, None), P()),
        check_vma=False,
    )
```

time: 141 us -> 131 us (0.929)
  waiting for transfers between devices: 46.2 us -> 33.6 us
  starting transfers between devices: 65.5 us -> 70.6 us
  local copies, waits for them, and re-layouts: 5.35 us -> 2.86 us
  Pallas kernels: 17.8 us -> 19.8 us
  other arithmetic: 3.91 us -> 2.06 us
    all_to_all x3 -> x2, waiting for transfers between devices: 34.4 us -> 17.7 us  [the longest x1 17.7 us: sum_in_planes(): plane = lax.all_to_all(pair, ('y', 'x', 'zb'), 0, 0, tiled=True)]
    ppermute x1 -> x2, starting transfers between devices: 5.52 us -> 15.7 us  [the longest x1 10.6 us: per_device(): other_half = lax.ppermute(half, 'c', [(0, 1), (1, 0)])]
    all_to_all x3 -> x2, starting transfers between devices: 30.7 us -> 23.7 us  [the longest x1 13.3 us: sum_in_planes(): plane = lax.all_to_all(pair, ('y', 'x', 'zb'), 0, 0, tiled=True)]
    ppermute x1, waiting for transfers between devices: 3.72 us -> 6.96 us  [per_device(): lax.ppermute(jnp.stack([drolled[252:288], back_lon[108:144]]), LAT, [(j,...]
    another operation x3 -> x1, other arithmetic: 2.77 us -> 0.08 us  [per_device(): jnp.stack([first, lat == 15, lax.axis_index('c'), east]).astype(jnp.int32)]
    ppermute x1, starting transfers between devices: 3.54 us -> 5.53 us  [per_device(): lax.ppermute(jnp.stack([drolled[252:288], back_lon[108:144]]), LAT, [(j,...]
    pallas_call x1 -> x2, Pallas kernels: 2.91 us -> 4.47 us  [the longest x1 3.37 us: weight_terms(): pl.pallas_call(weights_kernel, out_shape=(dealt, dealt), in_specs=[pl.Blo...]
    ppermute x1 -> x2, waiting for transfers between devices: 2.36 us -> 3.2 us  [the longest x1 2.36 us: sum_in_planes(): other = lax.ppermute(send, 'c', [(0, 1), (1, 0)])]
  transfers between devices with their start and end apart: 13 -> 13, of which waited for: 8 -> 7; matrix products, arithmetic and copies ran while one was open for 3% -> 2% of each run, Pallas kernels for 4% -> 4%
where the time goes in v4:
time: 131 us; the launch traced here: 130 us
  starting transfers between devices  70.6 us (54%)
  waiting for transfers between devices  33.6 us (26%)
  Pallas kernels  19.8 us (15%)
  local copies, waits for them, and re-layouts  2.86 us (2%)
  other arithmetic  2.06 us (2%)
    all_to_all x1, waiting for transfers between devices, sum_in_planes(): plane = lax.all_to_all(pair, ('y', 'x', 'zb'), 0, 0, tiled=True)  17.7 us
    ppermute x1, starting transfers between devices, fetch(): halfway = lax.ppermute(blocks, ALL, out)  14.1 us
    all_to_all x1, starting transfers between devices, sum_in_planes(): plane = lax.all_to_all(pair, ('y', 'x', 'zb'), 0, 0, tiled=True)  13.3 us
    pallas_call x1, Pallas kernels, block(): pl.pallas_call(block_kernel, out_shape=(half(ALL_TOKENS, feature), half(5...  11.3 us
    ppermute x1, starting transfers between devices, per_device(): other_half = lax.ppermute(half, 'c', [(0, 1), (1, 0)])  10.6 us
    all_to_all x1, starting transfers between devices, per_device(): column = lax.all_to_all(plane, ALONG_Z, 0, 0, tiled=True)  10.3 us
    ppermute x1, waiting for transfers between devices, per_device(): lax.ppermute(jnp.stack([drolled[252:288], back_lon[108:144]]), LAT, [(j,...  6.96 us
    ppermute x1, starting transfers between devices, per_device(): lax.ppermute(jnp.stack([drolled[252:288], back_lon[108:144]]), LAT, [(j,...  5.53 us
  transfers between devices with their start and end apart: 13, of which 7 were waited for; matrix products, arithmetic and copies ran while one was open for 2% of the time, Pallas kernels for 4%

profile of v4, /device:TPU:1, one launch (start us, length us, event | category | flops | bytes accessed | tf_op | source)
XLA Modules:
  0.0 130.0 jit_solution(7897661507505410824)
XLA Ops:
  0.6 0.0 copy-start
  0.6 1.0 copy-done
  1.6 0.0 copy-start.1
  1.6 1.0 copy-done.1
  2.6 0.0 copy-start.3
  2.6 1.1 pack.1
  3.7 14.1 %collective-permute-start.5 = (bf16[3,2,36,512]{3,2,1,0:T(8,128)(2,1)}, bf16[3,2,36,512]{3,2,1,0:T(8,128)(2,1)S(1)}, u32[]{:S(2)}, u32[]{:S(2)}) collective-permute-start(bf16[3,2,36,512]{3,2,1,0:T(8,128)(2,1)} %get-tuple-element.330), channel_id=1, source_target_pairs={{0,50},{1,319},{2,196},{3,193},{4,214},{5,211},{6,120},{7,117},{8,... | collective-permute-start | bytes 663560 | tf_op jit(solution)/shard_map/ppermute | solution.py:427
  17.8 1.3 collective-permute-start.6
  19.1 1.5 %collective-permute-done.6 = bf16[2,36,512]{2,1,0:T(8,128)(2,1)S(1)} collective-permute-done((bf16[2,36,512]{2,1,0:T(8,128)(2,1)S(1)}, bf16[2,36,512]{2,1,0:T(8,128)(2,1)S(1)}, u32[]{:S(2)}, u32[]{:S(2)}) %collective-permute-start.6) | collective-permute-done | bytes 73760 | tf_op jit(solution)/shard_map/ppermute | solution.py:428
  20.6 0.7 collective-permute-done.5
  21.2 0.0 copy-start.2
  21.2 0.8 pad_maximum_fusion
  22.0 0.7 collective-permute-start.7
  22.7 0.1 pad_add_fusion.place
  22.8 0.0 copy-start.4
  22.8 9.7 %while.38 = (s32[]{:T(128)}, bf16[3,2,36,512]{3,2,1,0:T(8,128)(2,1)}, bf16[2,36,512]{2,1,0:T(8,128)(2,1)S(1)}, bf16[2,36,512]{2,1,0:T(8,128)(2,1)S(1)}, bf16[2,3...) while((s32[]{:T(128)}, bf16[3,2,36,512]{3,2,1,0:T(8,128)(2,1)}, bf16[2,36,512]{2,1,0:T(8,128)(2,1)S(1)}, ...), condition=%wide.region_1.0_spmd, body=%wide.region_0.0_spmd.sunk | while | flops 2 | bytes 2654445 | solution.py:408
  22.8 1.3 collective-permute-start
  24.1 1.3 collective-permute-start.1
  25.4 1.9 %collective-permute-start.2 = (bf16[2,36,512]{2,1,0:T(8,128)(2,1)S(1)}, bf16[2,36,512]{2,1,0:T(8,128)(2,1)S(1)}, u32[]{:S(2)}, u32[]{:S(2)}) collective-permute-start(bf16[2,36,512]{2,1,0:T(8,128)(2,1)S(1)} %get-tuple-element.310), channel_id=1, source_target_pairs={{1,0},{2,1},{3,2},{4,3},{5,4},{6,5},{7,6},{8,7},{9,8},{10,9},{11,1... | collective-permute-start | bytes 221192 | tf_op jit(solution)/shard_map/while/body/ppermute | solution.py:441
  27.3 0.7 collective-permute-start.3
  28.0 3.7 %collective-permute-done.1 = bf16[2,36,512]{2,1,0:T(8,128)(2,1)S(1)} collective-permute-done((bf16[2,36,512]{2,1,0:T(8,128)(2,1)S(1)}, bf16[2,36,512]{2,1,0:T(8,128)(2,1)S(1)}, u32[]{:S(2)}, u32[]{:S(2)}) %collective-permute-start.1) | collective-permute-done | bytes 73760 | tf_op jit(solution)/shard_map/while/body/ppermute | solution.py:438
  31.7 0.0 collective-permute-done.2
  31.7 0.0 collective-permute-done.3
  31.8 0.0 collective-permute-done
  31.8 0.7 copy.20
  32.5 0.0 collective-permute-done.7.crossed_ref
  32.5 0.0 copy-done.3
  32.5 0.0 copy-done.2
  32.5 0.0 copy-done.4
  32.5 11.3 %window_block.1 = (bf16[368,512]{1,0:T(8,128)(2,1)S(1)}, bf16[180,512]{1,0:T(8,128)(2,1)}, bf16[368,512]{1,0:T(8,128)(2,1)}, bf16[368,512]{1,0:T(8,128)(2,1)}, b...) custom-call(s32[4]{0:T(128)S(1)} %pad_add_fusion.place, ...), custom_call_target="tpu_custom_call" | custom-call | flops 2000000000 | bytes 6000000 | tf_op jit(solution)/shard_map/window_block/pallas_call | solution.py:218
  43.8 4.5 %collective-permute-start.8 = (bf16[180,512]{1,0:T(8,128)(2,1)}, bf16[180,512]{1,0:T(8,128)(2,1)S(1)}, u32[]{:S(2)}, u32[]{:S(2)}) collective-permute-start(bf16[180,512]{1,0:T(8,128)(2,1)} %get-tuple-element.153), channel_id=1, source_target_pairs={{0,16},{16,32},{32,48},{48,64},{64,80},{80,96},{96,112},{112,128},... | collective-permute-start | bytes 552968 | tf_op jit(solution)/shard_map/ppermute | solution.py:463
  48.3 44.1 %while.39 = (s32[]{:T(128)}, bf16[368,512]{1,0:T(8,128)(2,1)}, bf16[368,1536]{1,0:T(8,128)(2,1)}, bf16[2,512,144]{2,1,0:T(8,128)(2,1)}, bf16[512,80]{1,0:T(8,128...) while((s32[]{:T(128)}, bf16[368,512]{1,0:T(8,128)(2,1)}, ...), condition=%wide.region_3.4_spmd, body=%wide.region_2.3_spmd.sunk | while | flops 700000000 | bytes 11798965 | solution.py:408
  48.3 3.4 %weight_terms.1 = (bf16[16,2,136,128]{3,2,1,0:T(8,128)(2,1)S(1)}, bf16[16,2,136,128]{3,2,1,0:T(8,128)(2,1)S(1)}) custom-call(s32[4]{0:T(128)S(1)} %get-tuple-element.381.place, bf16[368,512]{1,0:T(8,128)(2,1)} %get-tuple-element.373.hidden_ref, bf16[368,1536]{1,0:T(8,128)(2,1)} %get-tuple-element.374.dqkv_ref, ...), custom_call_target="tpu_custom_call" | custom-call | flops 700000000 | bytes 4000000 | tf_op jit(solution)/shard_map/while/body/weight_terms/pallas_call | solution.py:284
  51.7 5.1 %collective-permute-start.4 = (bf16[16,2,136,128]{3,2,1,0:T(8,128)(2,1)S(1)}, bf16[16,2,136,128]{3,2,1,0:T(8,128)(2,1)S(1)}, u32[]{:S(2)}, u32[]{:S(2)}) collective-permute-start(bf16[16,2,136,128]{3,2,1,0:T(8,128)(2,1)S(1)} %get-tuple-element.328), channel_id=1, source_target_pairs={{0,1},{1,0},{2,3},{3,2},{4,5},{5,4},{6,7},{7,6},{8,9},{9,8},{10,11... | collective-permute-start | bytes 3342344 | tf_op jit(solution)/shard_map/while/body/ppermute | solution.py:467
  56.7 2.4 %collective-permute-done.4 = bf16[16,2,136,128]{3,2,1,0:T(8,128)(2,1)S(1)} collective-permute-done((bf16[16,2,136,128]{3,2,1,0:T(8,128)(2,1)S(1)}, bf16[16,2,136,128]{3,2,1,0:T(8,128)(2,1)S(1)}, u32[]{:S(2)}, u32[]{:S(2)}) %collective-permute-start.4) | collective-permute-done | bytes 1114144 | tf_op jit(solution)/shard_map/while/body/ppermute | solution.py:467
  59.1 1.4 %pair_sum.1 = bf16[32,136,128]{2,1,0:T(8,128)(2,1)} custom-call(bf16[32,136,128]{2,1,0:T(8,128)(2,1)S(1)} %bitcast.28, bf16[32,136,128]{2,1,0:T(8,128)(2,1)S(1)} %bitcast.29), custom_call_target="tpu_custom_call" | custom-call | tf_op jit(solution)/shard_map/while/body/pair_sum/pallas_call | solution.py:302
  60.5 13.3 %all-to-all-start = ((bf16[32,136,128]{2,1,0:T(8,128)(2,1)}), bf16[32,136,128]{2,1,0:T(8,128)(2,1)S(1)}, u32[]{:S(2)}, u32[]{:S(2)}) async-start(bf16[32,136,128]{2,1,0:T(8,128)(2,1)} %pair_sum.1), calls=%async_computation | async-start | bytes 2228224 | tf_op jit(solution)/shard_map/while/body/all_to_all | solution.py:472
  73.8 17.7 %all-to-all-done.parts_ref = bf16[32,136,128]{2,1,0:T(8,128)(2,1)S(1)} async-done(((bf16[32,136,128]{2,1,0:T(8,128)(2,1)}), bf16[32,136,128]{2,1,0:T(8,128)(2,1)S(1)}, u32[]{:S(2)}, u32[]{:S(2)}) %all-to-all-start) | async-done | bytes 1114144 | tf_op jit(solution)/shard_map/while/body/all_to_all | solution.py:472
  91.5 0.9 plane_sum.1
  92.4 0.0 collective-permute-done.8
  92.4 10.3 %all-to-all-start.1 = ((bf16[16,72,128]{2,1,0:T(8,128)(2,1)}), bf16[16,72,128]{2,1,0:T(8,128)(2,1)S(1)}, u32[]{:S(2)}, u32[]{:S(2)}) async-start(bf16[16,72,128]{2,1,0:T(8,128)(2,1)} %get-tuple-element.154), calls=%async_computation.1 | async-start | bytes 589824 | tf_op jit(solution)/shard_map/all_to_all | solution.py:485
  102.8 5.5 %collective-permute-start.9 = (bf16[2,36,512]{2,1,0:T(8,128)(2,1)S(1)}, bf16[2,36,512]{2,1,0:T(8,128)(2,1)S(1)}, u32[]{:S(2)}, u32[]{:S(2)}) collective-permute-start(bf16[2,36,512]{2,1,0:T(8,128)(2,1)S(1)} %pad_maximum_fusion.1), channel_id=1, source_target_pairs={{0,1},{1,2},{2,3},{3,4},{4,5},{5,6},{6,7},{7,8},{8,9},{9,10},{10,1... | collective-permute-start | bytes 221192 | tf_op jit(solution)/shard_map/ppermute | solution.py:482
  108.3 7.0 %collective-permute-done.9 = bf16[2,36,512]{2,1,0:T(8,128)(2,1)S(1)} collective-permute-done((bf16[2,36,512]{2,1,0:T(8,128)(2,1)S(1)}, bf16[2,36,512]{2,1,0:T(8,128)(2,1)S(1)}, u32[]{:S(2)}, u32[]{:S(2)}) %collective-permute-start.9) | collective-permute-done | bytes 73760 | tf_op jit(solution)/shard_map/ppermute | solution.py:482
  115.5 1.2 maximum_maximum_fusion
  116.7 0.0 all-to-all-done.1.parts_ref
  116.7 0.6 column_sum.1
  117.3 10.6 %collective-permute-start.10 = (bf16[128,128]{1,0:T(8,128)(2,1)S(1)}, bf16[128,128]{1,0:T(8,128)(2,1)S(1)}, u32[]{:S(2)}, u32[]{:S(2)}) collective-permute-start(bf16[128,128]{1,0:T(8,128)(2,1)S(1)} %get-tuple-element.159.own_ref), channel_id=1, source_target_pairs={{0,1},{1,0},{2,3},{3,2},{4,5},{5,4},{6,7},{7,6},{8,9},{9,8},{10,11... | collective-permute-start | bytes 98312 | tf_op jit(solution)/shard_map/ppermute | solution.py:505
  127.9 0.8 collective-permute-done.10.other_ref
  128.8 1.2 spread.1
  (16 shorter events, 0.3 us)
Async XLA Ops:
  0.6 1.0 copy-start
  1.6 1.0 copy-start.1
  2.6 29.9 %copy-start.3 = (bf16[512,512]{1,0:T(8,128)(2,1)S(1)}, bf16[512,512]{1,0:T(8,128)(2,1)}, u32[]{:S(2)}) copy-start(bf16[512,512]{1,0:T(8,128)(2,1)} %w_out_ref.1) | copy-start | bytes 1572868
  3.7 17.6 %collective-permute-start.5 = (bf16[3,2,36,512]{3,2,1,0:T(8,128)(2,1)}, bf16[3,2,36,512]{3,2,1,0:T(8,128)(2,1)S(1)}, u32[]{:S(2)}, u32[]{:S(2)}) collective-permute-start(bf16[3,2,36,512]{3,2,1,0:T(8,128)(2,1)} %get-tuple-element.330), channel_id=1, source_target_pairs={{0,50},{1,319},{2,196},{3,193},{4,214},{5,211},{6,120},{7,117},{8,... | collective-permute-start | bytes 663560 | tf_op jit(solution)/shard_map/ppermute | solution.py:427
  17.8 2.8 %collective-permute-start.6 = (bf16[2,36,512]{2,1,0:T(8,128)(2,1)S(1)}, bf16[2,36,512]{2,1,0:T(8,128)(2,1)S(1)}, u32[]{:S(2)}, u32[]{:S(2)}) collective-permute-start(bf16[2,36,512]{2,1,0:T(8,128)(2,1)S(1)} %get-tuple-element.333), channel_id=1, source_target_pairs={{1,50},{2,319},{3,196},{4,193},{5,214},{6,211},{7,120},{8,117},{9,... | collective-permute-start | bytes 221192 | tf_op jit(solution)/shard_map/ppermute | solution.py:428
  21.2 11.2 %copy-start.2 = (bf16[512,1536]{1,0:T(8,128)(2,1)S(1)}, bf16[512,1536]{1,0:T(8,128)(2,1)}, u32[]{:S(2)}) copy-start(bf16[512,1536]{1,0:T(8,128)(2,1)} %w_qkv_ref.1) | copy-start | bytes 4718596
  22.0 10.5 %collective-permute-start.7 = (bf16[4,2,36,512]{3,2,1,0:T(8,128)(2,1)}, bf16[4,2,36,512]{3,2,1,0:T(8,128)(2,1)S(1)}, u32[]{:S(2)}, u32[]{:S(2)}) collective-permute-start(bf16[4,2,36,512]{3,2,1,0:T(8,128)(2,1)} %pad_maximum_fusion), channel_id=1, source_target_pairs={{50,496},{319,497},{196,498},{193,499},{214,500},{211,501},{120,50... | collective-permute-start | bytes 884744 | tf_op jit(solution)/shard_map/ppermute | solution.py:432
  22.8 9.7 %copy-start.4 = (f32[512]{0:T(512)S(1)}, f32[512]{0:T(512)}, u32[]{:S(2)}) copy-start(f32[512]{0:T(512)} %param.11) | copy-start | bytes 6148
  22.8 8.9 %collective-permute-start = (bf16[3,2,36,512]{3,2,1,0:T(8,128)(2,1)}, bf16[3,2,36,512]{3,2,1,0:T(8,128)(2,1)S(1)}, u32[]{:S(2)}, u32[]{:S(2)}) collective-permute-start(bf16[3,2,36,512]{3,2,1,0:T(8,128)(2,1)} %get-tuple-element.308), channel_id=1, source_target_pairs={{16,0},{32,16},{48,32},{64,48},{80,64},{96,80},{112,96},{128,112},... | collective-permute-start | bytes 663560 | tf_op jit(solution)/shard_map/while/body/ppermute | solution.py:437
  24.1 7.6 %collective-permute-start.1 = (bf16[2,36,512]{2,1,0:T(8,128)(2,1)S(1)}, bf16[2,36,512]{2,1,0:T(8,128)(2,1)S(1)}, u32[]{:S(2)}, u32[]{:S(2)}) collective-permute-start(bf16[2,36,512]{2,1,0:T(8,128)(2,1)S(1)} %get-tuple-element.309), channel_id=1, source_target_pairs={{17,0},{18,1},{19,2},{20,3},{21,4},{22,5},{23,6},{24,7},{25,8},{26... | collective-permute-start | bytes 221192 | tf_op jit(solution)/shard_map/while/body/ppermute | solution.py:438
  25.4 6.3 %collective-permute-start.2 = (bf16[2,36,512]{2,1,0:T(8,128)(2,1)S(1)}, bf16[2,36,512]{2,1,0:T(8,128)(2,1)S(1)}, u32[]{:S(2)}, u32[]{:S(2)}) collective-permute-start(bf16[2,36,512]{2,1,0:T(8,128)(2,1)S(1)} %get-tuple-element.310), channel_id=1, source_target_pairs={{1,0},{2,1},{3,2},{4,3},{5,4},{6,5},{7,6},{8,7},{9,8},{10,9},{11,1... | collective-permute-start | bytes 221192 | tf_op jit(solution)/shard_map/while/body/ppermute | solution.py:441
  27.3 4.4 %collective-permute-start.3 = (bf16[2,36,512]{2,1,0:T(8,128)(2,1)S(1)}, bf16[2,36,512]{2,1,0:T(8,128)(2,1)S(1)}, u32[]{:S(2)}, u32[]{:S(2)}) collective-permute-start(bf16[2,36,512]{2,1,0:T(8,128)(2,1)S(1)} %get-tuple-element.311), channel_id=1, source_target_pairs={{16,0},{32,16},{48,32},{64,48},{80,64},{96,80},{112,96},{128,112},... | collective-permute-start | bytes 221192 | tf_op jit(solution)/shard_map/while/body/ppermute | solution.py:442
  43.8 48.6 %collective-permute-start.8 = (bf16[180,512]{1,0:T(8,128)(2,1)}, bf16[180,512]{1,0:T(8,128)(2,1)S(1)}, u32[]{:S(2)}, u32[]{:S(2)}) collective-permute-start(bf16[180,512]{1,0:T(8,128)(2,1)} %get-tuple-element.153), channel_id=1, source_target_pairs={{0,16},{16,32},{32,48},{48,64},{64,80},{80,96},{96,112},{112,128},... | collective-permute-start | bytes 552968 | tf_op jit(solution)/shard_map/ppermute | solution.py:463
  51.7 7.4 %collective-permute-start.4 = (bf16[16,2,136,128]{3,2,1,0:T(8,128)(2,1)S(1)}, bf16[16,2,136,128]{3,2,1,0:T(8,128)(2,1)S(1)}, u32[]{:S(2)}, u32[]{:S(2)}) collective-permute-start(bf16[16,2,136,128]{3,2,1,0:T(8,128)(2,1)S(1)} %get-tuple-element.328), channel_id=1, source_target_pairs={{0,1},{1,0},{2,3},{3,2},{4,5},{5,4},{6,7},{7,6},{8,9},{9,8},{10,11... | collective-permute-start | bytes 3342344 | tf_op jit(solution)/shard_map/while/body/ppermute | solution.py:467
  60.5 31.0 %all-to-all-start = ((bf16[32,136,128]{2,1,0:T(8,128)(2,1)}), bf16[32,136,128]{2,1,0:T(8,128)(2,1)S(1)}, u32[]{:S(2)}, u32[]{:S(2)}) async-start(bf16[32,136,128]{2,1,0:T(8,128)(2,1)} %pair_sum.1), calls=%async_computation | async-start | bytes 2228224 | tf_op jit(solution)/shard_map/while/body/all_to_all | solution.py:472
  92.4 24.3 %all-to-all-start.1 = ((bf16[16,72,128]{2,1,0:T(8,128)(2,1)}), bf16[16,72,128]{2,1,0:T(8,128)(2,1)S(1)}, u32[]{:S(2)}, u32[]{:S(2)}) async-start(bf16[16,72,128]{2,1,0:T(8,128)(2,1)} %get-tuple-element.154), calls=%async_computation.1 | async-start | bytes 589824 | tf_op jit(solution)/shard_map/all_to_all | solution.py:485
  102.8 12.5 %collective-permute-start.9 = (bf16[2,36,512]{2,1,0:T(8,128)(2,1)S(1)}, bf16[2,36,512]{2,1,0:T(8,128)(2,1)S(1)}, u32[]{:S(2)}, u32[]{:S(2)}) collective-permute-start(bf16[2,36,512]{2,1,0:T(8,128)(2,1)S(1)} %pad_maximum_fusion.1), channel_id=1, source_target_pairs={{0,1},{1,2},{2,3},{3,4},{4,5},{5,6},{6,7},{7,8},{8,9},{9,10},{10,1... | collective-permute-start | bytes 221192 | tf_op jit(solution)/shard_map/ppermute | solution.py:482
  117.3 11.5 %collective-permute-start.10 = (bf16[128,128]{1,0:T(8,128)(2,1)S(1)}, bf16[128,128]{1,0:T(8,128)(2,1)S(1)}, u32[]{:S(2)}, u32[]{:S(2)}) collective-permute-start(bf16[128,128]{1,0:T(8,128)(2,1)S(1)} %get-tuple-element.159.own_ref), channel_id=1, source_target_pairs={{0,1},{1,0},{2,3},{3,2},{4,5},{5,4},{6,7},{7,6},{8,9},{9,8},{10,11... | collective-permute-start | bytes 98312 | tf_op jit(solution)/shard_map/ppermute | solution.py:505

commit v5 on v4

--- a/solution.py
+++ b/solution.py
@@ -172,7 +172,7 @@
     groups = HEADS // GROUP
 
     def attention(windows):
-        @pl.loop(0, windows * groups)
+        @pl.loop(0, windows * groups, unroll=4)
         def _(step):
             window = step // groups
             attention_group(
@@ -196,7 +196,7 @@
         project(pl.ds(0, ALL_TOKENS))
         attention(TOKENS // WINDOW)
 
-        @pl.loop(0, groups)
+        @pl.loop(0, groups, unroll=4)
         def _(group):
             attention_group(
                 TOKENS, EXTRA, first == 1, group,

time: 131 us -> 129 us (0.985)
  no operation moved by 1% of the time
where the time goes in v5:
time: 129 us; the launch traced here: 128 us
  starting transfers between devices  70.2 us (54%)
  waiting for transfers between devices  33.6 us (26%)
  Pallas kernels  18.6 us (14%)
  local copies, waits for them, and re-layouts  2.86 us (2%)
  other arithmetic  2.06 us (2%)
    all_to_all x1, waiting for transfers between devices, sum_in_planes(): plane = lax.all_to_all(pair, ('y', 'x', 'zb'), 0, 0, tiled=True)  17.7 us
    ppermute x1, starting transfers between devices, fetch(): halfway = lax.ppermute(blocks, ALL, out)  14.1 us
    all_to_all x1, starting transfers between devices, sum_in_planes(): plane = lax.all_to_all(pair, ('y', 'x', 'zb'), 0, 0, tiled=True)  13.3 us
    ppermute x1, starting transfers between devices, per_device(): other_half = lax.ppermute(half, 'c', [(0, 1), (1, 0)])  10.6 us
    all_to_all x1, starting transfers between devices, per_device(): column = lax.all_to_all(plane, ALONG_Z, 0, 0, tiled=True)  10.3 us
    pallas_call x1, Pallas kernels, block(): pl.pallas_call(block_kernel, out_shape=(half(ALL_TOKENS, feature), half(5...  10.1 us
    ppermute x1, waiting for transfers between devices, per_device(): lax.ppermute(jnp.stack([drolled[252:288], back_lon[108:144]]), LAT, [(j,...  6.96 us
    ppermute x1, starting transfers between devices, per_device(): lax.ppermute(jnp.stack([drolled[252:288], back_lon[108:144]]), LAT, [(j,...  5.53 us
  transfers between devices with their start and end apart: 13, of which 7 were waited for; matrix products, arithmetic and copies ran while one was open for 2% of the time, Pallas kernels for 4%

profile of v5, /device:TPU:1, one launch (start us, length us, event | category | flops | bytes accessed | tf_op | source)
XLA Modules:
  0.0 128.2 jit_solution(18442492525491589009)
XLA Ops:
  0.6 0.0 copy-start
  0.6 1.0 copy-done
  1.6 0.0 copy-start.1
  1.6 1.0 copy-done.1
  2.6 0.0 copy-start.3
  2.6 1.1 pack.1
  3.7 14.1 %collective-permute-start.5 = (bf16[3,2,36,512]{3,2,1,0:T(8,128)(2,1)}, bf16[3,2,36,512]{3,2,1,0:T(8,128)(2,1)S(1)}, u32[]{:S(2)}, u32[]{:S(2)}) collective-permute-start(bf16[3,2,36,512]{3,2,1,0:T(8,128)(2,1)} %get-tuple-element.330), channel_id=1, source_target_pairs={{0,50},{1,319},{2,196},{3,193},{4,214},{5,211},{6,120},{7,117},{8,... | collective-permute-start | bytes 663560 | tf_op jit(solution)/shard_map/ppermute | solution.py:427
  17.8 1.3 %collective-permute-start.6 = (bf16[2,36,512]{2,1,0:T(8,128)(2,1)S(1)}, bf16[2,36,512]{2,1,0:T(8,128)(2,1)S(1)}, u32[]{:S(2)}, u32[]{:S(2)}) collective-permute-start(bf16[2,36,512]{2,1,0:T(8,128)(2,1)S(1)} %get-tuple-element.333), channel_id=1, source_target_pairs={{1,50},{2,319},{3,196},{4,193},{5,214},{6,211},{7,120},{8,117},{9,... | collective-permute-start | bytes 221192 | tf_op jit(solution)/shard_map/ppermute | solution.py:428
  19.1 1.5 %collective-permute-done.6 = bf16[2,36,512]{2,1,0:T(8,128)(2,1)S(1)} collective-permute-done((bf16[2,36,512]{2,1,0:T(8,128)(2,1)S(1)}, bf16[2,36,512]{2,1,0:T(8,128)(2,1)S(1)}, u32[]{:S(2)}, u32[]{:S(2)}) %collective-permute-start.6) | collective-permute-done | bytes 73760 | tf_op jit(solution)/shard_map/ppermute | solution.py:428
  20.6 0.7 collective-permute-done.5
  21.2 0.0 copy-start.2
  21.2 0.8 pad_maximum_fusion
  22.0 0.7 collective-permute-start.7
  22.7 0.1 pad_add_fusion.place
  22.8 0.0 copy-start.4
  22.8 9.7 %while.38 = (s32[]{:T(128)}, bf16[3,2,36,512]{3,2,1,0:T(8,128)(2,1)}, bf16[2,36,512]{2,1,0:T(8,128)(2,1)S(1)}, bf16[2,36,512]{2,1,0:T(8,128)(2,1)S(1)}, bf16[2,3...) while((s32[]{:T(128)}, bf16[3,2,36,512]{3,2,1,0:T(8,128)(2,1)}, bf16[2,36,512]{2,1,0:T(8,128)(2,1)S(1)}, ...), condition=%wide.region_1.0_spmd, body=%wide.region_0.0_spmd.sunk | while | flops 2 | bytes 2654445 | solution.py:408
  22.8 1.3 %collective-permute-start = (bf16[3,2,36,512]{3,2,1,0:T(8,128)(2,1)}, bf16[3,2,36,512]{3,2,1,0:T(8,128)(2,1)S(1)}, u32[]{:S(2)}, u32[]{:S(2)}) collective-permute-start(bf16[3,2,36,512]{3,2,1,0:T(8,128)(2,1)} %get-tuple-element.308), channel_id=1, source_target_pairs={{16,0},{32,16},{48,32},{64,48},{80,64},{96,80},{112,96},{128,112},... | collective-permute-start | bytes 663560 | tf_op jit(solution)/shard_map/while/body/ppermute | solution.py:437
  24.1 1.3 %collective-permute-start.1 = (bf16[2,36,512]{2,1,0:T(8,128)(2,1)S(1)}, bf16[2,36,512]{2,1,0:T(8,128)(2,1)S(1)}, u32[]{:S(2)}, u32[]{:S(2)}) collective-permute-start(bf16[2,36,512]{2,1,0:T(8,128)(2,1)S(1)} %get-tuple-element.309), channel_id=1, source_target_pairs={{17,0},{18,1},{19,2},{20,3},{21,4},{22,5},{23,6},{24,7},{25,8},{26... | collective-permute-start | bytes 221192 | tf_op jit(solution)/shard_map/while/body/ppermute | solution.py:438
  25.4 1.9 %collective-permute-start.2 = (bf16[2,36,512]{2,1,0:T(8,128)(2,1)S(1)}, bf16[2,36,512]{2,1,0:T(8,128)(2,1)S(1)}, u32[]{:S(2)}, u32[]{:S(2)}) collective-permute-start(bf16[2,36,512]{2,1,0:T(8,128)(2,1)S(1)} %get-tuple-element.310), channel_id=1, source_target_pairs={{1,0},{2,1},{3,2},{4,3},{5,4},{6,5},{7,6},{8,7},{9,8},{10,9},{11,1... | collective-permute-start | bytes 221192 | tf_op jit(solution)/shard_map/while/body/ppermute | solution.py:441
  27.3 0.7 collective-permute-start.3
  28.0 3.7 %collective-permute-done.1 = bf16[2,36,512]{2,1,0:T(8,128)(2,1)S(1)} collective-permute-done((bf16[2,36,512]{2,1,0:T(8,128)(2,1)S(1)}, bf16[2,36,512]{2,1,0:T(8,128)(2,1)S(1)}, u32[]{:S(2)}, u32[]{:S(2)}) %collective-permute-start.1) | collective-permute-done | bytes 73760 | tf_op jit(solution)/shard_map/while/body/ppermute | solution.py:438
  31.7 0.0 collective-permute-done.2
  31.7 0.0 collective-permute-done.3
  31.8 0.0 collective-permute-done
  31.8 0.7 copy.20
  32.5 0.0 collective-permute-done.7.crossed_ref
  32.5 0.0 copy-done.3
  32.5 0.0 copy-done.2
  32.5 0.0 copy-done.4
  32.5 10.1 %window_block.1 = (bf16[368,512]{1,0:T(8,128)(2,1)S(1)}, bf16[180,512]{1,0:T(8,128)(2,1)}, bf16[368,512]{1,0:T(8,128)(2,1)}, bf16[368,512]{1,0:T(8,128)(2,1)}, b...) custom-call(s32[4]{0:T(128)S(1)} %pad_add_fusion.place, ...), custom_call_target="tpu_custom_call" | custom-call | flops 2000000000 | bytes 6000000 | tf_op jit(solution)/shard_map/window_block/pallas_call | solution.py:218
  42.5 4.7 %collective-permute-start.8 = (bf16[180,512]{1,0:T(8,128)(2,1)}, bf16[180,512]{1,0:T(8,128)(2,1)S(1)}, u32[]{:S(2)}, u32[]{:S(2)}) collective-permute-start(bf16[180,512]{1,0:T(8,128)(2,1)} %get-tuple-element.153), channel_id=1, source_target_pairs={{0,16},{16,32},{32,48},{48,64},{64,80},{80,96},{96,112},{112,128},... | collective-permute-start | bytes 552968 | tf_op jit(solution)/shard_map/ppermute | solution.py:463
  47.2 43.4 %while.39 = (s32[]{:T(128)}, bf16[368,512]{1,0:T(8,128)(2,1)}, bf16[368,1536]{1,0:T(8,128)(2,1)}, bf16[2,512,144]{2,1,0:T(8,128)(2,1)}, bf16[512,80]{1,0:T(8,128...) while((s32[]{:T(128)}, bf16[368,512]{1,0:T(8,128)(2,1)}, ...), condition=%wide.region_3.4_spmd, body=%wide.region_2.3_spmd.sunk | while | flops 700000000 | bytes 11798965 | solution.py:408
  47.2 3.4 %weight_terms.1 = (bf16[16,2,136,128]{3,2,1,0:T(8,128)(2,1)S(1)}, bf16[16,2,136,128]{3,2,1,0:T(8,128)(2,1)S(1)}) custom-call(s32[4]{0:T(128)S(1)} %get-tuple-element.381.place, bf16[368,512]{1,0:T(8,128)(2,1)} %get-tuple-element.373.hidden_ref, bf16[368,1536]{1,0:T(8,128)(2,1)} %get-tuple-element.374.dqkv_ref, ...), custom_call_target="tpu_custom_call" | custom-call | flops 700000000 | bytes 4000000 | tf_op jit(solution)/shard_map/while/body/weight_terms/pallas_call | solution.py:284
  50.6 4.4 %collective-permute-start.4 = (bf16[16,2,136,128]{3,2,1,0:T(8,128)(2,1)S(1)}, bf16[16,2,136,128]{3,2,1,0:T(8,128)(2,1)S(1)}, u32[]{:S(2)}, u32[]{:S(2)}) collective-permute-start(bf16[16,2,136,128]{3,2,1,0:T(8,128)(2,1)S(1)} %get-tuple-element.328), channel_id=1, source_target_pairs={{0,1},{1,0},{2,3},{3,2},{4,5},{5,4},{6,7},{7,6},{8,9},{9,8},{10,11... | collective-permute-start | bytes 3342344 | tf_op jit(solution)/shard_map/while/body/ppermute | solution.py:467
  55.0 2.4 %collective-permute-done.4 = bf16[16,2,136,128]{3,2,1,0:T(8,128)(2,1)S(1)} collective-permute-done((bf16[16,2,136,128]{3,2,1,0:T(8,128)(2,1)S(1)}, bf16[16,2,136,128]{3,2,1,0:T(8,128)(2,1)S(1)}, u32[]{:S(2)}, u32[]{:S(2)}) %collective-permute-start.4) | collective-permute-done | bytes 1114144 | tf_op jit(solution)/shard_map/while/body/ppermute | solution.py:467
  57.4 1.4 %pair_sum.1 = bf16[32,136,128]{2,1,0:T(8,128)(2,1)} custom-call(bf16[32,136,128]{2,1,0:T(8,128)(2,1)S(1)} %bitcast.28, bf16[32,136,128]{2,1,0:T(8,128)(2,1)S(1)} %bitcast.29), custom_call_target="tpu_custom_call" | custom-call | tf_op jit(solution)/shard_map/while/body/pair_sum/pallas_call | solution.py:302
  58.8 13.3 %all-to-all-start = ((bf16[32,136,128]{2,1,0:T(8,128)(2,1)}), bf16[32,136,128]{2,1,0:T(8,128)(2,1)S(1)}, u32[]{:S(2)}, u32[]{:S(2)}) async-start(bf16[32,136,128]{2,1,0:T(8,128)(2,1)} %pair_sum.1), calls=%async_computation | async-start | bytes 2228224 | tf_op jit(solution)/shard_map/while/body/all_to_all | solution.py:472
  72.1 17.7 %all-to-all-done.parts_ref = bf16[32,136,128]{2,1,0:T(8,128)(2,1)S(1)} async-done(((bf16[32,136,128]{2,1,0:T(8,128)(2,1)}), bf16[32,136,128]{2,1,0:T(8,128)(2,1)S(1)}, u32[]{:S(2)}, u32[]{:S(2)}) %all-to-all-start) | async-done | bytes 1114144 | tf_op jit(solution)/shard_map/while/body/all_to_all | solution.py:472
  89.8 0.9 plane_sum.1
  90.6 0.0 collective-permute-done.8
  90.6 10.3 %all-to-all-start.1 = ((bf16[16,72,128]{2,1,0:T(8,128)(2,1)}), bf16[16,72,128]{2,1,0:T(8,128)(2,1)S(1)}, u32[]{:S(2)}, u32[]{:S(2)}) async-start(bf16[16,72,128]{2,1,0:T(8,128)(2,1)} %get-tuple-element.154), calls=%async_computation.1 | async-start | bytes 589824 | tf_op jit(solution)/shard_map/all_to_all | solution.py:485
  101.0 5.5 %collective-permute-start.9 = (bf16[2,36,512]{2,1,0:T(8,128)(2,1)S(1)}, bf16[2,36,512]{2,1,0:T(8,128)(2,1)S(1)}, u32[]{:S(2)}, u32[]{:S(2)}) collective-permute-start(bf16[2,36,512]{2,1,0:T(8,128)(2,1)S(1)} %pad_maximum_fusion.1), channel_id=1, source_target_pairs={{0,1},{1,2},{2,3},{3,4},{4,5},{5,6},{6,7},{7,8},{8,9},{9,10},{10,1... | collective-permute-start | bytes 221192 | tf_op jit(solution)/shard_map/ppermute | solution.py:482
  106.6 7.0 %collective-permute-done.9 = bf16[2,36,512]{2,1,0:T(8,128)(2,1)S(1)} collective-permute-done((bf16[2,36,512]{2,1,0:T(8,128)(2,1)S(1)}, bf16[2,36,512]{2,1,0:T(8,128)(2,1)S(1)}, u32[]{:S(2)}, u32[]{:S(2)}) %collective-permute-start.9) | collective-permute-done | bytes 73760 | tf_op jit(solution)/shard_map/ppermute | solution.py:482
  113.8 1.2 maximum_maximum_fusion
  115.0 0.0 all-to-all-done.1.parts_ref
  115.0 0.6 column_sum.1
  115.6 10.6 %collective-permute-start.10 = (bf16[128,128]{1,0:T(8,128)(2,1)S(1)}, bf16[128,128]{1,0:T(8,128)(2,1)S(1)}, u32[]{:S(2)}, u32[]{:S(2)}) collective-permute-start(bf16[128,128]{1,0:T(8,128)(2,1)S(1)} %get-tuple-element.159.own_ref), channel_id=1, source_target_pairs={{0,1},{1,0},{2,3},{3,2},{4,5},{5,4},{6,7},{7,6},{8,9},{9,8},{10,11... | collective-permute-start | bytes 98312 | tf_op jit(solution)/shard_map/ppermute | solution.py:505
  126.2 0.8 collective-permute-done.10.other_ref
  127.0 1.2 spread.1
  (16 shorter events, 0.3 us)
Async XLA Ops:
  0.6 1.0 copy-start
  1.6 1.0 copy-start.1
  2.6 29.9 %copy-start.3 = (bf16[512,512]{1,0:T(8,128)(2,1)S(1)}, bf16[512,512]{1,0:T(8,128)(2,1)}, u32[]{:S(2)}) copy-start(bf16[512,512]{1,0:T(8,128)(2,1)} %w_out_ref.1) | copy-start | bytes 1572868
  3.7 17.6 %collective-permute-start.5 = (bf16[3,2,36,512]{3,2,1,0:T(8,128)(2,1)}, bf16[3,2,36,512]{3,2,1,0:T(8,128)(2,1)S(1)}, u32[]{:S(2)}, u32[]{:S(2)}) collective-permute-start(bf16[3,2,36,512]{3,2,1,0:T(8,128)(2,1)} %get-tuple-element.330), channel_id=1, source_target_pairs={{0,50},{1,319},{2,196},{3,193},{4,214},{5,211},{6,120},{7,117},{8,... | collective-permute-start | bytes 663560 | tf_op jit(solution)/shard_map/ppermute | solution.py:427
  17.8 2.8 %collective-permute-start.6 = (bf16[2,36,512]{2,1,0:T(8,128)(2,1)S(1)}, bf16[2,36,512]{2,1,0:T(8,128)(2,1)S(1)}, u32[]{:S(2)}, u32[]{:S(2)}) collective-permute-start(bf16[2,36,512]{2,1,0:T(8,128)(2,1)S(1)} %get-tuple-element.333), channel_id=1, source_target_pairs={{1,50},{2,319},{3,196},{4,193},{5,214},{6,211},{7,120},{8,117},{9,... | collective-permute-start | bytes 221192 | tf_op jit(solution)/shard_map/ppermute | solution.py:428
  21.2 11.2 %copy-start.2 = (bf16[512,1536]{1,0:T(8,128)(2,1)S(1)}, bf16[512,1536]{1,0:T(8,128)(2,1)}, u32[]{:S(2)}) copy-start(bf16[512,1536]{1,0:T(8,128)(2,1)} %w_qkv_ref.1) | copy-start | bytes 4718596
  22.0 10.5 %collective-permute-start.7 = (bf16[4,2,36,512]{3,2,1,0:T(8,128)(2,1)}, bf16[4,2,36,512]{3,2,1,0:T(8,128)(2,1)S(1)}, u32[]{:S(2)}, u32[]{:S(2)}) collective-permute-start(bf16[4,2,36,512]{3,2,1,0:T(8,128)(2,1)} %pad_maximum_fusion), channel_id=1, source_target_pairs={{50,496},{319,497},{196,498},{193,499},{214,500},{211,501},{120,50... | collective-permute-start | bytes 884744 | tf_op jit(solution)/shard_map/ppermute | solution.py:432
  22.8 9.7 %copy-start.4 = (f32[512]{0:T(512)S(1)}, f32[512]{0:T(512)}, u32[]{:S(2)}) copy-start(f32[512]{0:T(512)} %param.11) | copy-start | bytes 6148
  22.8 8.9 %collective-permute-start = (bf16[3,2,36,512]{3,2,1,0:T(8,128)(2,1)}, bf16[3,2,36,512]{3,2,1,0:T(8,128)(2,1)S(1)}, u32[]{:S(2)}, u32[]{:S(2)}) collective-permute-start(bf16[3,2,36,512]{3,2,1,0:T(8,128)(2,1)} %get-tuple-element.308), channel_id=1, source_target_pairs={{16,0},{32,16},{48,32},{64,48},{80,64},{96,80},{112,96},{128,112},... | collective-permute-start | bytes 663560 | tf_op jit(solution)/shard_map/while/body/ppermute | solution.py:437
  24.1 7.6 %collective-permute-start.1 = (bf16[2,36,512]{2,1,0:T(8,128)(2,1)S(1)}, bf16[2,36,512]{2,1,0:T(8,128)(2,1)S(1)}, u32[]{:S(2)}, u32[]{:S(2)}) collective-permute-start(bf16[2,36,512]{2,1,0:T(8,128)(2,1)S(1)} %get-tuple-element.309), channel_id=1, source_target_pairs={{17,0},{18,1},{19,2},{20,3},{21,4},{22,5},{23,6},{24,7},{25,8},{26... | collective-permute-start | bytes 221192 | tf_op jit(solution)/shard_map/while/body/ppermute | solution.py:438
  25.4 6.3 %collective-permute-start.2 = (bf16[2,36,512]{2,1,0:T(8,128)(2,1)S(1)}, bf16[2,36,512]{2,1,0:T(8,128)(2,1)S(1)}, u32[]{:S(2)}, u32[]{:S(2)}) collective-permute-start(bf16[2,36,512]{2,1,0:T(8,128)(2,1)S(1)} %get-tuple-element.310), channel_id=1, source_target_pairs={{1,0},{2,1},{3,2},{4,3},{5,4},{6,5},{7,6},{8,7},{9,8},{10,9},{11,1... | collective-permute-start | bytes 221192 | tf_op jit(solution)/shard_map/while/body/ppermute | solution.py:441
  27.3 4.4 %collective-permute-start.3 = (bf16[2,36,512]{2,1,0:T(8,128)(2,1)S(1)}, bf16[2,36,512]{2,1,0:T(8,128)(2,1)S(1)}, u32[]{:S(2)}, u32[]{:S(2)}) collective-permute-start(bf16[2,36,512]{2,1,0:T(8,128)(2,1)S(1)} %get-tuple-element.311), channel_id=1, source_target_pairs={{16,0},{32,16},{48,32},{64,48},{80,64},{96,80},{112,96},{128,112},... | collective-permute-start | bytes 221192 | tf_op jit(solution)/shard_map/while/body/ppermute | solution.py:442
  42.5 48.1 %collective-permute-start.8 = (bf16[180,512]{1,0:T(8,128)(2,1)}, bf16[180,512]{1,0:T(8,128)(2,1)S(1)}, u32[]{:S(2)}, u32[]{:S(2)}) collective-permute-start(bf16[180,512]{1,0:T(8,128)(2,1)} %get-tuple-element.153), channel_id=1, source_target_pairs={{0,16},{16,32},{32,48},{48,64},{64,80},{80,96},{96,112},{112,128},... | collective-permute-start | bytes 552968 | tf_op jit(solution)/shard_map/ppermute | solution.py:463
  50.6 6.8 %collective-permute-start.4 = (bf16[16,2,136,128]{3,2,1,0:T(8,128)(2,1)S(1)}, bf16[16,2,136,128]{3,2,1,0:T(8,128)(2,1)S(1)}, u32[]{:S(2)}, u32[]{:S(2)}) collective-permute-start(bf16[16,2,136,128]{3,2,1,0:T(8,128)(2,1)S(1)} %get-tuple-element.328), channel_id=1, source_target_pairs={{0,1},{1,0},{2,3},{3,2},{4,5},{5,4},{6,7},{7,6},{8,9},{9,8},{10,11... | collective-permute-start | bytes 3342344 | tf_op jit(solution)/shard_map/while/body/ppermute | solution.py:467
  58.8 31.0 %all-to-all-start = ((bf16[32,136,128]{2,1,0:T(8,128)(2,1)}), bf16[32,136,128]{2,1,0:T(8,128)(2,1)S(1)}, u32[]{:S(2)}, u32[]{:S(2)}) async-start(bf16[32,136,128]{2,1,0:T(8,128)(2,1)} %pair_sum.1), calls=%async_computation | async-start | bytes 2228224 | tf_op jit(solution)/shard_map/while/body/all_to_all | solution.py:472
  90.6 24.3 %all-to-all-start.1 = ((bf16[16,72,128]{2,1,0:T(8,128)(2,1)}), bf16[16,72,128]{2,1,0:T(8,128)(2,1)S(1)}, u32[]{:S(2)}, u32[]{:S(2)}) async-start(bf16[16,72,128]{2,1,0:T(8,128)(2,1)} %get-tuple-element.154), calls=%async_computation.1 | async-start | bytes 589824 | tf_op jit(solution)/shard_map/all_to_all | solution.py:485
  101.0 12.5 %collective-permute-start.9 = (bf16[2,36,512]{2,1,0:T(8,128)(2,1)S(1)}, bf16[2,36,512]{2,1,0:T(8,128)(2,1)S(1)}, u32[]{:S(2)}, u32[]{:S(2)}) collective-permute-start(bf16[2,36,512]{2,1,0:T(8,128)(2,1)S(1)} %pad_maximum_fusion.1), channel_id=1, source_target_pairs={{0,1},{1,2},{2,3},{3,4},{4,5},{5,6},{6,7},{7,8},{8,9},{9,10},{10,1... | collective-permute-start | bytes 221192 | tf_op jit(solution)/shard_map/ppermute | solution.py:482
  115.6 11.5 %collective-permute-start.10 = (bf16[128,128]{1,0:T(8,128)(2,1)S(1)}, bf16[128,128]{1,0:T(8,128)(2,1)S(1)}, u32[]{:S(2)}, u32[]{:S(2)}) collective-permute-start(bf16[128,128]{1,0:T(8,128)(2,1)S(1)} %get-tuple-element.159.own_ref), channel_id=1, source_target_pairs={{0,1},{1,0},{2,3},{3,2},{4,5},{5,4},{6,7},{7,6},{8,9},{9,8},{10,11... | collective-permute-start | bytes 98312 | tf_op jit(solution)/shard_map/ppermute | solution.py:505

commit v6 on v5

--- a/solution.py
+++ b/solution.py
@@ -172,7 +172,7 @@
     groups = HEADS // GROUP
 
     def attention(windows):
-        @pl.loop(0, windows * groups, unroll=4)
+        @pl.loop(0, windows * groups, unroll=8)
         def _(step):
             window = step // groups
             attention_group(
@@ -242,56 +242,53 @@
 
 
 def weights_kernel(
-    place, hidden_ref, dqkv_ref, attended_ref, attended_extra_ref, dy_ref, gain_tile_ref,
-    keep_ref, send_ref, total_ref,
+    kept, place, hidden_ref, dqkv_ref, attended_ref, attended_extra_ref, dy_ref, gain_tile_ref,
+    dealt_ref, total_ref,
 ):
-    core = place[2]
     feature = HEADS * HEAD_DIM
-    total_ref[:, 0 : 3 * feature] = tn(hidden_ref[...], dqkv_ref[...]).astype(BF16)
-    out_total = nn(attended_extra_ref[...], dy_ref[TOKENS:, :])
-    for window in range(TOKENS // WINDOW):
-        rows = slice(window * WINDOW, (window + 1) * WINDOW)
-        out_total = out_total + nn(attended_ref[window], dy_ref[rows, :])
-    total_ref[:, 3 * feature :] = out_total.astype(BF16)
+    half = place[2] if kept else 1 - place[2]
+
+    @pl.when(half == 0)
+    def _():
+        total_ref[...] = tn(hidden_ref[...], dqkv_ref[:, 0 : 2 * feature]).astype(BF16)
+
+    @pl.when(half == 1)
+    def _():
+        total_ref[:, 0:feature] = tn(hidden_ref[...], dqkv_ref[:, 2 * feature :]).astype(BF16)
+        out_total = nn(attended_extra_ref[...], dy_ref[TOKENS:, :])
+        for window in range(TOKENS // WINDOW):
+            rows = slice(window * WINDOW, (window + 1) * WINDOW)
+            out_total = out_total + nn(attended_ref[window], dy_ref[rows, :])
+        total_ref[:, feature:] = out_total.astype(BF16)
+
     for lon in range(16):
-        for ref in (keep_ref, send_ref):
-            ref[lon, 0, 128:136] = gain_tile_ref[...]
-            ref[lon, 1, 128:136] = gain_tile_ref[...]
-
-    def deal(halves):
-        @pl.loop(0, 16)
-        def _(lon):
-            for zh in range(2):
-                start = pl.multiple_of(zh * 256 + lon * 16, 16)
-                rows = total_ref[pl.ds(start, 16), :]
-                for j in range(16):
-                    tile = (zh * 4 + j % 4) * 16
-                    halves[j // 8][lon, j % 8 // 4, tile : tile + 16] = rows[:, 128 * j : 128 * (j + 1)]
-
-    @pl.when(core == 0)
-    def _():
-        deal((keep_ref, send_ref))
-
-    @pl.when(core == 1)
-    def _():
-        deal((send_ref, keep_ref))
-
-
-def weight_terms(place, *operands):
+        dealt_ref[lon, 0, 128:136] = gain_tile_ref[...]
+        dealt_ref[lon, 1, 128:136] = gain_tile_ref[...]
+
+    @pl.loop(0, 16)
+    def _(lon):
+        for zh in range(2):
+            start = pl.multiple_of(zh * 256 + lon * 16, 16)
+            rows = total_ref[pl.ds(start, 16), :]
+            for j in range(8):
+                tile = (zh * 4 + j % 4) * 16
+                dealt_ref[lon, j // 4, tile : tile + 16] = rows[:, 128 * j : 128 * (j + 1)]
+
+
+def weight_terms(kept, place, *operands):
     feature = HEADS * HEAD_DIM
     vmem = pl.BlockSpec(memory_space=pltpu.VMEM)
-    dealt = jax.ShapeDtypeStruct((16, 2, 136, 128), BF16)
     return pl.pallas_call(
-        weights_kernel,
-        out_shape=(dealt, dealt),
+        functools.partial(weights_kernel, kept),
+        out_shape=jax.ShapeDtypeStruct((16, 2, 136, 128), BF16),
         in_specs=[pl.BlockSpec(memory_space=pltpu.SMEM)] + [vmem] * len(operands),
-        out_specs=(vmem, vmem),
-        scratch_shapes=[pltpu.VMEM((feature, 4 * feature), BF16)],
+        out_specs=vmem,
+        scratch_shapes=[pltpu.VMEM((feature, 2 * feature), BF16)],
         compiler_params=pltpu.CompilerParams(vmem_limit_bytes=40 * 1024 * 1024),
         cost_estimate=pl.CostEstimate(
-            flops=700_000_000, bytes_accessed=4_000_000, transcendentals=0
+            flops=2_000_000_000, bytes_accessed=8_000_000, transcendentals=0
         ),
-        name="weight_terms",
+        name="kept_terms" if kept else "sent_terms",
     )(place, *operands)
 
 
@@ -463,8 +460,9 @@
     back_lon = lax.ppermute(back, LON, [(i, (i + 1) % 32) for i in range(32)])
 
     def sum_in_planes(*operands):
-        keep, send = weight_terms(place, *operands[:-1])
+        send = weight_terms(False, place, *operands[:-1])
         other = lax.ppermute(send, "c", [(0, 1), (1, 0)])
+        keep = weight_terms(True, place, *operands[:-1])
         pair = small_call(
             pair_kernel, "pair_sum", jax.ShapeDtypeStruct((32, 136, 128), BF16),
             keep.reshape(32, 136, 128), other.reshape(32, 136, 128),

time: 129 us -> 128 us (level)
  waiting for transfers between devices: 33.6 us -> 31.9 us
    ppermute x1, waiting for transfers between devices: 2.36 us -> 0.66 us  [sum_in_planes(): other = lax.ppermute(send, 'c', [(0, 1), (1, 0)])]
    pallas_call x1 -> x2, Pallas kernels: 3.37 us -> 4.39 us  [weight_terms(): pl.pallas_call(functools.partial(weights_kernel, kept), out_shape=jax.Sha...]
  transfers between devices with their start and end apart: 13 -> 13, of which waited for: 7 -> 7; matrix products, arithmetic and copies ran while one was open for 2% -> 2% of each run, Pallas kernels for 4% -> 5%
where the time goes in v6:
time: 128 us; the launch traced here: 127 us
  starting transfers between devices  70.2 us (55%)
  waiting for transfers between devices  31.9 us (25%)
  Pallas kernels  19.2 us (15%)
  local copies, waits for them, and re-layouts  2.88 us (2%)
  other arithmetic  2.06 us (2%)
    all_to_all x1, waiting for transfers between devices, sum_in_planes(): plane = lax.all_to_all(pair, ('y', 'x', 'zb'), 0, 0, tiled=True)  17.7 us
    ppermute x1, starting transfers between devices, fetch(): halfway = lax.ppermute(blocks, ALL, out)  14.1 us
    all_to_all x1, starting transfers between devices, sum_in_planes(): plane = lax.all_to_all(pair, ('y', 'x', 'zb'), 0, 0, tiled=True)  13.4 us
    ppermute x1, starting transfers between devices, per_device(): other_half = lax.ppermute(half, 'c', [(0, 1), (1, 0)])  10.6 us
    all_to_all x1, starting transfers between devices, per_device(): column = lax.all_to_all(plane, ALONG_Z, 0, 0, tiled=True)  10.3 us
    pallas_call x1, Pallas kernels, block(): pl.pallas_call(block_kernel, out_shape=(half(ALL_TOKENS, feature), half(5...  9.66 us
    ppermute x1, waiting for transfers between devices, per_device(): lax.ppermute(jnp.stack([drolled[252:288], back_lon[108:144]]), LAT, [(j,...  6.96 us
    ppermute x1, starting transfers between devices, per_device(): lax.ppermute(jnp.stack([drolled[252:288], back_lon[108:144]]), LAT, [(j,...  5.53 us
  transfers between devices with their start and end apart: 13, of which 7 were waited for; matrix products, arithmetic and copies ran while one was open for 2% of the time, Pallas kernels for 5%

profile of v6, /device:TPU:1, one launch (start us, length us, event | category | flops | bytes accessed | tf_op | source)
XLA Modules:
  0.0 127.3 jit_solution(11515829802300931171)
XLA Ops:
  0.6 0.0 copy-start
  0.6 1.0 copy-done
  1.6 0.0 copy-start.1
  1.6 1.0 copy-done.1
  2.6 0.0 copy-start.3
  2.6 1.1 pack.1
  3.7 14.1 %collective-permute-start.5 = (bf16[3,2,36,512]{3,2,1,0:T(8,128)(2,1)}, bf16[3,2,36,512]{3,2,1,0:T(8,128)(2,1)S(1)}, u32[]{:S(2)}, u32[]{:S(2)}) collective-permute-start(bf16[3,2,36,512]{3,2,1,0:T(8,128)(2,1)} %get-tuple-element.324), channel_id=1, source_target_pairs={{0,50},{1,319},{2,196},{3,193},{4,214},{5,211},{6,120},{7,117},{8,... | collective-permute-start | bytes 663560 | tf_op jit(solution)/shard_map/ppermute | solution.py:424
  17.8 1.3 %collective-permute-start.6 = (bf16[2,36,512]{2,1,0:T(8,128)(2,1)S(1)}, bf16[2,36,512]{2,1,0:T(8,128)(2,1)S(1)}, u32[]{:S(2)}, u32[]{:S(2)}) collective-permute-start(bf16[2,36,512]{2,1,0:T(8,128)(2,1)S(1)} %get-tuple-element.327), channel_id=1, source_target_pairs={{1,50},{2,319},{3,196},{4,193},{5,214},{6,211},{7,120},{8,117},{9,... | collective-permute-start | bytes 221192 | tf_op jit(solution)/shard_map/ppermute | solution.py:425
  19.1 1.5 %collective-permute-done.6 = bf16[2,36,512]{2,1,0:T(8,128)(2,1)S(1)} collective-permute-done((bf16[2,36,512]{2,1,0:T(8,128)(2,1)S(1)}, bf16[2,36,512]{2,1,0:T(8,128)(2,1)S(1)}, u32[]{:S(2)}, u32[]{:S(2)}) %collective-permute-start.6) | collective-permute-done | bytes 73760 | tf_op jit(solution)/shard_map/ppermute | solution.py:425
  20.6 0.7 collective-permute-done.5
  21.2 0.0 copy-start.2
  21.2 0.8 pad_maximum_fusion
  22.0 0.7 collective-permute-start.7
  22.7 0.1 pad_add_fusion.place
  22.8 0.0 copy-start.4
  22.8 9.7 %while.38 = (s32[]{:T(128)}, bf16[3,2,36,512]{3,2,1,0:T(8,128)(2,1)}, bf16[2,36,512]{2,1,0:T(8,128)(2,1)S(1)}, bf16[2,36,512]{2,1,0:T(8,128)(2,1)S(1)}, bf16[2,3...) while((s32[]{:T(128)}, bf16[3,2,36,512]{3,2,1,0:T(8,128)(2,1)}, bf16[2,36,512]{2,1,0:T(8,128)(2,1)S(1)}, ...), condition=%wide.region_1.0_spmd, body=%wide.region_0.0_spmd.sunk | while | flops 2 | bytes 2654445 | solution.py:405
  22.8 1.3 %collective-permute-start = (bf16[3,2,36,512]{3,2,1,0:T(8,128)(2,1)}, bf16[3,2,36,512]{3,2,1,0:T(8,128)(2,1)S(1)}, u32[]{:S(2)}, u32[]{:S(2)}) collective-permute-start(bf16[3,2,36,512]{3,2,1,0:T(8,128)(2,1)} %get-tuple-element.304), channel_id=1, source_target_pairs={{16,0},{32,16},{48,32},{64,48},{80,64},{96,80},{112,96},{128,112},... | collective-permute-start | bytes 663560 | tf_op jit(solution)/shard_map/while/body/ppermute | solution.py:434
  24.1 1.3 %collective-permute-start.1 = (bf16[2,36,512]{2,1,0:T(8,128)(2,1)S(1)}, bf16[2,36,512]{2,1,0:T(8,128)(2,1)S(1)}, u32[]{:S(2)}, u32[]{:S(2)}) collective-permute-start(bf16[2,36,512]{2,1,0:T(8,128)(2,1)S(1)} %get-tuple-element.305), channel_id=1, source_target_pairs={{17,0},{18,1},{19,2},{20,3},{21,4},{22,5},{23,6},{24,7},{25,8},{26... | collective-permute-start | bytes 221192 | tf_op jit(solution)/shard_map/while/body/ppermute | solution.py:435
  25.4 1.9 %collective-permute-start.2 = (bf16[2,36,512]{2,1,0:T(8,128)(2,1)S(1)}, bf16[2,36,512]{2,1,0:T(8,128)(2,1)S(1)}, u32[]{:S(2)}, u32[]{:S(2)}) collective-permute-start(bf16[2,36,512]{2,1,0:T(8,128)(2,1)S(1)} %get-tuple-element.306), channel_id=1, source_target_pairs={{1,0},{2,1},{3,2},{4,3},{5,4},{6,5},{7,6},{8,7},{9,8},{10,9},{11,1... | collective-permute-start | bytes 221192 | tf_op jit(solution)/shard_map/while/body/ppermute | solution.py:438
  27.3 0.7 collective-permute-start.3
  28.0 3.7 %collective-permute-done.1 = bf16[2,36,512]{2,1,0:T(8,128)(2,1)S(1)} collective-permute-done((bf16[2,36,512]{2,1,0:T(8,128)(2,1)S(1)}, bf16[2,36,512]{2,1,0:T(8,128)(2,1)S(1)}, u32[]{:S(2)}, u32[]{:S(2)}) %collective-permute-start.1) | collective-permute-done | bytes 73760 | tf_op jit(solution)/shard_map/while/body/ppermute | solution.py:435
  31.7 0.0 collective-permute-done.2
  31.7 0.0 collective-permute-done.3
  31.7 0.0 collective-permute-done
  31.8 0.7 copy.20
  32.5 0.0 collective-permute-done.7.crossed_ref
  32.5 0.0 copy-done.3
  32.5 0.0 copy-done.2
  32.5 0.0 copy-done.4
  32.5 9.7 %window_block.1 = (bf16[368,512]{1,0:T(8,128)(2,1)S(1)}, bf16[180,512]{1,0:T(8,128)(2,1)}, bf16[368,512]{1,0:T(8,128)(2,1)}, bf16[368,512]{1,0:T(8,128)(2,1)}, b...) custom-call(s32[4]{0:T(128)S(1)} %pad_add_fusion.place, ...), custom_call_target="tpu_custom_call" | custom-call | flops 2000000000 | bytes 6000000 | tf_op jit(solution)/shard_map/window_block/pallas_call | solution.py:218
  42.1 4.5 %collective-permute-start.8 = (bf16[180,512]{1,0:T(8,128)(2,1)}, bf16[180,512]{1,0:T(8,128)(2,1)S(1)}, u32[]{:S(2)}, u32[]{:S(2)}) collective-permute-start(bf16[180,512]{1,0:T(8,128)(2,1)} %get-tuple-element.151), channel_id=1, source_target_pairs={{0,16},{16,32},{32,48},{48,64},{64,80},{80,96},{96,112},{112,128},... | collective-permute-start | bytes 552968 | tf_op jit(solution)/shard_map/ppermute | solution.py:460
  46.7 43.0 %while.39 = (s32[]{:T(128)}, bf16[368,512]{1,0:T(8,128)(2,1)}, bf16[368,1536]{1,0:T(8,128)(2,1)}, bf16[2,512,144]{2,1,0:T(8,128)(2,1)}, bf16[512,80]{1,0:T(8,128...) while((s32[]{:T(128)}, bf16[368,512]{1,0:T(8,128)(2,1)}, ...), condition=%wide.region_3.4_spmd, body=%wide.region_2.3_spmd.sunk | while | flops 4000000000 | bytes 32515364 | solution.py:405
  46.7 0.0 copy-start.5
  46.7 0.0 copy-start.6
  46.7 0.0 copy-start.7
  46.7 0.0 copy-start.8
  46.7 2.7 %sent_terms.1 = bf16[16,2,136,128]{3,2,1,0:T(8,128)(2,1)S(1)} custom-call(s32[4]{0:T(128)S(1)} %get-tuple-element.375.place, bf16[368,512]{1,0:T(8,128)(2,1)} %get-tuple-element.367.hidden_ref, bf16[368,1536]{1,0:T(8,128)(2,1)} %get-tuple-element.368.dqkv_ref, bf16[2,512,144]{2,1,0:T(8,128)(2,1)} %get-tuple-element.369.attended_ref, ...), custom_call_target="tpu_custom_call" | custom-call | flops 2000000000 | bytes 8000000 | tf_op jit(solution)/shard_map/while/body/sent_terms/pallas_call | solution.py:281
  49.5 4.6 %collective-permute-start.4 = (bf16[16,2,136,128]{3,2,1,0:T(8,128)(2,1)S(1)}, bf16[16,2,136,128]{3,2,1,0:T(8,128)(2,1)S(1)}, u32[]{:S(2)}, u32[]{:S(2)}) collective-permute-start(bf16[16,2,136,128]{3,2,1,0:T(8,128)(2,1)S(1)} %sent_terms.1), channel_id=1, source_target_pairs={{0,1},{1,0},{2,3},{3,2},{4,5},{5,4},{6,7},{7,6},{8,9},{9,8},{10,11... | collective-permute-start | bytes 3342344 | tf_op jit(solution)/shard_map/while/body/ppermute | solution.py:464
  54.0 0.0 copy-done.5
  54.0 0.0 copy-done.6
  54.0 0.0 copy-done.7
  54.1 0.0 copy-done.8
  54.1 1.7 %kept_terms.1 = bf16[16,2,136,128]{3,2,1,0:T(8,128)(2,1)S(1)} custom-call(s32[4]{0:T(128)S(1)} %get-tuple-element.375.place, bf16[368,512]{1,0:T(8,128)(2,1)S(1)} %copy-done.8, bf16[368,1536]{1,0:T(8,128)(2,1)S(1)} %copy-done.5, bf16[2,512,144]{2,1,0:T(8,128)(2,1)S(1)} %copy-done.6, bf16[512,80]{1,0:T(8,128)(2,1)S(1)} %get-tuple-element.370.attended_extra_ref, ...), custom_call_target="tpu_custom_call" | custom-call | flops 2000000000 | bytes 8000000 | tf_op jit(solution)/shard_map/while/body/kept_terms/pallas_call | solution.py:281
  55.7 0.7 collective-permute-done.4
  56.4 1.4 %pair_sum.1 = bf16[32,136,128]{2,1,0:T(8,128)(2,1)} custom-call(bf16[32,136,128]{2,1,0:T(8,128)(2,1)S(1)} %bitcast.29, bf16[32,136,128]{2,1,0:T(8,128)(2,1)S(1)} %bitcast.28), custom_call_target="tpu_custom_call" | custom-call | tf_op jit(solution)/shard_map/while/body/pair_sum/pallas_call | solution.py:299
  57.8 13.4 %all-to-all-start = ((bf16[32,136,128]{2,1,0:T(8,128)(2,1)}), bf16[32,136,128]{2,1,0:T(8,128)(2,1)S(1)}, u32[]{:S(2)}, u32[]{:S(2)}) async-start(bf16[32,136,128]{2,1,0:T(8,128)(2,1)} %pair_sum.1), calls=%async_computation | async-start | bytes 2228224 | tf_op jit(solution)/shard_map/while/body/all_to_all | solution.py:470
  71.1 17.7 %all-to-all-done.parts_ref = bf16[32,136,128]{2,1,0:T(8,128)(2,1)S(1)} async-done(((bf16[32,136,128]{2,1,0:T(8,128)(2,1)}), bf16[32,136,128]{2,1,0:T(8,128)(2,1)S(1)}, u32[]{:S(2)}, u32[]{:S(2)}) %all-to-all-start) | async-done | bytes 1114144 | tf_op jit(solution)/shard_map/while/body/all_to_all | solution.py:470
  88.8 0.9 plane_sum.1
  89.7 0.0 collective-permute-done.8
  89.7 10.3 %all-to-all-start.1 = ((bf16[16,72,128]{2,1,0:T(8,128)(2,1)}), bf16[16,72,128]{2,1,0:T(8,128)(2,1)S(1)}, u32[]{:S(2)}, u32[]{:S(2)}) async-start(bf16[16,72,128]{2,1,0:T(8,128)(2,1)} %get-tuple-element.152), calls=%async_computation.1 | async-start | bytes 589824 | tf_op jit(solution)/shard_map/all_to_all | solution.py:483
  100.1 5.5 %collective-permute-start.9 = (bf16[2,36,512]{2,1,0:T(8,128)(2,1)S(1)}, bf16[2,36,512]{2,1,0:T(8,128)(2,1)S(1)}, u32[]{:S(2)}, u32[]{:S(2)}) collective-permute-start(bf16[2,36,512]{2,1,0:T(8,128)(2,1)S(1)} %pad_maximum_fusion.1), channel_id=1, source_target_pairs={{0,1},{1,2},{2,3},{3,4},{4,5},{5,6},{6,7},{7,8},{8,9},{9,10},{10,1... | collective-permute-start | bytes 221192 | tf_op jit(solution)/shard_map/ppermute | solution.py:480
  105.6 7.0 %collective-permute-done.9 = bf16[2,36,512]{2,1,0:T(8,128)(2,1)S(1)} collective-permute-done((bf16[2,36,512]{2,1,0:T(8,128)(2,1)S(1)}, bf16[2,36,512]{2,1,0:T(8,128)(2,1)S(1)}, u32[]{:S(2)}, u32[]{:S(2)}) %collective-permute-start.9) | collective-permute-done | bytes 73760 | tf_op jit(solution)/shard_map/ppermute | solution.py:480
  112.8 1.2 maximum_maximum_fusion
  114.0 0.0 all-to-all-done.1.parts_ref
  114.0 0.6 column_sum.1
  114.6 10.6 %collective-permute-start.10 = (bf16[128,128]{1,0:T(8,128)(2,1)S(1)}, bf16[128,128]{1,0:T(8,128)(2,1)S(1)}, u32[]{:S(2)}, u32[]{:S(2)}) collective-permute-start(bf16[128,128]{1,0:T(8,128)(2,1)S(1)} %get-tuple-element.157.own_ref), channel_id=1, source_target_pairs={{0,1},{1,0},{2,3},{3,2},{4,5},{5,4},{6,7},{7,6},{8,9},{9,8},{10,11... | collective-permute-start | bytes 98312 | tf_op jit(solution)/shard_map/ppermute | solution.py:503
  125.2 0.8 collective-permute-done.10.other_ref
  126.1 1.2 spread.1
  (16 shorter events, 0.3 us)
Async XLA Ops:
  0.6 1.0 copy-start
  1.6 1.0 copy-start.1
  2.6 29.9 %copy-start.3 = (bf16[512,512]{1,0:T(8,128)(2,1)S(1)}, bf16[512,512]{1,0:T(8,128)(2,1)}, u32[]{:S(2)}) copy-start(bf16[512,512]{1,0:T(8,128)(2,1)} %w_out_ref.1) | copy-start | bytes 1572868
  3.7 17.6 %collective-permute-start.5 = (bf16[3,2,36,512]{3,2,1,0:T(8,128)(2,1)}, bf16[3,2,36,512]{3,2,1,0:T(8,128)(2,1)S(1)}, u32[]{:S(2)}, u32[]{:S(2)}) collective-permute-start(bf16[3,2,36,512]{3,2,1,0:T(8,128)(2,1)} %get-tuple-element.324), channel_id=1, source_target_pairs={{0,50},{1,319},{2,196},{3,193},{4,214},{5,211},{6,120},{7,117},{8,... | collective-permute-start | bytes 663560 | tf_op jit(solution)/shard_map/ppermute | solution.py:424
  17.8 2.8 %collective-permute-start.6 = (bf16[2,36,512]{2,1,0:T(8,128)(2,1)S(1)}, bf16[2,36,512]{2,1,0:T(8,128)(2,1)S(1)}, u32[]{:S(2)}, u32[]{:S(2)}) collective-permute-start(bf16[2,36,512]{2,1,0:T(8,128)(2,1)S(1)} %get-tuple-element.327), channel_id=1, source_target_pairs={{1,50},{2,319},{3,196},{4,193},{5,214},{6,211},{7,120},{8,117},{9,... | collective-permute-start | bytes 221192 | tf_op jit(solution)/shard_map/ppermute | solution.py:425
  21.2 11.2 %copy-start.2 = (bf16[512,1536]{1,0:T(8,128)(2,1)S(1)}, bf16[512,1536]{1,0:T(8,128)(2,1)}, u32[]{:S(2)}) copy-start(bf16[512,1536]{1,0:T(8,128)(2,1)} %w_qkv_ref.1) | copy-start | bytes 4718596
  22.0 10.5 %collective-permute-start.7 = (bf16[4,2,36,512]{3,2,1,0:T(8,128)(2,1)}, bf16[4,2,36,512]{3,2,1,0:T(8,128)(2,1)S(1)}, u32[]{:S(2)}, u32[]{:S(2)}) collective-permute-start(bf16[4,2,36,512]{3,2,1,0:T(8,128)(2,1)} %pad_maximum_fusion), channel_id=1, source_target_pairs={{50,496},{319,497},{196,498},{193,499},{214,500},{211,501},{120,50... | collective-permute-start | bytes 884744 | tf_op jit(solution)/shard_map/ppermute | solution.py:429
  22.8 9.7 %copy-start.4 = (f32[512]{0:T(512)S(1)}, f32[512]{0:T(512)}, u32[]{:S(2)}) copy-start(f32[512]{0:T(512)} %param.11) | copy-start | bytes 6148
  22.8 8.9 %collective-permute-start = (bf16[3,2,36,512]{3,2,1,0:T(8,128)(2,1)}, bf16[3,2,36,512]{3,2,1,0:T(8,128)(2,1)S(1)}, u32[]{:S(2)}, u32[]{:S(2)}) collective-permute-start(bf16[3,2,36,512]{3,2,1,0:T(8,128)(2,1)} %get-tuple-element.304), channel_id=1, source_target_pairs={{16,0},{32,16},{48,32},{64,48},{80,64},{96,80},{112,96},{128,112},... | collective-permute-start | bytes 663560 | tf_op jit(solution)/shard_map/while/body/ppermute | solution.py:434
  24.1 7.6 %collective-permute-start.1 = (bf16[2,36,512]{2,1,0:T(8,128)(2,1)S(1)}, bf16[2,36,512]{2,1,0:T(8,128)(2,1)S(1)}, u32[]{:S(2)}, u32[]{:S(2)}) collective-permute-start(bf16[2,36,512]{2,1,0:T(8,128)(2,1)S(1)} %get-tuple-element.305), channel_id=1, source_target_pairs={{17,0},{18,1},{19,2},{20,3},{21,4},{22,5},{23,6},{24,7},{25,8},{26... | collective-permute-start | bytes 221192 | tf_op jit(solution)/shard_map/while/body/ppermute | solution.py:435
  25.4 6.3 %collective-permute-start.2 = (bf16[2,36,512]{2,1,0:T(8,128)(2,1)S(1)}, bf16[2,36,512]{2,1,0:T(8,128)(2,1)S(1)}, u32[]{:S(2)}, u32[]{:S(2)}) collective-permute-start(bf16[2,36,512]{2,1,0:T(8,128)(2,1)S(1)} %get-tuple-element.306), channel_id=1, source_target_pairs={{1,0},{2,1},{3,2},{4,3},{5,4},{6,5},{7,6},{8,7},{9,8},{10,9},{11,1... | collective-permute-start | bytes 221192 | tf_op jit(solution)/shard_map/while/body/ppermute | solution.py:438
  27.3 4.4 %collective-permute-start.3 = (bf16[2,36,512]{2,1,0:T(8,128)(2,1)S(1)}, bf16[2,36,512]{2,1,0:T(8,128)(2,1)S(1)}, u32[]{:S(2)}, u32[]{:S(2)}) collective-permute-start(bf16[2,36,512]{2,1,0:T(8,128)(2,1)S(1)} %get-tuple-element.307), channel_id=1, source_target_pairs={{16,0},{32,16},{48,32},{64,48},{80,64},{96,80},{112,96},{128,112},... | collective-permute-start | bytes 221192 | tf_op jit(solution)/shard_map/while/body/ppermute | solution.py:439
  42.1 47.6 %collective-permute-start.8 = (bf16[180,512]{1,0:T(8,128)(2,1)}, bf16[180,512]{1,0:T(8,128)(2,1)S(1)}, u32[]{:S(2)}, u32[]{:S(2)}) collective-permute-start(bf16[180,512]{1,0:T(8,128)(2,1)} %get-tuple-element.151), channel_id=1, source_target_pairs={{0,16},{16,32},{32,48},{48,64},{64,80},{80,96},{96,112},{112,128},... | collective-permute-start | bytes 552968 | tf_op jit(solution)/shard_map/ppermute | solution.py:460
  46.7 7.4 %copy-start.5 = (bf16[368,1536]{1,0:T(8,128)(2,1)S(1)}, bf16[368,1536]{1,0:T(8,128)(2,1)}, u32[]{:S(2)}) copy-start(bf16[368,1536]{1,0:T(8,128)(2,1)} %get-tuple-element.368.dqkv_ref) | copy-start | bytes 3391492 | tf_op jit(solution)/shard_map/while
  46.7 7.4 %copy-start.6 = (bf16[2,512,144]{2,1,0:T(8,128)(2,1)S(1)}, bf16[2,512,144]{2,1,0:T(8,128)(2,1)}, u32[]{:S(2)}) copy-start(bf16[2,512,144]{2,1,0:T(8,128)(2,1)} %get-tuple-element.369.attended_ref) | copy-start | bytes 884740 | tf_op jit(solution)/shard_map/while
  46.7 7.4 %copy-start.7 = (bf16[368,512]{1,0:T(8,128)(2,1)S(1)}, bf16[368,512]{1,0:T(8,128)(2,1)}, u32[]{:S(2)}) copy-start(bf16[368,512]{1,0:T(8,128)(2,1)} %get-tuple-element.371.dy_ref) | copy-start | bytes 1130500 | tf_op jit(solution)/shard_map/while
  46.7 7.4 %copy-start.8 = (bf16[368,512]{1,0:T(8,128)(2,1)S(1)}, bf16[368,512]{1,0:T(8,128)(2,1)}, u32[]{:S(2)}) copy-start(bf16[368,512]{1,0:T(8,128)(2,1)} %get-tuple-element.367.hidden_ref) | copy-start | bytes 1130500 | tf_op jit(solution)/shard_map/while
  49.5 6.9 %collective-permute-start.4 = (bf16[16,2,136,128]{3,2,1,0:T(8,128)(2,1)S(1)}, bf16[16,2,136,128]{3,2,1,0:T(8,128)(2,1)S(1)}, u32[]{:S(2)}, u32[]{:S(2)}) collective-permute-start(bf16[16,2,136,128]{3,2,1,0:T(8,128)(2,1)S(1)} %sent_terms.1), channel_id=1, source_target_pairs={{0,1},{1,0},{2,3},{3,2},{4,5},{5,4},{6,7},{7,6},{8,9},{9,8},{10,11... | collective-permute-start | bytes 3342344 | tf_op jit(solution)/shard_map/while/body/ppermute | solution.py:464
  57.8 31.0 %all-to-all-start = ((bf16[32,136,128]{2,1,0:T(8,128)(2,1)}), bf16[32,136,128]{2,1,0:T(8,128)(2,1)S(1)}, u32[]{:S(2)}, u32[]{:S(2)}) async-start(bf16[32,136,128]{2,1,0:T(8,128)(2,1)} %pair_sum.1), calls=%async_computation | async-start | bytes 2228224 | tf_op jit(solution)/shard_map/while/body/all_to_all | solution.py:470
  89.7 24.3 %all-to-all-start.1 = ((bf16[16,72,128]{2,1,0:T(8,128)(2,1)}), bf16[16,72,128]{2,1,0:T(8,128)(2,1)S(1)}, u32[]{:S(2)}, u32[]{:S(2)}) async-start(bf16[16,72,128]{2,1,0:T(8,128)(2,1)} %get-tuple-element.152), calls=%async_computation.1 | async-start | bytes 589824 | tf_op jit(solution)/shard_map/all_to_all | solution.py:483
  100.1 12.5 %collective-permute-start.9 = (bf16[2,36,512]{2,1,0:T(8,128)(2,1)S(1)}, bf16[2,36,512]{2,1,0:T(8,128)(2,1)S(1)}, u32[]{:S(2)}, u32[]{:S(2)}) collective-permute-start(bf16[2,36,512]{2,1,0:T(8,128)(2,1)S(1)} %pad_maximum_fusion.1), channel_id=1, source_target_pairs={{0,1},{1,2},{2,3},{3,4},{4,5},{5,6},{6,7},{7,8},{8,9},{9,10},{10,1... | collective-permute-start | bytes 221192 | tf_op jit(solution)/shard_map/ppermute | solution.py:480
  114.6 11.5 %collective-permute-start.10 = (bf16[128,128]{1,0:T(8,128)(2,1)S(1)}, bf16[128,128]{1,0:T(8,128)(2,1)S(1)}, u32[]{:S(2)}, u32[]{:S(2)}) collective-permute-start(bf16[128,128]{1,0:T(8,128)(2,1)S(1)} %get-tuple-element.157.own_ref), channel_id=1, source_target_pairs={{0,1},{1,0},{2,3},{3,2},{4,5},{5,4},{6,7},{7,6},{8,9},{9,8},{10,11... | collective-permute-start | bytes 98312 | tf_op jit(solution)/shard_map/ppermute | solution.py:503
